TPU v7x, 32 devices: a whole 2x2x4 slice. The times are simulated.
32 devices in a mesh: mem: 4 (over y, x), tile: 8 (over z, core).
Axes of the slice: x: 2, y: 2, z: 4, core: 2. Of those that a mesh axis runs over, the one named last changes fastest.
Arguments:
- alpha: float32 [8, 32, 128, 128], P('mem', None, 'tile'), may hold values from -6 to 6
- members: bfloat16 [8, 2, 32, 128, 128], P('mem', None, None, 'tile'), may hold values from -5 to 5
- scales: float32 [32], replicated, may hold values from 4 to 256
- observed: float32 [256, 256], P('tile'), may hold values from -6 to 6
- precision: float32 [256, 256], P('tile'), may hold values from 0.5 to 4
- ray_weights: float32 [256, 2, 256], P('tile'), may hold values from -1 to 1
- cell_index: int32 [256, 256], P('tile'), may hold values from 0 to 65535
- owner: int32 [256, 1], P('tile'), may hold values from 0 to 7; in each aligned block of 32 rows (0 to 31, 32 to 63, ...) at most 12 rows name the same one
Outputs:
- gradient: float32 [8, 32, 128, 128], P('mem', None, 'tile')
Inputs may be any that keep to these rules, and one draw needn't show every extreme that they name: Among the rays of one strip, at most 12 name the same owner, and in every draw some strip sends exactly 12 rays to one owner. `cell_index`: A gate's index refers to a cell of the strip named by owner.
All inputs are finite; a program needn't handle non-finite values.
Results may differ from a plain program's by a relative error of at most 0.0003.
Values sent between devices are 32-bit elements; how exact they have to be, the bound alone decides.
No kernel may reach another device: no remote copies, remote signals or barrier semaphores. Data moves between devices by JAX's collectives and lax.ppermute only.
A program may use at most 192 MiB of HBM per device.

v0:
```python
import jax
import jax.numpy as jnp
from jax import lax
from jax.sharding import PartitionSpec as P


def carried_in(x, axis, combine, identity, reverse):
    peers, place = (lax.axis_size(axis), lax.axis_index(axis))
    everything = jax.tree.map(lambda part: lax.all_gather(part, axis), x)
    start = jax.tree.map(
        lambda part, zero: jnp.broadcast_to(jnp.asarray(zero, part.dtype), part.shape), x, identity
    )

    def turn(k, before):
        at = peers - 1 - k if reverse else k
        reached = at > place if reverse else at < place
        new = combine(before, jax.tree.map(lambda part: part[at], everything))
        return jax.tree.map(lambda a, b: jnp.where(reached, a, b), new, before)

    return lax.fori_loop(0, peers, turn, start)


def kernel(log_rate, count):
    pos = jnp.arange(count).astype(jnp.float32)
    dist = jnp.abs(pos[:, None] - pos[None, :])
    top = jnp.maximum(pos[:, None], pos[None, :])
    rate = log_rate[:, None, None]
    decay = jnp.exp(rate)
    norm = jnp.sqrt((1.0 + decay) * -jnp.expm1(rate)) / (1.0 + decay)
    return norm * jnp.exp(rate * dist) * -jnp.expm1(2.0 * rate * (count - top))


def combine(earlier, later):
    return (earlier[0] * later[0], later[0] * earlier[1] + later[1])


def rows_chain(field, rate):
    hp = lax.Precision.HIGHEST
    rows = field.shape[2]
    pos = jnp.arange(rows).astype(jnp.float32)
    diff = pos[:, None] - pos[None, :]
    lvl_rate = rate[:, None, None]
    lower = jnp.where(
        diff >= 0, -jnp.expm1(lvl_rate) * jnp.exp(lvl_rate * jnp.maximum(diff, 0.0)), 0.0
    )
    whole_power = jnp.exp(rate * rows)[:, None]
    blank = (
        jnp.ones_like(whole_power),
        jnp.zeros((field.shape[0], field.shape[1], field.shape[3]), jnp.float32),
    )
    ahead = jnp.einsum("lij,bljy->bliy", lower, field, precision=hp)
    below = carried_in((whole_power, ahead[:, :, -1, :]), "tile", combine, blank, False)[1]
    ahead = ahead + jnp.exp(rate[:, None] * (pos + 1.0))[None, :, :, None] * below[:, :, None, :]
    behind = jnp.einsum("lji,bljy->bliy", lower, ahead, precision=hp)
    above = carried_in((whole_power, behind[:, :, 0, :]), "tile", combine, blank, True)[1]
    behind = behind + jnp.exp(rate[:, None] * (rows - pos))[None, :, :, None] * above[:, :, None, :]
    decay = jnp.exp(rate)
    factor = jnp.sqrt((1.0 + decay) / -jnp.expm1(rate))
    return behind * factor[None, :, None, None]


def localize(field, rate, matrix_y, matrix_z):
    hp = lax.Precision.HIGHEST
    field = jnp.einsum("kl,blxy->bkxy", matrix_z, field, precision=hp)
    field = jnp.einsum("lyz,blxz->blxy", matrix_y, field, precision=hp)
    return rows_chain(field, rate)


def per_device(alpha, members, scales, observed, precision, ray_weights, cell_index, owner):
    tiles = lax.axis_size("tile")
    count_rays = owner.shape[0]
    gates = observed.shape[1]
    capacity = 3 * count_rays // tiles
    levels = alpha.shape[1]
    columns = alpha.shape[3]
    cells_total = levels * alpha.shape[2] * columns
    payload = jnp.concatenate([ray_weights, observed[:, None, :], precision[:, None, :]], axis=1)
    onehot = (owner == jnp.arange(tiles, dtype=jnp.int32)[None, :]).astype(jnp.int32)
    before = jnp.cumsum(onehot, axis=0) - onehot
    slot = jnp.sum(before * onehot, axis=1)
    target = owner[:, 0] * capacity + slot
    send_float = jnp.zeros((tiles * capacity, 4, gates), jnp.float32).at[target].set(payload)
    send_cells = (
        jnp.full((tiles * capacity, gates), cells_total, jnp.int32).at[target].set(cell_index)
    )
    got_float, got_cells = (
        lax.all_to_all(send_float, "tile", split_axis=0, concat_axis=0, tiled=True),
        lax.all_to_all(send_cells, "tile", split_axis=0, concat_axis=0, tiled=True),
    )
    rate = -1.0 / scales
    matrix_y = kernel(rate, columns)
    matrix_z = kernel(jnp.full((1,), -1.0 / 3.0, jnp.float32), levels)[0]
    smooth = localize(alpha, rate, matrix_y, matrix_z)
    share = jnp.sum(members.astype(jnp.float32) * smooth[:, None], axis=0)
    weights_pair = jnp.stack([got_float[:, 0], got_float[:, 1]], axis=-1)
    increment = lax.psum(share, "mem")
    table = increment.reshape(2, -1).T
    picked = jnp.take(table, got_cells, axis=0, mode="fill", fill_value=0.0)
    modelled = jnp.sum(weights_pair * picked, axis=-1)
    departure = got_float[:, 3] * (modelled - got_float[:, 2])
    places = got_cells.reshape(-1)
    values = (weights_pair * departure[..., None]).reshape(-1, 2)
    table = jnp.zeros((cells_total, 2), jnp.float32).at[places].add(values, mode="drop")
    adjoint = table.T.reshape(share.shape)
    mixed = jnp.sum(members.astype(jnp.float32) * adjoint[None], axis=1)
    return alpha + localize(mixed, rate, matrix_y, matrix_z)


def solution(mesh):
    return jax.shard_map(
        per_device,
        mesh=mesh,
        in_specs=(
            P("mem", None, "tile", None),
            P("mem", None, None, "tile", None),
            P(),
            P("tile", None),
            P("tile", None),
            P("tile", None, None),
            P("tile", None),
            P("tile", None),
        ),
        out_specs=P("mem", None, "tile", None),
        check_vma=False,
    )
```

profile of v0, /device:TPU:0, one launch (start us, length us, event | category | flops | bytes accessed | tf_op | source)
XLA Modules:
  0.0 970.1 jit_solution(10521462874363660963)
XLA Ops:
  6.5 0.7 fusion.74
  7.3 0.8 select_reduce_fusion
  8.2 0.7 fusion.87
  8.8 1.0 scatter_custom_fusion
  9.8 0.7 all_to_all.13
  10.4 6.3 all-to-all-start
  17.0 0.7 divide_sqrt_fusion
  17.7 0.1 subtract_abs_fusion
  17.8 1.2 dynamic-slice
  19.7 1.8 convolution_bitcast_fusion.5
  21.5 0.1 exponential_dynamic-update-slice_fusion
  21.6 4.3 fusion.14
  25.8 0.8 convolution_bitcast_fusion.4
  26.7 13.4 %all-gather.1 = f32[16,32,1,128]{3,2,0,1:T(1,128)S(1)} all-gather(f32[2,32,1,128]{3,2,0,1:T(1,128)S(1)} %slice.37), channel_id=3, replica_groups=mesh['mem'=4,'tile'=8] {'tile'}, dimensions={0}, use_global_device_ids=true | all-gather | bytes 294912 | tf_op jit(solution)/shard_map/all_gather | solution.py:9
  40.0 13.9 %all-reduce = f32[256]{0:T(256)S(1)} all-reduce(f32[256]{0:T(256)S(1)} %get-tuple-element.663), channel_id=2, replica_groups=mesh['mem'=4,'tile'=8] {'tile'}, use_global_device_ids=true, to_apply=%add | all-reduce | flops 256 | bytes 2048
  54.0 0.9 while.60
  55.1 0.7 convolution_bitcast_fusion.3
  55.9 10.1 %all-gather.2 = f32[16,32,1,128]{3,2,0,1:T(1,128)S(1)} all-gather(f32[2,32,1,128]{3,2,0,1:T(1,128)S(1)} %slice.38), channel_id=4, replica_groups=mesh['mem'=4,'tile'=8] {'tile'}, dimensions={0}, use_global_device_ids=true | all-gather | bytes 294912 | tf_op jit(solution)/shard_map/all_gather | solution.py:9
  66.0 1.0 while.61
  67.0 0.2 fusion.20
  67.2 16.3 %copy.77 = f32[2,32,16,128]{0,3,2,1:T(8,128)} copy(f32[2,32,16,128]{3,2,1,0:T(8,128)S(1)} %fusion.20) | data formatting | bytes 1048576 | tf_op jit(solution)/shard_map/reduce_sum | solution.py:94
  83.6 0.7 copy-done.3
  84.4 0.1 pad_maximum_fusion
  84.5 0.8 broadcast_in_dim.31
  85.3 3.9 scatter_fusion
  89.2 3.6 all-to-all-start.1
  92.9 0.1 reshape.326
  93.0 0.1 compare_select_fusion
  93.2 567.3 %all-reduce.3.cloned.1.call-done = f32[65536,2]{1,0:T(8,128)} async-done(((f32[65536,2]{1,0:T(8,128)}), f32[65536,2]{1,0:T(8,128)}) %all-reduce.3.cloned.1.call-update) | async-done | bytes 524304 | tf_op jit(solution)/shard_map/psum | solution.py:96
  660.5 91.8 %gather_fusion = f32[24576,2]{1,0:T(8,128)} fusion(f32[65536,2]{1,0:T(8,128)} %all-reduce.3.cloned.1.call-done, s32[24576]{0:T(1024)S(1)} %broadcast_clamp_fusion), kind=kCustom, calls=%fused_computation | custom fusion | bytes 491520 | tf_op jit(solution)/shard_map/jit(_take)/gather | solution.py:98
  752.3 7.5 copy.79
  759.9 0.3 fusion.100
  760.2 0.5 fusion.48
  760.8 0.2 maximum_multiply_fusion
  761.0 6.7 copy.80
  767.8 144.1 %scatter_custom_fusion.2 = f32[65536,2]{1,0:T(8,128)} fusion(s32[24576]{0:T(1024)S(1)} %bitcast.149, f32[24576,2]{1,0:T(8,128)} %copy.80, f32[]{:T(128)} %constant.179.clone.1), kind=kCustom, calls=%fused_computation.24 | custom fusion | flops 49152 | bytes 524800 | tf_op jit(solution)/shard_map/scatter-add | solution.py:103
  911.9 18.7 %copy.81 = f32[2,32,16,128]{3,2,1,0:T(8,128)S(1)} copy(f32[2,32,16,128]{0,3,2,1:T(8,128)} %bitcast.136) | data formatting | bytes 1048576 | tf_op jit(solution)/shard_map/mul | solution.py:105
  930.6 0.1 fusion.21
  930.7 0.8 convolution_bitcast_fusion.2
  931.5 4.3 fusion.17
  935.7 0.8 convolution_bitcast_fusion.1
  936.6 12.9 %all-gather.3 = f32[16,32,1,128]{3,2,0,1:T(1,128)S(1)} all-gather(f32[2,32,1,128]{3,2,0,1:T(1,128)S(1)} %slice.40), channel_id=5, replica_groups=mesh['mem'=4,'tile'=8] {'tile'}, dimensions={0}, use_global_device_ids=true | all-gather | bytes 294912 | tf_op jit(solution)/shard_map/all_gather | solution.py:9
  949.5 0.9 while.62
  950.5 0.7 convolution_bitcast_fusion
  951.2 10.0 %all-gather.4 = f32[16,32,1,128]{3,2,0,1:T(1,128)S(1)} all-gather(f32[2,32,1,128]{3,2,0,1:T(1,128)S(1)} %slice.41), channel_id=6, replica_groups=mesh['mem'=4,'tile'=8] {'tile'}, dimensions={0}, use_global_device_ids=true | all-gather | bytes 294912 | tf_op jit(solution)/shard_map/all_gather | solution.py:9
  961.3 1.0 while.63
  962.3 0.2 copy_add_fusion
  962.5 0.8 copy.90
  (141 shorter events, 4.1 us)
Async XLA Ops:
  10.4 78.7 %all-to-all-start = ((s32[8,12,256]{2,1,0:T(8,128)}), s32[8,12,256]{2,1,0:T(8,128)S(1)}, u32[]{:S(2)}, u32[]{:S(2)}) async-start(s32[8,12,256]{2,1,0:T(8,128)} %all_to_all.13), calls=%async_computation | async-start | bytes 262144 | tf_op jit(solution)/shard_map/all_to_all | solution.py:88
  16.8 643.7 %all-reduce.3.cloned.1.call-start = ((), (), s32[]{:S(2)}) async-start(), calls=%async_computation.2 | async-start | bytes 67108864 | tf_op jit(solution)/shard_map/psum | solution.py:96
  26.6 40.3 %copy-start = (bf16[2,2,32,16,128]{4,3,2,1,0:T(8,128)(2,1)S(1)}, bf16[2,2,32,16,128]{4,3,2,1,0:T(8,128)(2,1)}, u32[]{:S(2)}) copy-start(bf16[2,2,32,16,128]{4,3,2,1,0:T(8,128)(2,1)} %param.17) | copy-start | bytes 1572868
  83.5 0.8 copy-start.3
  83.5 0.8 copy-start.4
  83.5 0.9 copy-start.2
  89.2 670.7 %all-to-all-start.1 = ((f32[96,4,256]{2,1,0:T(4,128)}), f32[96,4,256]{2,1,0:T(4,128)S(1)}, u32[]{:S(2)}, u32[]{:S(2)}) async-start(f32[96,4,256]{2,1,0:T(4,128)} %scatter_fusion), calls=%async_computation.1 | async-start | bytes 786432 | tf_op jit(solution)/shard_map/all_to_all | solution.py:87
  936.5 25.7 %copy-start.1 = (f32[2,32,16,128]{3,2,1,0:T(8,128)S(1)}, f32[2,32,16,128]{3,2,1,0:T(8,128)}, u32[]{:S(2)}) copy-start(f32[2,32,16,128]{3,2,1,0:T(8,128)} %param.16) | copy-start | bytes 1572868
Sparse Core Ops, SparseCore 0:
  83.7 576.7 all-reduce.2
where the time goes:
time: 971 us; the launch traced here: 970 us
  waiting for transfers between devices  567 us (58%)
  local copies, waits for them, and re-layouts  152 us (16%)
  other arithmetic  151 us (16%)
  blocking collectives  60.3 us (6%)
  between operations  14.5 us (1%)
  matrix products  14 us (1%)
  starting transfers between devices  10 us (1%)
    psum x1, waiting for transfers between devices, per_device(): increment = lax.psum(share, 'mem')  567 us
    scatter-add x1, other arithmetic, per_device(): jnp.zeros((cells_total, 2), jnp.float32).at[places].add(values, mode='drop')  144 us
    gather x2, local copies, waits for them, and re-layouts, per_device(): picked = jnp.take(table, got_cells, axis=0, mode='fill', fill_value=0.0)  99.4 us
    all_gather x4, blocking collectives, carried_in(): everything = jax.tree.map(lambda part: lax.all_gather(part, axis), x)  46.4 us
  transfers between devices with their start and end apart: 3, of which 1 were waited for; matrix products, arithmetic and copies ran while one was open for 14% of the time, Pallas kernels for 0%

commit v1 on v0

v1 whole, which is shorter than its diff:
```python
import functools
import math

import jax
import jax.numpy as jnp
from jax import lax
from jax.experimental import pallas as pl
from jax.experimental.pallas import tpu as pltpu
from jax.sharding import PartitionSpec as P

F32 = jnp.float32
BF16 = jnp.bfloat16
I32 = jnp.int32
LANES = 128
FIELDS = 5
Z_DECAY = math.exp(-1.0 / 3.0)
Z_GAIN = (1.0 - Z_DECAY) ** 2 * math.sqrt((1.0 + Z_DECAY) / (1.0 - Z_DECAY))
VMEM = pl.BlockSpec(memory_space=pltpu.VMEM)
PARAMS = pltpu.CompilerParams(vmem_limit_bytes=48 * 1024 * 1024)


def split(x):
    high = x.astype(BF16)
    return high, (x - high.astype(F32)).astype(BF16)


def dot(a, b):
    return jnp.dot(a, b, preferred_element_type=F32)


def dot3(a, b):
    (ah, al), (bh, bl) = split(a), split(b)
    return dot(ah, bh) + (dot(ah, bl) + dot(al, bh))


def iota(shape, dim):
    return lax.broadcasted_iota(I32, shape, dim)


def norm_of(rate):
    x = -rate
    series = jnp.ones_like(x)
    for k in (8, 7, 6, 5, 4, 3, 2):
        series = 1.0 - series * x * (1.0 / k)
    return jnp.sqrt(x * series / (1.0 + jnp.exp(rate)))


def pack_rays_kernel(tiles, per, owner_ref, cell_ref, weights_ref, observed_ref, precision_ref, *outs):
    rays, gates = observed_ref.shape
    halves = gates // LANES
    place, part = lax.axis_index("tile"), lax.axis_index("mem")
    owner = owner_ref[...]
    named = (owner == iota((rays, LANES), 1)).astype(F32)
    earlier = (iota((rays, rays), 0) > iota((rays, rays), 1)).astype(F32)
    rank = jnp.sum(dot(earlier, named) * named, axis=1, keepdims=True).astype(I32)
    step = lax.rem(owner - place + tiles, tiles)
    column = iota((rays, LANES), 1)
    target, row = column // per, column % per + part * per
    picks = [
        ((step == target) & (rank * halves + half == row)).astype(F32).T[: tiles * per]
        for half in range(halves)
    ]
    fields = (
        cell_ref[...].astype(F32),
        weights_ref[:, 0, :],
        weights_ref[:, 1, :],
        observed_ref[...],
        precision_ref[...],
    )
    for f, field in enumerate(fields):
        got = sum(
            jnp.dot(
                picks[half],
                field[:, half * LANES : (half + 1) * LANES],
                precision=lax.Precision.HIGHEST,
                preferred_element_type=F32,
            )
            for half in range(halves)
        )
        for k in range(tiles):
            outs[k][f] = got[k * per : (k + 1) * per]


def filter_levels(field_ref, out_ref):
    levels = field_ref.shape[1]
    state = field_ref[:, 0]
    out_ref[:, 0] = state
    for l in range(1, levels):
        state = field_ref[:, l] + Z_DECAY * state
        out_ref[:, l] = state
    for l in range(levels - 2, -1, -1):
        state = out_ref[:, l] + Z_DECAY * state
        out_ref[:, l] = state


def filter_columns(field_ref, high_ref, low_ref, out_ref):
    members, levels, rows, columns = field_ref.shape

    def level(l, _):
        field = field_ref[:, l].reshape(members * rows, columns)
        high, low = split(field)
        both = dot(jnp.concatenate([high, low], axis=0), high_ref[l])
        total = both[: members * rows] + (both[members * rows :] + dot(high, low_ref[l]))
        out_ref[:, l] = total.reshape(members, rows, columns)
        return 0

    lax.fori_loop(0, levels, level, 0, unroll=4)


def columns_matrix(rate_ref, high_ref, low_ref):
    levels, n, _ = high_ref.shape
    i, j = iota((n, n), 0), iota((n, n), 1)
    dist = jnp.abs(i - j).astype(F32)
    left = (2 * (n - jnp.maximum(i, j))).astype(F32)

    def level(l, _):
        rate = rate_ref[pl.ds(l, 1), :]
        matrix = (Z_GAIN * norm_of(rate)) * jnp.exp(rate * dist) * (1.0 - jnp.exp(rate * left))
        high_ref[l], low_ref[l] = split(matrix)
        return 0

    lax.fori_loop(0, levels, level, 0, unroll=2)


def states(tiles, rate_ref, field_ref, outs):
    members, levels, rows, columns = field_ref.shape
    place = lax.axis_index("tile")
    per = LANES // rows
    level, column = iota((per, LANES), 0), iota((per, LANES), 1)
    same = level == column // rows
    at = (column % rows).astype(F32)
    left = (2 * (rows * tiles - rows * place) - 2 * (column % rows)).astype(F32)
    for g in range(levels // per):
        rate = rate_ref[g * per : (g + 1) * per]
        norm = norm_of(rate)
        forward = jnp.where(same, norm * jnp.exp(rate * (rows - 1.0 - at)), 0.0)
        backward = jnp.where(same, norm * jnp.exp(rate * at) * (1.0 - jnp.exp(rate * left)), 0.0)
        both = jnp.concatenate([forward, backward], axis=0)
        for b in range(members):
            field = field_ref[b, g * per : (g + 1) * per].reshape(per * rows, columns)
            got = dot3(both, field)
            for k in range(1, tiles):
                outs[k - 1][b, g * per : (g + 1) * per] = jnp.where(place + k < tiles, got[:per], got[per:])


def first_kernel(tiles, rate_ref, alpha_ref, high_ref, low_ref, out_ref, *rest):
    outs, scratch = rest[:-1], rest[-1]
    columns_matrix(rate_ref, high_ref, low_ref)
    filter_levels(alpha_ref, scratch)
    filter_columns(scratch, high_ref, low_ref, out_ref)
    states(tiles, rate_ref, out_ref, outs)


def within_kernel(tiles, rate_ref, field_ref, out_ref):
    members, levels, rows, columns = field_ref.shape
    place = lax.axis_index("tile")
    per = LANES // rows
    n = per * rows
    row, column = iota((n, n), 0), iota((n, n), 1)
    same = row // rows == column // rows
    i, j = row % rows, column % rows
    dist = jnp.abs(i - j).astype(F32)
    left = (2 * (rows * tiles - rows * place) - 2 * jnp.maximum(i, j)).astype(F32)
    for g in range(levels // per):
        rate = jnp.concatenate(
            [jnp.broadcast_to(rate_ref[l : l + 1], (rows, LANES)) for l in range(g * per, (g + 1) * per)], axis=0
        )
        matrix = jnp.where(same, norm_of(rate) * jnp.exp(rate * dist) * (1.0 - jnp.exp(rate * left)), 0.0)
        for b in range(members):
            field = field_ref[b, g * per : (g + 1) * per].reshape(n, columns)
            out_ref[b, g * per : (g + 1) * per] = dot3(matrix, field).reshape(per, rows, columns)


def add_others(tiles, rate_ref, own_ref, received, out_ref, extra_ref=None):
    members, levels, rows, columns = own_ref.shape
    place = lax.axis_index("tile")
    rate = rate_ref[...]
    zero = jnp.zeros((levels, columns), F32)
    below, above = [zero] * members, [zero] * members
    for k in range(1, tiles):
        up = jnp.where(place >= k, jnp.exp(rate * (rows * (k - 1.0))), 0.0)
        down = jnp.where(place < k, jnp.exp(rate * (rows * (tiles - k - 1.0))), 0.0)
        for b in range(members):
            below[b] = below[b] + up * received[k - 1][b]
            above[b] = above[b] + down * received[k - 1][b]
    i = iota((rows, columns), 0)
    at = i.astype(F32)
    left = (2 * (rows * tiles - rows * place) - 2 * i).astype(F32)
    for l in range(levels):
        r = rate_ref[l : l + 1]
        from_below = jnp.exp(r * (at + 1.0)) * (1.0 - jnp.exp(r * left))
        from_above = jnp.exp(r * (rows - at))
        for b in range(members):
            total = own_ref[b, l] + (from_below * below[b][l : l + 1] + from_above * above[b][l : l + 1])
            out_ref[b, l] = total if extra_ref is None else total + extra_ref[b, l]


def indices(cells):
    whole = (cells + 0.5).astype(I32)
    return whole >> 7, whole & (LANES - 1)


def gather_kernel(tiles, blocks, rate_ref, own_ref, members_ref, *rest):
    received, rays = rest[: tiles - 1], rest[tiles - 1 : tiles - 1 + blocks]
    out_ref, smooth_ref, table_ref = rest[tiles - 1 + blocks :]
    add_others(tiles, rate_ref, own_ref, received, smooth_ref)
    members, levels, rows, columns = own_ref.shape
    high_rows = levels * rows
    for f in range(2):
        share = jnp.zeros((high_rows, columns), F32)
        for b in range(members):
            share = share + members_ref[b, f].reshape(high_rows, columns).astype(F32) * smooth_ref[b].reshape(
                high_rows, columns
            )
        high, low = split(share.T)
        table_ref[f * LANES : (f + 1) * LANES] = high
        table_ref[(f + 2) * LANES : (f + 3) * LANES] = low
    row_of = iota((high_rows, LANES), 0)
    lane_of = iota((LANES, LANES), 0)
    for block in range(blocks):
        ray = rays[block]

        def chunk(c, _, ray=ray, block=block):
            at = pl.ds(pl.multiple_of(c * 8, 8), 8)
            high, low = indices(ray[0, at, :])
            first, second = ray[1, at, :], ray[2, at, :]
            lines = []
            for pair in range(4):
                hot = jnp.concatenate(
                    [
                        jnp.where(row_of == high[r : r + 1], 1.0, 0.0).astype(BF16)
                        for r in (2 * pair, 2 * pair + 1)
                    ],
                    axis=1,
                )
                got = dot(table_ref[...], hot)
                for h in range(2):
                    r = 2 * pair + h
                    part = got[:, h * LANES : (h + 1) * LANES]
                    u = part[:LANES] + part[2 * LANES : 3 * LANES]
                    v = part[LANES : 2 * LANES] + part[3 * LANES :]
                    both = u * first[r : r + 1] + v * second[r : r + 1]
                    lines.append(
                        jnp.sum(jnp.where(lane_of == low[r : r + 1], both, 0.0), axis=0, keepdims=True)
                    )
            out_ref[block, at, :] = jnp.concatenate(lines, axis=0)
            return 0

        lax.fori_loop(0, ray.shape[1] // 8, chunk, 0)


def scatter_kernel(tiles, blocks, rate_ref, high_ref, low_ref, members_ref, own_ref, *rest):
    others, rays = rest[: blocks - 1], rest[blocks - 1 : 2 * blocks - 1]
    out_ref = rest[2 * blocks - 1]
    outs = rest[2 * blocks : 2 * blocks + tiles - 1]
    total_ref, mixed_ref = rest[2 * blocks + tiles - 1 :]
    members, levels, rows, columns = out_ref.shape
    high_rows = levels * rows
    row_of = iota((high_rows, LANES), 0)
    lane_of = iota((LANES, LANES), 0)
    total_ref[...] = jnp.zeros_like(total_ref)
    for block in range(blocks):
        ray = rays[block]

        def chunk(c, _, ray=ray, block=block):
            at = pl.ds(pl.multiple_of(c * 8, 8), 8)
            high, low = indices(ray[0, at, :])
            modelled = own_ref[block, at, :]
            for k in range(1, blocks):
                modelled = modelled + others[k - 1][block ^ k, at, :]
            departure = ray[4, at, :] * (modelled - ray[3, at, :])
            values = []
            for f in range(2):
                value = ray[1 + f, at, :] * departure
                part = value.astype(BF16).astype(F32)
                values.append((part, value - part))
            hots, sides = [], [[], []]
            for r in range(8):
                hots.append(jnp.where(row_of == high[r : r + 1], 1.0, 0.0).astype(BF16))
                here = lane_of == low[r : r + 1]
                for piece in range(2):
                    sides[piece].append(
                        jnp.concatenate(
                            [jnp.where(here, values[f][piece][r : r + 1], 0.0).astype(BF16) for f in range(2)],
                            axis=0,
                        )
                    )
            left = jnp.concatenate(hots, axis=1)
            dims = (((1,), (1,)), ((), ()))
            added = None
            for piece in range(2):
                right = jnp.concatenate(sides[piece], axis=1)
                term = lax.dot_general(left, right, dims, preferred_element_type=F32)
                added = term if added is None else added + term
            total_ref[...] += added
            return 0

        lax.fori_loop(0, ray.shape[1] // 8, chunk, 0)
    for l in range(levels):
        u = total_ref[l * rows : (l + 1) * rows, :LANES]
        v = total_ref[l * rows : (l + 1) * rows, LANES:]
        for b in range(members):
            mixed_ref[b, l] = members_ref[b, 0, l].astype(F32) * u + members_ref[b, 1, l].astype(F32) * v
    filter_levels(mixed_ref, mixed_ref)
    filter_columns(mixed_ref, high_ref, low_ref, out_ref)
    states(tiles, rate_ref, out_ref, outs)


def last_kernel(tiles, rate_ref, alpha_ref, own_ref, *rest):
    add_others(tiles, rate_ref, own_ref, rest[:-1], rest[-1], alpha_ref)


def call(body, outs, scratch=(), cost=None):
    def run(*args):
        return pl.pallas_call(
            body,
            out_shape=outs,
            in_specs=[VMEM] * len(args),
            out_specs=jax.tree.map(lambda _: VMEM, outs),
            scratch_shapes=list(scratch),
            compiler_params=PARAMS,
            cost_estimate=cost,
        )(*args)

    return run


def shaped(*shape, dtype=F32):
    return jax.ShapeDtypeStruct(shape, dtype)


def over_tiles(parts, tiles):
    return [
        lax.ppermute(part, "tile", [(i, (i + k) % tiles) for i in range(tiles)])
        for k, part in enumerate(parts, 1)
    ]


def over_members(part, blocks):
    return [lax.ppermute(part, "mem", [(i, i ^ k) for i in range(blocks)]) for k in range(1, blocks)]


def per_device(alpha, members, scales, observed, precision, ray_weights, cell_index, owner):
    tiles, blocks = lax.axis_size("tile"), lax.axis_size("mem")
    count_rays, gates = observed.shape
    capacity = 3 * count_rays // tiles
    per = -(-capacity * (gates // LANES) // blocks)
    shape = alpha.shape
    count, levels, rows, columns = shape
    sent = call(
        functools.partial(pack_rays_kernel, tiles, per),
        [shaped(FIELDS, per, LANES) for _ in range(tiles)],
    )(owner, cell_index, ray_weights, observed, precision)
    rate = jnp.broadcast_to((-1.0 / scales)[:, None], (levels, LANES))
    here = jnp.concatenate([sent[0], *over_tiles(sent[1:], tiles)], axis=1)
    rays = [here, *over_members(here, blocks)]

    state = shaped(count, levels, columns)
    high, low, field, *given = call(
        functools.partial(first_kernel, tiles),
        [shaped(levels, columns, columns, dtype=BF16)] * 2 + [shaped(*shape)] + [state] * (tiles - 1),
        [pltpu.VMEM(shape, F32)],
    )(rate, alpha)
    received = over_tiles(given, tiles)
    own = call(functools.partial(within_kernel, tiles), shaped(*shape))(rate, field)
    modelled = call(
        functools.partial(gather_kernel, tiles, blocks),
        shaped(blocks, tiles * per, LANES),
        [pltpu.VMEM(shape, F32), pltpu.VMEM((4 * LANES, levels * rows), BF16)],
    )(rate, own, members, *received, *rays)
    others = over_members(modelled, blocks)
    field, *given = call(
        functools.partial(scatter_kernel, tiles, blocks),
        [shaped(*shape)] + [state] * (tiles - 1),
        [pltpu.VMEM((levels * rows, 2 * LANES), F32), pltpu.VMEM(shape, F32)],
    )(rate, high, low, members, modelled, *others, *rays)
    received = over_tiles(given, tiles)
    own = call(functools.partial(within_kernel, tiles), shaped(*shape))(rate, field)
    return call(functools.partial(last_kernel, tiles), shaped(*shape))(rate, alpha, own, *received)


def solution(mesh):
    return jax.shard_map(
        per_device,
        mesh=mesh,
        in_specs=(
            P("mem", None, "tile", None),
            P("mem", None, None, "tile", None),
            P(),
            P("tile", None),
            P("tile", None),
            P("tile", None, None),
            P("tile", None),
            P("tile", None),
        ),
        out_specs=P("mem", None, "tile", None),
        check_vma=False,
    )
```

time: 971 us -> 97.7 us (0.10)
  waiting for transfers between devices: 567 us -> 19.2 us
  other arithmetic: 151 us -> 0.01 us
  local copies, waits for them, and re-layouts: 152 us -> 5.4 us
  blocking collectives: 60.3 us -> 0 us
  Pallas kernels: 0 us -> 45.3 us
  starting transfers between devices: 10 us -> 26.6 us
  between operations: 14.5 us -> 0.15 us
  matrix products: 14 us -> 0 us
    psum x1 -> x0, waiting for transfers between devices: 567 us -> none  [per_device(): increment = lax.psum(share, 'mem')]
    scatter-add x1 -> x0, other arithmetic: 144 us -> none  [per_device(): jnp.zeros((cells_total, 2), jnp.float32).at[places].add(values, mode='drop')]
    gather x2 -> x0, local copies, waits for them, and re-layouts: 99.4 us -> none  [per_device(): picked = jnp.take(table, got_cells, axis=0, mode='fill', fill_value=0.0)]
    all_gather x4 -> x0, blocking collectives: 46.4 us -> none  [carried_in(): everything = jax.tree.map(lambda part: lax.all_gather(part, axis), x)]
    pallas_call x0 -> x7, Pallas kernels: none -> 45.3 us  [run(): pl.pallas_call(body, out_shape=outs, in_specs=[VMEM] * len(args), out_spe...]
    ppermute x0 -> x27, starting transfers between devices: none -> 26.6 us  [the longest x21 19.5 us: over_tiles(): lax.ppermute(part, 'tile', [(i, (i + k) % tiles) for i in range(tiles)])]
    mul x34 -> x0, local copies, waits for them, and re-layouts: 25.8 us -> none  [the longest x1 18.7 us: per_device(): mixed = jnp.sum(members.astype(jnp.float32) * adjoint[None], axis=1)]
    ppermute x0 -> x27, waiting for transfers between devices: none -> 19.2 us  [the longest x21 14.3 us: over_tiles(): lax.ppermute(part, 'tile', [(i, (i + k) % tiles) for i in range(tiles)])]
  transfers between devices with their start and end apart: 3 -> 27, of which waited for: 1 -> 10; matrix products, arithmetic and copies ran while one was open for 14% -> 1% of each run, Pallas kernels for 0% -> 5%
where the time goes in v1:
time: 97.7 us; the launch traced here: 96.6 us
  Pallas kernels  45.3 us (46%)
  starting transfers between devices  26.6 us (27%)
  waiting for transfers between devices  19.2 us (20%)
  local copies, waits for them, and re-layouts  5.4 us (6%)
    pallas_call x7, Pallas kernels, run(): pl.pallas_call(body, out_shape=outs, in_specs=[VMEM] * len(args), out_spe...  45.3 us
    ppermute x21, starting transfers between devices, over_tiles(): lax.ppermute(part, 'tile', [(i, (i + k) % tiles) for i in range(tiles)])  19.5 us
    ppermute x21, waiting for transfers between devices, over_tiles(): lax.ppermute(part, 'tile', [(i, (i + k) % tiles) for i in range(tiles)])  14.3 us
    ppermute x6, starting transfers between devices, over_members(): lax.ppermute(part, 'mem', [(i, i ^ k) for i in range(blocks)])  7.11 us
    ppermute x6, waiting for transfers between devices, over_members(): lax.ppermute(part, 'mem', [(i, i ^ k) for i in range(blocks)])  4.93 us
    unnamed x17, local copies, waits for them, and re-layouts  4.91 us
  transfers between devices with their start and end apart: 27, of which 10 were waited for; matrix products, arithmetic and copies ran while one was open for 1% of the time, Pallas kernels for 5%

profile of v1, /device:TPU:0, one launch (start us, length us, event | category | flops | bytes accessed | tf_op | source)
XLA Modules:
  0.0 96.6 jit_solution(13846854843530466159)
XLA Ops:
  0.0 0.7 copy.9.owner_ref
  0.7 0.8 copy-done.3
  1.6 0.8 copy-done.4
  2.3 0.8 copy-done.5
  3.1 0.8 copy-done.6
  3.9 0.7 shard_map.84
  4.6 0.5 collective-permute-start.7
  5.1 2.6 %collective-permute-start.8 = (f32[5,6,128]{2,1,0:T(8,128)S(1)}, f32[5,6,128]{2,1,0:T(8,128)S(1)}, u32[]{:S(2)}, u32[]{:S(2)}) collective-permute-start(f32[5,6,128]{2,1,0:T(8,128)S(1)} %get-tuple-element.43), channel_id=1, source_target_pairs={{0,2},{1,3},{2,4},{3,5},{4,6},{5,7},{6,0},{7,1},{8,10},{9,11},{10,... | collective-permute-start | bytes 46088 | tf_op jit(solution)/shard_map/ppermute | solution.py:334
  7.7 2.5 %collective-permute-start.9 = (f32[5,6,128]{2,1,0:T(8,128)S(1)}, f32[5,6,128]{2,1,0:T(8,128)S(1)}, u32[]{:S(2)}, u32[]{:S(2)}) collective-permute-start(f32[5,6,128]{2,1,0:T(8,128)S(1)} %get-tuple-element.44), channel_id=1, source_target_pairs={{0,3},{1,4},{2,5},{3,6},{4,7},{5,0},{6,1},{7,2},{8,11},{9,12},{10,... | collective-permute-start | bytes 46088 | tf_op jit(solution)/shard_map/ppermute | solution.py:334
  10.2 1.2 %collective-permute-start.10 = (f32[5,6,128]{2,1,0:T(8,128)S(1)}, f32[5,6,128]{2,1,0:T(8,128)S(1)}, u32[]{:S(2)}, u32[]{:S(2)}) collective-permute-start(f32[5,6,128]{2,1,0:T(8,128)S(1)} %get-tuple-element.45), channel_id=1, source_target_pairs={{0,4},{1,5},{2,6},{3,7},{4,0},{5,1},{6,2},{7,3},{8,12},{9,13},{10,... | collective-permute-start | bytes 46088 | tf_op jit(solution)/shard_map/ppermute | solution.py:334
  11.5 1.2 %collective-permute-start.11 = (f32[5,6,128]{2,1,0:T(8,128)S(1)}, f32[5,6,128]{2,1,0:T(8,128)S(1)}, u32[]{:S(2)}, u32[]{:S(2)}) collective-permute-start(f32[5,6,128]{2,1,0:T(8,128)S(1)} %get-tuple-element.46), channel_id=1, source_target_pairs={{0,5},{1,6},{2,7},{3,0},{4,1},{5,2},{6,3},{7,4},{8,13},{9,14},{10,... | collective-permute-start | bytes 46088 | tf_op jit(solution)/shard_map/ppermute | solution.py:334
  12.7 1.3 %collective-permute-start.12 = (f32[5,6,128]{2,1,0:T(8,128)S(1)}, f32[5,6,128]{2,1,0:T(8,128)S(1)}, u32[]{:S(2)}, u32[]{:S(2)}) collective-permute-start(f32[5,6,128]{2,1,0:T(8,128)S(1)} %get-tuple-element.47), channel_id=1, source_target_pairs={{0,6},{1,7},{2,0},{3,1},{4,2},{5,3},{6,4},{7,5},{8,14},{9,15},{10,... | collective-permute-start | bytes 46088 | tf_op jit(solution)/shard_map/ppermute | solution.py:334
  14.0 1.4 %collective-permute-start.13 = (f32[5,6,128]{2,1,0:T(8,128)S(1)}, f32[5,6,128]{2,1,0:T(8,128)S(1)}, u32[]{:S(2)}, u32[]{:S(2)}) collective-permute-start(f32[5,6,128]{2,1,0:T(8,128)S(1)} %get-tuple-element.48), channel_id=1, source_target_pairs={{0,7},{1,0},{2,1},{3,2},{4,3},{5,4},{6,5},{7,6},{8,15},{9,8},{10,9... | collective-permute-start | bytes 46088 | tf_op jit(solution)/shard_map/ppermute | solution.py:334
  15.4 0.1 broadcast_in_dim.2.rate_ref
  15.5 1.0 %copy-done.1 = f32[2,32,16,128]{3,2,1,0:T(8,128)S(1)} copy-done((f32[2,32,16,128]{3,2,1,0:T(8,128)S(1)}, f32[2,32,16,128]{3,2,1,0:T(8,128)}, u32[]{:S(2)}) %copy-start.1) | copy-done | bytes 524312
  16.6 3.3 %shard_map.82 = (bf16[32,128,128]{2,1,0:T(8,128)(2,1)S(1)}, bf16[32,128,128]{2,1,0:T(8,128)(2,1)S(1)}, f32[2,32,16,128]{3,2,1,0:T(8,128)S(1)}, f32[2,32,128]{2,1...) custom-call(f32[32,128]{1,0:T(8,128)S(1)} %broadcast_in_dim.2.rate_r, ...), custom_call_target="tpu_custom_call" | custom-call | tf_op jit(solution)/shard_map/pallas_call | solution.py:315
  19.9 0.1 collective-permute-start
  20.0 0.4 concatenate.3.rest_7_.rest_3_
  20.4 1.6 %collective-permute-start.14 = (f32[5,48,128]{2,1,0:T(8,128)S(1)}, f32[5,48,128]{2,1,0:T(8,128)S(1)}, u32[]{:S(2)}, u32[]{:S(2)}) collective-permute-start(f32[5,48,128]{2,1,0:T(8,128)S(1)} %concatenate.3.rest_7_.rest_3_), channel_id=1, source_target_pairs={{0,8},{8,0},{16,24},{24,16},{1,9},{9,1},{17,25},{25,17},{2,10},{10... | collective-permute-start | bytes 368648 | tf_op jit(solution)/shard_map/ppermute | solution.py:340
  22.0 1.5 %collective-permute-start.15 = (f32[5,48,128]{2,1,0:T(8,128)S(1)}, f32[5,48,128]{2,1,0:T(8,128)S(1)}, u32[]{:S(2)}, u32[]{:S(2)}) collective-permute-start(f32[5,48,128]{2,1,0:T(8,128)S(1)} %concatenate.3.rest_7_.rest_3_), channel_id=1, source_target_pairs={{0,16},{8,24},{16,0},{24,8},{1,17},{9,25},{17,1},{25,9},{2,18},{10... | collective-permute-start | bytes 368648 | tf_op jit(solution)/shard_map/ppermute | solution.py:340
  23.5 0.5 collective-permute-start.16
  24.0 0.7 collective-permute-start.1
  24.6 0.4 collective-permute-done.rest_0_
  25.1 4.6 %collective-permute-done.1.rest_1_ = f32[2,32,128]{2,1,0:T(8,128)S(1)} collective-permute-done((f32[2,32,128]{2,1,0:T(8,128)S(1)}, f32[2,32,128]{2,1,0:T(8,128)S(1)}, u32[]{:S(2)}, u32[]{:S(2)}) %collective-permute-start.1) | collective-permute-done | bytes 32800 | tf_op jit(solution)/shard_map/ppermute | solution.py:334
  29.7 1.0 %collective-permute-start.4 = (f32[2,32,128]{2,1,0:T(8,128)S(1)}, f32[2,32,128]{2,1,0:T(8,128)S(1)}, u32[]{:S(2)}, u32[]{:S(2)}) collective-permute-start(f32[2,32,128]{2,1,0:T(8,128)S(1)} %get-tuple-element.38), channel_id=1, source_target_pairs={{0,5},{1,6},{2,7},{3,0},{4,1},{5,2},{6,3},{7,4},{8,13},{9,14},{10,... | collective-permute-start | bytes 98312 | tf_op jit(solution)/shard_map/ppermute | solution.py:334
  30.7 4.2 %collective-permute-done.3.rest_3_ = f32[2,32,128]{2,1,0:T(8,128)S(1)} collective-permute-done((f32[2,32,128]{2,1,0:T(8,128)S(1)}, f32[2,32,128]{2,1,0:T(8,128)S(1)}, u32[]{:S(2)}, u32[]{:S(2)}) %collective-permute-start.3) | collective-permute-done | bytes 32800 | tf_op jit(solution)/shard_map/ppermute | solution.py:334
  34.9 0.1 collective-permute-start.6
  35.1 0.6 shard_map.83.own_ref
  35.6 3.2 %collective-permute-done.5.rest_5_ = f32[2,32,128]{2,1,0:T(8,128)S(1)} collective-permute-done((f32[2,32,128]{2,1,0:T(8,128)S(1)}, f32[2,32,128]{2,1,0:T(8,128)S(1)}, u32[]{:S(2)}, u32[]{:S(2)}) %collective-permute-start.5) | collective-permute-done | bytes 32800 | tf_op jit(solution)/shard_map/ppermute | solution.py:334
  38.9 18.8 %shard_map.85.own_ref = f32[4,48,128]{2,1,0:T(8,128)S(1)} custom-call(f32[32,128]{1,0:T(8,128)S(1)} %broadcast_in_dim.2.rate_ref, f32[2,32,16,128]{3,2,1,0:T(8,128)S(1)} %shard_map.83.own_ref, bf16[2,2,32,16,128]{4,3,2,1,0:T(8,128)(2,1)S(1)} %copy-done, f32[2,32,128]{2,1,0:T(8,128)S(1)} %collective-permute-done.rest_0_, ...), custom_call_target="tpu_custom_call" | custom-call | tf_op jit(solution)/shard_map/pallas_call | solution.py:315
  57.7 1.4 %collective-permute-start.17 = (f32[4,48,128]{2,1,0:T(8,128)S(1)}, f32[4,48,128]{2,1,0:T(8,128)S(1)}, u32[]{:S(2)}, u32[]{:S(2)}) collective-permute-start(f32[4,48,128]{2,1,0:T(8,128)S(1)} %shard_map.85.own_ref), channel_id=1, source_target_pairs={{0,8},{8,0},{16,24},{24,16},{1,9},{9,1},{17,25},{25,17},{2,10},{10... | collective-permute-start | bytes 294920 | tf_op jit(solution)/shard_map/ppermute | solution.py:340
  59.2 1.5 %collective-permute-start.18 = (f32[4,48,128]{2,1,0:T(8,128)S(1)}, f32[4,48,128]{2,1,0:T(8,128)S(1)}, u32[]{:S(2)}, u32[]{:S(2)}) collective-permute-start(f32[4,48,128]{2,1,0:T(8,128)S(1)} %shard_map.85.own_ref), channel_id=1, source_target_pairs={{0,16},{8,24},{16,0},{24,8},{1,17},{9,25},{17,1},{25,9},{2,18},{10... | collective-permute-start | bytes 294920 | tf_op jit(solution)/shard_map/ppermute | solution.py:340
  60.7 0.6 collective-permute-start.19
  61.3 1.4 %collective-permute-done.17.rest_0_ = f32[4,48,128]{2,1,0:T(8,128)S(1)} collective-permute-done((f32[4,48,128]{2,1,0:T(8,128)S(1)}, f32[4,48,128]{2,1,0:T(8,128)S(1)}, u32[]{:S(2)}, u32[]{:S(2)}) %collective-permute-start.17) | collective-permute-done | bytes 98336 | tf_op jit(solution)/shard_map/ppermute | solution.py:340
  62.6 2.3 %collective-permute-done.18.rest_1_ = f32[4,48,128]{2,1,0:T(8,128)S(1)} collective-permute-done((f32[4,48,128]{2,1,0:T(8,128)S(1)}, f32[4,48,128]{2,1,0:T(8,128)S(1)}, u32[]{:S(2)}, u32[]{:S(2)}) %collective-permute-start.18) | collective-permute-done | bytes 98336 | tf_op jit(solution)/shard_map/ppermute | solution.py:340
  64.9 1.3 %collective-permute-done.19.rest_2_ = f32[4,48,128]{2,1,0:T(8,128)S(1)} collective-permute-done((f32[4,48,128]{2,1,0:T(8,128)S(1)}, f32[4,48,128]{2,1,0:T(8,128)S(1)}, u32[]{:S(2)}, u32[]{:S(2)}) %collective-permute-start.19) | collective-permute-done | bytes 98336 | tf_op jit(solution)/shard_map/ppermute | solution.py:340
  66.2 20.2 %shard_map.86 = (f32[2,32,16,128]{3,2,1,0:T(8,128)S(1)}, f32[2,32,128]{2,1,0:T(8,128)S(1)}, f32[2,32,128]{2,1,0:T(8,128)S(1)}, f32[2,32,128]{2,1,0:T(8,128)S(1)}...) custom-call(f32[32,128]{1,0:T(8,128)S(1)} %broadcast_in_dim.2.rate_r, ...), custom_call_target="tpu_custom_call" | custom-call | tf_op jit(solution)/shard_map/pallas_call | solution.py:315
  86.5 0.1 collective-permute-start.21
  86.5 2.3 %collective-permute-start.22 = (f32[2,32,128]{2,1,0:T(8,128)S(1)}, f32[2,32,128]{2,1,0:T(8,128)S(1)}, u32[]{:S(2)}, u32[]{:S(2)}) collective-permute-start(f32[2,32,128]{2,1,0:T(8,128)S(1)} %get-tuple-element.52), channel_id=1, source_target_pairs={{0,3},{1,4},{2,5},{3,6},{4,7},{5,0},{6,1},{7,2},{8,11},{9,12},{10,... | collective-permute-start | bytes 98312 | tf_op jit(solution)/shard_map/ppermute | solution.py:334
  88.8 1.8 %collective-permute-start.23 = (f32[2,32,128]{2,1,0:T(8,128)S(1)}, f32[2,32,128]{2,1,0:T(8,128)S(1)}, u32[]{:S(2)}, u32[]{:S(2)}) collective-permute-start(f32[2,32,128]{2,1,0:T(8,128)S(1)} %get-tuple-element.53), channel_id=1, source_target_pairs={{0,4},{1,5},{2,6},{3,7},{4,0},{5,1},{6,2},{7,3},{8,12},{9,13},{10,... | collective-permute-start | bytes 98312 | tf_op jit(solution)/shard_map/ppermute | solution.py:334
  90.6 0.7 collective-permute-start.24
  91.3 0.3 collective-permute-done.20.rest_0_
  91.6 1.6 %collective-permute-start.25 = (f32[2,32,128]{2,1,0:T(8,128)S(1)}, f32[2,32,128]{2,1,0:T(8,128)S(1)}, u32[]{:S(2)}, u32[]{:S(2)}) collective-permute-start(f32[2,32,128]{2,1,0:T(8,128)S(1)} %get-tuple-element.55), channel_id=1, source_target_pairs={{0,6},{1,7},{2,0},{3,1},{4,2},{5,3},{6,4},{7,5},{8,14},{9,15},{10,... | collective-permute-start | bytes 98312 | tf_op jit(solution)/shard_map/ppermute | solution.py:334
  93.2 0.3 collective-permute-start.26
  93.5 0.6 shard_map.87.own_ref
  94.1 0.3 collective-permute-done.24.rest_4_
  94.4 1.2 %collective-permute-done.25.rest_5_ = f32[2,32,128]{2,1,0:T(8,128)S(1)} collective-permute-done((f32[2,32,128]{2,1,0:T(8,128)S(1)}, f32[2,32,128]{2,1,0:T(8,128)S(1)}, u32[]{:S(2)}, u32[]{:S(2)}) %collective-permute-start.25) | collective-permute-done | bytes 32800 | tf_op jit(solution)/shard_map/ppermute | solution.py:334
  95.6 1.1 %shard_map.88 = f32[2,32,16,128]{3,2,1,0:T(8,128)} custom-call(f32[32,128]{1,0:T(8,128)S(1)} %broadcast_in_dim.2.rate_ref, f32[2,32,16,128]{3,2,1,0:T(8,128)S(1)} %copy-done.2, f32[2,32,16,128]{3,2,1,0:T(8,128)S(1)} %shard_map.87.own_ref, f32[2,32,128]{2,1,0:T(8,128)S(1)} %collective-permute-done.20.rest_0_, ...), custom_call_target="tpu_custom_call" | custom-call | tf_op jit(solution)/shard_map/pallas_call | solution.py:315
  (33 shorter events, 0.1 us)
Async XLA Ops:
  0.7 0.8 copy-start.3
  1.6 0.8 copy-start.4
  2.3 0.8 copy-start.5
  3.1 0.8 copy-start.6
  4.6 8.1 %collective-permute-start.7 = (f32[5,6,128]{2,1,0:T(8,128)S(1)}, f32[5,6,128]{2,1,0:T(8,128)S(1)}, u32[]{:S(2)}, u32[]{:S(2)}) collective-permute-start(f32[5,6,128]{2,1,0:T(8,128)S(1)} %get-tuple-element.42), channel_id=1, source_target_pairs={{0,1},{1,2},{2,3},{3,4},{4,5},{5,6},{6,7},{7,0},{8,9},{9,10},{10,1... | collective-permute-start | bytes 46088 | tf_op jit(solution)/shard_map/ppermute | solution.py:334
  5.1 8.9 %collective-permute-start.8 = (f32[5,6,128]{2,1,0:T(8,128)S(1)}, f32[5,6,128]{2,1,0:T(8,128)S(1)}, u32[]{:S(2)}, u32[]{:S(2)}) collective-permute-start(f32[5,6,128]{2,1,0:T(8,128)S(1)} %get-tuple-element.43), channel_id=1, source_target_pairs={{0,2},{1,3},{2,4},{3,5},{4,6},{5,7},{6,0},{7,1},{8,10},{9,11},{10,... | collective-permute-start | bytes 46088 | tf_op jit(solution)/shard_map/ppermute | solution.py:334
  7.7 12.2 %collective-permute-start.9 = (f32[5,6,128]{2,1,0:T(8,128)S(1)}, f32[5,6,128]{2,1,0:T(8,128)S(1)}, u32[]{:S(2)}, u32[]{:S(2)}) collective-permute-start(f32[5,6,128]{2,1,0:T(8,128)S(1)} %get-tuple-element.44), channel_id=1, source_target_pairs={{0,3},{1,4},{2,5},{3,6},{4,7},{5,0},{6,1},{7,2},{8,11},{9,12},{10,... | collective-permute-start | bytes 46088 | tf_op jit(solution)/shard_map/ppermute | solution.py:334
  10.2 9.7 %collective-permute-start.10 = (f32[5,6,128]{2,1,0:T(8,128)S(1)}, f32[5,6,128]{2,1,0:T(8,128)S(1)}, u32[]{:S(2)}, u32[]{:S(2)}) collective-permute-start(f32[5,6,128]{2,1,0:T(8,128)S(1)} %get-tuple-element.45), channel_id=1, source_target_pairs={{0,4},{1,5},{2,6},{3,7},{4,0},{5,1},{6,2},{7,3},{8,12},{9,13},{10,... | collective-permute-start | bytes 46088 | tf_op jit(solution)/shard_map/ppermute | solution.py:334
  11.5 8.5 %collective-permute-start.11 = (f32[5,6,128]{2,1,0:T(8,128)S(1)}, f32[5,6,128]{2,1,0:T(8,128)S(1)}, u32[]{:S(2)}, u32[]{:S(2)}) collective-permute-start(f32[5,6,128]{2,1,0:T(8,128)S(1)} %get-tuple-element.46), channel_id=1, source_target_pairs={{0,5},{1,6},{2,7},{3,0},{4,1},{5,2},{6,3},{7,4},{8,13},{9,14},{10,... | collective-permute-start | bytes 46088 | tf_op jit(solution)/shard_map/ppermute | solution.py:334
  12.7 2.8 %copy-start.7 = (f32[32]{0:T(128)S(1)}, f32[32]{0:T(128)}, u32[]{:S(2)}) copy-start(f32[32]{0:T(128)} %param.10) | copy-start | bytes 388
  12.7 7.3 %collective-permute-start.12 = (f32[5,6,128]{2,1,0:T(8,128)S(1)}, f32[5,6,128]{2,1,0:T(8,128)S(1)}, u32[]{:S(2)}, u32[]{:S(2)}) collective-permute-start(f32[5,6,128]{2,1,0:T(8,128)S(1)} %get-tuple-element.47), channel_id=1, source_target_pairs={{0,6},{1,7},{2,0},{3,1},{4,2},{5,3},{6,4},{7,5},{8,14},{9,15},{10,... | collective-permute-start | bytes 46088 | tf_op jit(solution)/shard_map/ppermute | solution.py:334
  14.0 5.9 %collective-permute-start.13 = (f32[5,6,128]{2,1,0:T(8,128)S(1)}, f32[5,6,128]{2,1,0:T(8,128)S(1)}, u32[]{:S(2)}, u32[]{:S(2)}) collective-permute-start(f32[5,6,128]{2,1,0:T(8,128)S(1)} %get-tuple-element.48), channel_id=1, source_target_pairs={{0,7},{1,0},{2,1},{3,2},{4,3},{5,4},{6,5},{7,6},{8,15},{9,8},{10,9... | collective-permute-start | bytes 46088 | tf_op jit(solution)/shard_map/ppermute | solution.py:334
  15.5 1.0 %copy-start.1 = (f32[2,32,16,128]{3,2,1,0:T(8,128)S(1)}, f32[2,32,16,128]{3,2,1,0:T(8,128)}, u32[]{:S(2)}) copy-start(f32[2,32,16,128]{3,2,1,0:T(8,128)} %alpha_ref.3) | copy-start | bytes 1572868
  19.9 5.2 %collective-permute-start = (f32[2,32,128]{2,1,0:T(8,128)S(1)}, f32[2,32,128]{2,1,0:T(8,128)S(1)}, u32[]{:S(2)}, u32[]{:S(2)}) collective-permute-start(f32[2,32,128]{2,1,0:T(8,128)S(1)} %get-tuple-element.34), channel_id=1, source_target_pairs={{0,1},{1,2},{2,3},{3,4},{4,5},{5,6},{6,7},{7,0},{8,9},{9,10},{10,1... | collective-permute-start | bytes 98312 | tf_op jit(solution)/shard_map/ppermute | solution.py:334
  20.4 18.4 %collective-permute-start.14 = (f32[5,48,128]{2,1,0:T(8,128)S(1)}, f32[5,48,128]{2,1,0:T(8,128)S(1)}, u32[]{:S(2)}, u32[]{:S(2)}) collective-permute-start(f32[5,48,128]{2,1,0:T(8,128)S(1)} %concatenate.3.rest_7_.rest_3_), channel_id=1, source_target_pairs={{0,8},{8,0},{16,24},{24,16},{1,9},{9,1},{17,25},{25,17},{2,10},{10... | collective-permute-start | bytes 368648 | tf_op jit(solution)/shard_map/ppermute | solution.py:340
  22.0 16.9 %collective-permute-start.15 = (f32[5,48,128]{2,1,0:T(8,128)S(1)}, f32[5,48,128]{2,1,0:T(8,128)S(1)}, u32[]{:S(2)}, u32[]{:S(2)}) collective-permute-start(f32[5,48,128]{2,1,0:T(8,128)S(1)} %concatenate.3.rest_7_.rest_3_), channel_id=1, source_target_pairs={{0,16},{8,24},{16,0},{24,8},{1,17},{9,25},{17,1},{25,9},{2,18},{10... | collective-permute-start | bytes 368648 | tf_op jit(solution)/shard_map/ppermute | solution.py:340
  23.5 15.4 %collective-permute-start.16 = (f32[5,48,128]{2,1,0:T(8,128)S(1)}, f32[5,48,128]{2,1,0:T(8,128)S(1)}, u32[]{:S(2)}, u32[]{:S(2)}) collective-permute-start(f32[5,48,128]{2,1,0:T(8,128)S(1)} %concatenate.3.rest_7_.rest_3_), channel_id=1, source_target_pairs={{0,24},{8,16},{16,8},{24,0},{1,25},{9,17},{17,9},{25,1},{2,26},{10... | collective-permute-start | bytes 368648 | tf_op jit(solution)/shard_map/ppermute | solution.py:340
  24.0 5.7 %collective-permute-start.1 = (f32[2,32,128]{2,1,0:T(8,128)S(1)}, f32[2,32,128]{2,1,0:T(8,128)S(1)}, u32[]{:S(2)}, u32[]{:S(2)}) collective-permute-start(f32[2,32,128]{2,1,0:T(8,128)S(1)} %get-tuple-element.35), channel_id=1, source_target_pairs={{0,2},{1,3},{2,4},{3,5},{4,6},{5,7},{6,0},{7,1},{8,10},{9,11},{10,... | collective-permute-start | bytes 98312 | tf_op jit(solution)/shard_map/ppermute | solution.py:334
  25.1 4.6 %collective-permute-start.2 = (f32[2,32,128]{2,1,0:T(8,128)S(1)}, f32[2,32,128]{2,1,0:T(8,128)S(1)}, u32[]{:S(2)}, u32[]{:S(2)}) collective-permute-start(f32[2,32,128]{2,1,0:T(8,128)S(1)} %get-tuple-element.36), channel_id=1, source_target_pairs={{0,3},{1,4},{2,5},{3,6},{4,7},{5,0},{6,1},{7,2},{8,11},{9,12},{10,... | collective-permute-start | bytes 98312 | tf_op jit(solution)/shard_map/ppermute | solution.py:334
  29.7 5.3 %collective-permute-start.3 = (f32[2,32,128]{2,1,0:T(8,128)S(1)}, f32[2,32,128]{2,1,0:T(8,128)S(1)}, u32[]{:S(2)}, u32[]{:S(2)}) collective-permute-start(f32[2,32,128]{2,1,0:T(8,128)S(1)} %get-tuple-element.37), channel_id=1, source_target_pairs={{0,4},{1,5},{2,6},{3,7},{4,0},{5,1},{6,2},{7,3},{8,12},{9,13},{10,... | collective-permute-start | bytes 98312 | tf_op jit(solution)/shard_map/ppermute | solution.py:334
  29.7 5.3 %collective-permute-start.4 = (f32[2,32,128]{2,1,0:T(8,128)S(1)}, f32[2,32,128]{2,1,0:T(8,128)S(1)}, u32[]{:S(2)}, u32[]{:S(2)}) collective-permute-start(f32[2,32,128]{2,1,0:T(8,128)S(1)} %get-tuple-element.38), channel_id=1, source_target_pairs={{0,5},{1,6},{2,7},{3,0},{4,1},{5,2},{6,3},{7,4},{8,13},{9,14},{10,... | collective-permute-start | bytes 98312 | tf_op jit(solution)/shard_map/ppermute | solution.py:334
  34.9 3.9 %collective-permute-start.5 = (f32[2,32,128]{2,1,0:T(8,128)S(1)}, f32[2,32,128]{2,1,0:T(8,128)S(1)}, u32[]{:S(2)}, u32[]{:S(2)}) collective-permute-start(f32[2,32,128]{2,1,0:T(8,128)S(1)} %get-tuple-element.39), channel_id=1, source_target_pairs={{0,6},{1,7},{2,0},{3,1},{4,2},{5,3},{6,4},{7,5},{8,14},{9,15},{10,... | collective-permute-start | bytes 98312 | tf_op jit(solution)/shard_map/ppermute | solution.py:334
  34.9 3.9 %collective-permute-start.6 = (f32[2,32,128]{2,1,0:T(8,128)S(1)}, f32[2,32,128]{2,1,0:T(8,128)S(1)}, u32[]{:S(2)}, u32[]{:S(2)}) collective-permute-start(f32[2,32,128]{2,1,0:T(8,128)S(1)} %get-tuple-element.40), channel_id=1, source_target_pairs={{0,7},{1,0},{2,1},{3,2},{4,3},{5,4},{6,5},{7,6},{8,15},{9,8},{10,9... | collective-permute-start | bytes 98312 | tf_op jit(solution)/shard_map/ppermute | solution.py:334
  35.1 3.8 %copy-start = (bf16[2,2,32,16,128]{4,3,2,1,0:T(8,128)(2,1)S(1)}, bf16[2,2,32,16,128]{4,3,2,1,0:T(8,128)(2,1)}, u32[]{:S(2)}) copy-start(bf16[2,2,32,16,128]{4,3,2,1,0:T(8,128)(2,1)} %members_ref.3) | copy-start | bytes 1572868
  57.7 4.9 %collective-permute-start.17 = (f32[4,48,128]{2,1,0:T(8,128)S(1)}, f32[4,48,128]{2,1,0:T(8,128)S(1)}, u32[]{:S(2)}, u32[]{:S(2)}) collective-permute-start(f32[4,48,128]{2,1,0:T(8,128)S(1)} %shard_map.85.own_ref), channel_id=1, source_target_pairs={{0,8},{8,0},{16,24},{24,16},{1,9},{9,1},{17,25},{25,17},{2,10},{10... | collective-permute-start | bytes 294920 | tf_op jit(solution)/shard_map/ppermute | solution.py:340
  59.2 5.8 %collective-permute-start.18 = (f32[4,48,128]{2,1,0:T(8,128)S(1)}, f32[4,48,128]{2,1,0:T(8,128)S(1)}, u32[]{:S(2)}, u32[]{:S(2)}) collective-permute-start(f32[4,48,128]{2,1,0:T(8,128)S(1)} %shard_map.85.own_ref), channel_id=1, source_target_pairs={{0,16},{8,24},{16,0},{24,8},{1,17},{9,25},{17,1},{25,9},{2,18},{10... | collective-permute-start | bytes 294920 | tf_op jit(solution)/shard_map/ppermute | solution.py:340
  60.7 5.5 %collective-permute-start.19 = (f32[4,48,128]{2,1,0:T(8,128)S(1)}, f32[4,48,128]{2,1,0:T(8,128)S(1)}, u32[]{:S(2)}, u32[]{:S(2)}) collective-permute-start(f32[4,48,128]{2,1,0:T(8,128)S(1)} %shard_map.85.own_ref), channel_id=1, source_target_pairs={{0,24},{8,16},{16,8},{24,0},{1,25},{9,17},{17,9},{25,1},{2,26},{10... | collective-permute-start | bytes 294920 | tf_op jit(solution)/shard_map/ppermute | solution.py:340
  86.4 5.2 %collective-permute-start.20 = (f32[2,32,128]{2,1,0:T(8,128)S(1)}, f32[2,32,128]{2,1,0:T(8,128)S(1)}, u32[]{:S(2)}, u32[]{:S(2)}) collective-permute-start(f32[2,32,128]{2,1,0:T(8,128)S(1)} %get-tuple-element.50), channel_id=1, source_target_pairs={{0,1},{1,2},{2,3},{3,4},{4,5},{5,6},{6,7},{7,0},{8,9},{9,10},{10,1... | collective-permute-start | bytes 98312 | tf_op jit(solution)/shard_map/ppermute | solution.py:334
  86.5 6.8 %collective-permute-start.21 = (f32[2,32,128]{2,1,0:T(8,128)S(1)}, f32[2,32,128]{2,1,0:T(8,128)S(1)}, u32[]{:S(2)}, u32[]{:S(2)}) collective-permute-start(f32[2,32,128]{2,1,0:T(8,128)S(1)} %get-tuple-element.51), channel_id=1, source_target_pairs={{0,2},{1,3},{2,4},{3,5},{4,6},{5,7},{6,0},{7,1},{8,10},{9,11},{10,... | collective-permute-start | bytes 98312 | tf_op jit(solution)/shard_map/ppermute | solution.py:334
  86.5 7.6 %collective-permute-start.22 = (f32[2,32,128]{2,1,0:T(8,128)S(1)}, f32[2,32,128]{2,1,0:T(8,128)S(1)}, u32[]{:S(2)}, u32[]{:S(2)}) collective-permute-start(f32[2,32,128]{2,1,0:T(8,128)S(1)} %get-tuple-element.52), channel_id=1, source_target_pairs={{0,3},{1,4},{2,5},{3,6},{4,7},{5,0},{6,1},{7,2},{8,11},{9,12},{10,... | collective-permute-start | bytes 98312 | tf_op jit(solution)/shard_map/ppermute | solution.py:334
  88.8 5.3 %collective-permute-start.23 = (f32[2,32,128]{2,1,0:T(8,128)S(1)}, f32[2,32,128]{2,1,0:T(8,128)S(1)}, u32[]{:S(2)}, u32[]{:S(2)}) collective-permute-start(f32[2,32,128]{2,1,0:T(8,128)S(1)} %get-tuple-element.53), channel_id=1, source_target_pairs={{0,4},{1,5},{2,6},{3,7},{4,0},{5,1},{6,2},{7,3},{8,12},{9,13},{10,... | collective-permute-start | bytes 98312 | tf_op jit(solution)/shard_map/ppermute | solution.py:334
  90.6 3.8 %collective-permute-start.24 = (f32[2,32,128]{2,1,0:T(8,128)S(1)}, f32[2,32,128]{2,1,0:T(8,128)S(1)}, u32[]{:S(2)}, u32[]{:S(2)}) collective-permute-start(f32[2,32,128]{2,1,0:T(8,128)S(1)} %get-tuple-element.54), channel_id=1, source_target_pairs={{0,5},{1,6},{2,7},{3,0},{4,1},{5,2},{6,3},{7,4},{8,13},{9,14},{10,... | collective-permute-start | bytes 98312 | tf_op jit(solution)/shard_map/ppermute | solution.py:334
  91.6 4.0 %collective-permute-start.25 = (f32[2,32,128]{2,1,0:T(8,128)S(1)}, f32[2,32,128]{2,1,0:T(8,128)S(1)}, u32[]{:S(2)}, u32[]{:S(2)}) collective-permute-start(f32[2,32,128]{2,1,0:T(8,128)S(1)} %get-tuple-element.55), channel_id=1, source_target_pairs={{0,6},{1,7},{2,0},{3,1},{4,2},{5,3},{6,4},{7,5},{8,14},{9,15},{10,... | collective-permute-start | bytes 98312 | tf_op jit(solution)/shard_map/ppermute | solution.py:334
  93.2 2.3 %collective-permute-start.26 = (f32[2,32,128]{2,1,0:T(8,128)S(1)}, f32[2,32,128]{2,1,0:T(8,128)S(1)}, u32[]{:S(2)}, u32[]{:S(2)}) collective-permute-start(f32[2,32,128]{2,1,0:T(8,128)S(1)} %get-tuple-element.56), channel_id=1, source_target_pairs={{0,7},{1,0},{2,1},{3,2},{4,3},{5,4},{6,5},{7,6},{8,15},{9,8},{10,9... | collective-permute-start | bytes 98312 | tf_op jit(solution)/shard_map/ppermute | solution.py:334
  93.5 2.1 %copy-start.2 = (f32[2,32,16,128]{3,2,1,0:T(8,128)S(1)}, f32[2,32,16,128]{3,2,1,0:T(8,128)}, u32[]{:S(2)}) copy-start(f32[2,32,16,128]{3,2,1,0:T(8,128)} %alpha_ref.3) | copy-start | bytes 1572868

commit v2 on v1

--- a/solution.py
+++ b/solution.py
@@ -11,11 +11,13 @@
 F32 = jnp.float32
 BF16 = jnp.bfloat16
 I32 = jnp.int32
+F8 = jnp.float8_e4m3fn
+PIECES = 3
 LANES = 128
-FIELDS = 5
 Z_DECAY = math.exp(-1.0 / 3.0)
 Z_GAIN = (1.0 - Z_DECAY) ** 2 * math.sqrt((1.0 + Z_DECAY) / (1.0 - Z_DECAY))
 VMEM = pl.BlockSpec(memory_space=pltpu.VMEM)
+COST = pl.CostEstimate(flops=2 * 10**10, bytes_accessed=4 * 10**6, transcendentals=0)
 PARAMS = pltpu.CompilerParams(vmem_limit_bytes=48 * 1024 * 1024)
 
 
@@ -45,20 +47,18 @@
     return jnp.sqrt(x * series / (1.0 + jnp.exp(rate)))
 
 
-def pack_rays_kernel(tiles, per, owner_ref, cell_ref, weights_ref, observed_ref, precision_ref, *outs):
+def pack_rays_kernel(per, owner_ref, cell_ref, weights_ref, observed_ref, precision_ref, out_ref):
     rays, gates = observed_ref.shape
     halves = gates // LANES
-    place, part = lax.axis_index("tile"), lax.axis_index("mem")
+    wide = out_ref.shape[0] * per
     owner = owner_ref[...]
     named = (owner == iota((rays, LANES), 1)).astype(F32)
     earlier = (iota((rays, rays), 0) > iota((rays, rays), 1)).astype(F32)
     rank = jnp.sum(dot(earlier, named) * named, axis=1, keepdims=True).astype(I32)
-    step = lax.rem(owner - place + tiles, tiles)
-    column = iota((rays, LANES), 1)
-    target, row = column // per, column % per + part * per
+    column = iota((rays, -(-wide // LANES) * LANES), 1)
+    target, row = column // per, column % per
     picks = [
-        ((step == target) & (rank * halves + half == row)).astype(F32).T[: tiles * per]
-        for half in range(halves)
+        ((owner == target) & (rank * halves + half == row)).astype(F32).T[:wide] for half in range(halves)
     ]
     fields = (
         cell_ref[...].astype(F32),
@@ -77,8 +77,7 @@
             )
             for half in range(halves)
         )
-        for k in range(tiles):
-            outs[k][f] = got[k * per : (k + 1) * per]
+        out_ref[:, f] = got.reshape(-1, per, LANES)
 
 
 def filter_levels(field_ref, out_ref):
@@ -200,102 +199,124 @@
     return whole >> 7, whole & (LANES - 1)
 
 
-def gather_kernel(tiles, blocks, rate_ref, own_ref, members_ref, *rest):
-    received, rays = rest[: tiles - 1], rest[tiles - 1 : tiles - 1 + blocks]
-    out_ref, smooth_ref, table_ref = rest[tiles - 1 + blocks :]
+def chunks_of(shape):
+    tiles, per = shape[0], shape[-2]
+
+    def run(body):
+        def step(c, _):
+            body(c // (per // 8), pl.ds(pl.multiple_of(c % (per // 8) * 8, 8), 8))
+            return 0
+
+        lax.fori_loop(0, tiles * (per // 8), step, 0, unroll=8)
+
+    return run
+
+
+def hot_rows(high, row_of, high_rows):
+    count, _ = row_of.shape
+    one, zero = jnp.ones((), BF16), jnp.zeros((), BF16)
+    high = high.astype(F32)
+    blocks = high_rows // count
+
+    def rows(r):
+        line = high[r : r + 1]
+        return jnp.concatenate(
+            [jnp.where(row_of == (line - float(count * h)).astype(BF16), one, zero) for h in range(blocks)], axis=0
+        )
+
+    return rows
+
+
+def gather_kernel(tiles, rate_ref, own_ref, members_ref, *rest):
+    received, ray = rest[: tiles - 1], rest[tiles - 1]
+    out_ref, smooth_ref, table_ref = rest[tiles:]
     add_others(tiles, rate_ref, own_ref, received, smooth_ref)
     members, levels, rows, columns = own_ref.shape
     high_rows = levels * rows
+    shares = []
     for f in range(2):
         share = jnp.zeros((high_rows, columns), F32)
         for b in range(members):
             share = share + members_ref[b, f].reshape(high_rows, columns).astype(F32) * smooth_ref[b].reshape(
                 high_rows, columns
             )
-        high, low = split(share.T)
-        table_ref[f * LANES : (f + 1) * LANES] = high
-        table_ref[(f + 2) * LANES : (f + 3) * LANES] = low
-    row_of = iota((high_rows, LANES), 0)
+        shares.append(share)
+    largest = jnp.maximum(jnp.max(jnp.maximum(jnp.abs(shares[0]), jnp.abs(shares[1]))), 1e-30)
+    scale, back = 256.0 / largest, largest * (1.0 / 256.0)
+    for f in range(2):
+        rest_of = shares[f].T * scale
+        for k in range(PIECES):
+            piece = rest_of.astype(F8)
+            table_ref[(2 * k + f) * LANES : (2 * k + f + 1) * LANES] = piece
+            rest_of = (rest_of - piece.astype(F32)) * 16.0
+    row_of = iota((256, LANES), 0).astype(F32).astype(BF16)
     lane_of = iota((LANES, LANES), 0)
-    for block in range(blocks):
-        ray = rays[block]
-
-        def chunk(c, _, ray=ray, block=block):
-            at = pl.ds(pl.multiple_of(c * 8, 8), 8)
-            high, low = indices(ray[0, at, :])
-            first, second = ray[1, at, :], ray[2, at, :]
-            lines = []
-            for pair in range(4):
-                hot = jnp.concatenate(
-                    [
-                        jnp.where(row_of == high[r : r + 1], 1.0, 0.0).astype(BF16)
-                        for r in (2 * pair, 2 * pair + 1)
-                    ],
-                    axis=1,
-                )
-                got = dot(table_ref[...], hot)
-                for h in range(2):
-                    r = 2 * pair + h
-                    part = got[:, h * LANES : (h + 1) * LANES]
-                    u = part[:LANES] + part[2 * LANES : 3 * LANES]
-                    v = part[LANES : 2 * LANES] + part[3 * LANES :]
-                    both = u * first[r : r + 1] + v * second[r : r + 1]
-                    lines.append(
-                        jnp.sum(jnp.where(lane_of == low[r : r + 1], both, 0.0), axis=0, keepdims=True)
-                    )
-            out_ref[block, at, :] = jnp.concatenate(lines, axis=0)
-            return 0
-
-        lax.fori_loop(0, ray.shape[1] // 8, chunk, 0)
-
-
-def scatter_kernel(tiles, blocks, rate_ref, high_ref, low_ref, members_ref, own_ref, *rest):
-    others, rays = rest[: blocks - 1], rest[blocks - 1 : 2 * blocks - 1]
-    out_ref = rest[2 * blocks - 1]
-    outs = rest[2 * blocks : 2 * blocks + tiles - 1]
-    total_ref, mixed_ref = rest[2 * blocks + tiles - 1 :]
+
+    @chunks_of(out_ref.shape)
+    def _(s, at):
+        high, low = indices(ray[s, 0, at, :])
+        hot_row = hot_rows(high, row_of, high_rows)
+        first, second = ray[s, 1, at, :] * back, ray[s, 2, at, :] * back
+        lines = []
+        for pair in range(4):
+            hot = jnp.concatenate([hot_row(2 * pair), hot_row(2 * pair + 1)], axis=1).astype(F8)
+            got = dot(table_ref[...], hot)
+            total = got[: 2 * LANES]
+            for k in range(1, PIECES):
+                total = total + got[2 * k * LANES : 2 * (k + 1) * LANES] * 16.0**-k
+            for h in range(2):
+                r = 2 * pair + h
+                here = lane_of == low[r : r + 1]
+                part = total[:, h * LANES : (h + 1) * LANES]
+                u = jnp.sum(jnp.where(here, part[:LANES], 0.0), axis=0, keepdims=True)
+                v = jnp.sum(jnp.where(here, part[LANES:], 0.0), axis=0, keepdims=True)
+                lines.append(u * first[r : r + 1] + v * second[r : r + 1])
+        out_ref[s, at, :] = jnp.concatenate(lines, axis=0)
+
+
+def scatter_kernel(tiles, blocks, rate_ref, high_ref, low_ref, members_ref, ray, *rest):
+    partial = rest[:blocks]
+    out_ref = rest[blocks]
+    outs = rest[blocks + 1 : blocks + tiles]
+    total_ref, mixed_ref = rest[blocks + tiles :]
     members, levels, rows, columns = out_ref.shape
     high_rows = levels * rows
-    row_of = iota((high_rows, LANES), 0)
-    lane_of = iota((LANES, LANES), 0)
+    row_of = iota((256, LANES), 0).astype(F32).astype(BF16)
+    lane_of = iota((LANES, LANES), 0).astype(F32).astype(BF16)
+    none = jnp.zeros((), BF16)
     total_ref[...] = jnp.zeros_like(total_ref)
-    for block in range(blocks):
-        ray = rays[block]
-
-        def chunk(c, _, ray=ray, block=block):
-            at = pl.ds(pl.multiple_of(c * 8, 8), 8)
-            high, low = indices(ray[0, at, :])
-            modelled = own_ref[block, at, :]
-            for k in range(1, blocks):
-                modelled = modelled + others[k - 1][block ^ k, at, :]
-            departure = ray[4, at, :] * (modelled - ray[3, at, :])
-            values = []
-            for f in range(2):
-                value = ray[1 + f, at, :] * departure
-                part = value.astype(BF16).astype(F32)
-                values.append((part, value - part))
-            hots, sides = [], [[], []]
-            for r in range(8):
-                hots.append(jnp.where(row_of == high[r : r + 1], 1.0, 0.0).astype(BF16))
-                here = lane_of == low[r : r + 1]
-                for piece in range(2):
-                    sides[piece].append(
-                        jnp.concatenate(
-                            [jnp.where(here, values[f][piece][r : r + 1], 0.0).astype(BF16) for f in range(2)],
-                            axis=0,
-                        )
+
+    @chunks_of(partial[0].shape)
+    def _(s, at):
+        high, low = indices(ray[s, 0, at, :])
+        hot_row = hot_rows(high, row_of, high_rows)
+        low = low.astype(F32)
+        modelled = partial[0][s, at, :]
+        for other in partial[1:]:
+            modelled = modelled + other[s, at, :]
+        departure = ray[s, 4, at, :] * (modelled - ray[s, 3, at, :])
+        values = []
+        for f in range(2):
+            value = ray[s, 1 + f, at, :] * departure
+            part = value.astype(BF16).astype(F32)
+            values.append((part, value - part))
+        sides = [[], []]
+        for r in range(8):
+            here = lane_of == low[r : r + 1].astype(BF16)
+            for piece in range(2):
+                sides[piece].append(
+                    jnp.concatenate(
+                        [jnp.where(here, values[f][piece][r : r + 1].astype(BF16), none) for f in range(2)], axis=0
                     )
-            left = jnp.concatenate(hots, axis=1)
-            dims = (((1,), (1,)), ((), ()))
-            added = None
-            for piece in range(2):
-                right = jnp.concatenate(sides[piece], axis=1)
-                term = lax.dot_general(left, right, dims, preferred_element_type=F32)
-                added = term if added is None else added + term
-            total_ref[...] += added
-            return 0
-
-        lax.fori_loop(0, ray.shape[1] // 8, chunk, 0)
+                )
+        left = [hot_row(r) for r in range(8)]
+        total_ref[...] += lax.dot_general(
+            jnp.concatenate(left + left, axis=1),
+            jnp.concatenate(sides[0] + sides[1], axis=1),
+            (((1,), (1,)), ((), ())),
+            preferred_element_type=F32,
+        )
+
     for l in range(levels):
         u = total_ref[l * rows : (l + 1) * rows, :LANES]
         v = total_ref[l * rows : (l + 1) * rows, LANES:]
@@ -344,16 +365,14 @@
     tiles, blocks = lax.axis_size("tile"), lax.axis_size("mem")
     count_rays, gates = observed.shape
     capacity = 3 * count_rays // tiles
-    per = -(-capacity * (gates // LANES) // blocks)
+    per = -(-capacity * (gates // LANES) // 8) * 8
     shape = alpha.shape
     count, levels, rows, columns = shape
-    sent = call(
-        functools.partial(pack_rays_kernel, tiles, per),
-        [shaped(FIELDS, per, LANES) for _ in range(tiles)],
-    )(owner, cell_index, ray_weights, observed, precision)
+    ray = call(functools.partial(pack_rays_kernel, per), shaped(tiles, 5, per, LANES))(
+        owner, cell_index, ray_weights, observed, precision
+    )
+    ray = lax.all_to_all(ray, "tile", split_axis=0, concat_axis=0, tiled=True)
     rate = jnp.broadcast_to((-1.0 / scales)[:, None], (levels, LANES))
-    here = jnp.concatenate([sent[0], *over_tiles(sent[1:], tiles)], axis=1)
-    rays = [here, *over_members(here, blocks)]
 
     state = shaped(count, levels, columns)
     high, low, field, *given = call(
@@ -364,16 +383,17 @@
     received = over_tiles(given, tiles)
     own = call(functools.partial(within_kernel, tiles), shaped(*shape))(rate, field)
     modelled = call(
-        functools.partial(gather_kernel, tiles, blocks),
-        shaped(blocks, tiles * per, LANES),
-        [pltpu.VMEM(shape, F32), pltpu.VMEM((4 * LANES, levels * rows), BF16)],
-    )(rate, own, members, *received, *rays)
-    others = over_members(modelled, blocks)
+        functools.partial(gather_kernel, tiles),
+        shaped(tiles, per, LANES),
+        [pltpu.VMEM(shape, F32), pltpu.VMEM((2 * PIECES * LANES, levels * rows), F8)],
+        COST,
+    )(rate, own, members, *received, ray)
     field, *given = call(
         functools.partial(scatter_kernel, tiles, blocks),
         [shaped(*shape)] + [state] * (tiles - 1),
         [pltpu.VMEM((levels * rows, 2 * LANES), F32), pltpu.VMEM(shape, F32)],
-    )(rate, high, low, members, modelled, *others, *rays)
+        COST,
+    )(rate, high, low, members, ray, modelled, *over_members(modelled, blocks))
     received = over_tiles(given, tiles)
     own = call(functools.partial(within_kernel, tiles), shaped(*shape))(rate, field)
     return call(functools.partial(last_kernel, tiles), shaped(*shape))(rate, alpha, own, *received)

time: 97.7 us -> 81.3 us (0.83)
  Pallas kernels: 45.3 us -> 36.1 us
  waiting for transfers between devices: 19.2 us -> 14.8 us
  local copies, waits for them, and re-layouts: 5.4 us -> 3.94 us
    pallas_call x7, Pallas kernels: 45.3 us -> 36.1 us  [run(): pl.pallas_call(body, out_shape=outs, in_specs=[VMEM] * len(args), out_spe...]
    all_to_all x0 -> x1, starting transfers between devices: none -> 6.46 us  [per_device(): ray = lax.all_to_all(ray, 'tile', split_axis=0, concat_axis=0, tiled=True)]
    ppermute x21 -> x14, waiting for transfers between devices: 14.3 us -> 9.73 us  [over_tiles(): lax.ppermute(part, 'tile', [(i, (i + k) % tiles) for i in range(tiles)])]
    ppermute x6 -> x3, starting transfers between devices: 7.11 us -> 3.55 us  [over_members(): lax.ppermute(part, 'mem', [(i, i ^ k) for i in range(blocks)])]
    ppermute x21 -> x14, starting transfers between devices: 19.5 us -> 15.9 us  [over_tiles(): lax.ppermute(part, 'tile', [(i, (i + k) % tiles) for i in range(tiles)])]
    unnamed x17 -> x19, local copies, waits for them, and re-layouts: 4.91 us -> 3.87 us
    ppermute x6 -> x3, waiting for transfers between devices: 4.93 us -> 5.04 us  [over_members(): lax.ppermute(part, 'mem', [(i, i ^ k) for i in range(blocks)])]
  transfers between devices with their start and end apart: 27 -> 18, of which waited for: 10 -> 10; matrix products, arithmetic and copies ran while one was open for 1% -> 0% of each run, Pallas kernels for 5% -> 5%
where the time goes in v2:
time: 81.3 us; the launch traced here: 80.9 us
  Pallas kernels  36.1 us (44%)
  starting transfers between devices  25.9 us (32%)
  waiting for transfers between devices  14.8 us (18%)
  local copies, waits for them, and re-layouts  3.94 us (5%)
    pallas_call x7, Pallas kernels, run(): pl.pallas_call(body, out_shape=outs, in_specs=[VMEM] * len(args), out_spe...  36.1 us
    ppermute x14, starting transfers between devices, over_tiles(): lax.ppermute(part, 'tile', [(i, (i + k) % tiles) for i in range(tiles)])  15.9 us
    ppermute x14, waiting for transfers between devices, over_tiles(): lax.ppermute(part, 'tile', [(i, (i + k) % tiles) for i in range(tiles)])  9.73 us
    all_to_all x1, starting transfers between devices, per_device(): ray = lax.all_to_all(ray, 'tile', split_axis=0, concat_axis=0, tiled=True)  6.46 us
    ppermute x3, waiting for transfers between devices, over_members(): lax.ppermute(part, 'mem', [(i, i ^ k) for i in range(blocks)])  5.04 us
    unnamed x19, local copies, waits for them, and re-layouts  3.87 us
    ppermute x3, starting transfers between devices, over_members(): lax.ppermute(part, 'mem', [(i, i ^ k) for i in range(blocks)])  3.55 us
  transfers between devices with their start and end apart: 18, of which 10 were waited for; matrix products, arithmetic and copies ran while one was open for 0% of the time, Pallas kernels for 5%

profile of v2, /device:TPU:0, one launch (start us, length us, event | category | flops | bytes accessed | tf_op | source)
XLA Modules:
  0.0 80.9 jit_solution(9931758795282041472)
XLA Ops:
  0.0 0.7 copy.9.owner_ref
  0.7 0.8 %copy-done.1 = f32[32,2,256]{2,1,0:T(2,128)S(1)} copy-done((f32[32,2,256]{2,1,0:T(2,128)S(1)}, f32[32,2,256]{2,1,0:T(2,128)}, u32[]{:S(2)}) %copy-start.1) | copy-done | bytes 65560
  1.6 0.8 copy-done.2
  2.3 0.8 copy-done.3
  3.1 0.8 copy-done.4
  3.9 2.0 %shard_map.83 = f32[8,5,24,128]{3,2,1,0:T(8,128)} custom-call(s32[32,1]{1,0:T(8,128)S(1)} %copy.9.owner_ref, s32[32,256]{1,0:T(8,128)S(1)} %copy-done.2, f32[32,2,256]{2,1,0:T(2,128)S(1)} %copy-done.1, f32[32,256]{1,0:T(8,128)S(1)} %copy-done.3, f32[32,256]{1,0:T(8,128)S(1)} %copy-done.4), custom_call_target="tpu_custom_call" | custom-call | tf_op jit(solution)/shard_map/pallas_call | solution.py:336
  5.9 6.5 %all-to-all-start = ((f32[8,5,24,128]{3,2,1,0:T(8,128)}), f32[8,5,24,128]{3,2,1,0:T(8,128)S(1)}, u32[]{:S(2)}, u32[]{:S(2)}) async-start(f32[8,5,24,128]{3,2,1,0:T(8,128)} %shard_map.83), calls=%async_computation | async-start | bytes 983040 | tf_op jit(solution)/shard_map/all_to_all | solution.py:374
  12.3 0.1 broadcast_in_dim.2.rate_ref
  12.4 3.3 %shard_map.82 = (bf16[32,128,128]{2,1,0:T(8,128)(2,1)S(1)}, bf16[32,128,128]{2,1,0:T(8,128)(2,1)S(1)}, f32[2,32,16,128]{3,2,1,0:T(8,128)S(1)}, f32[2,32,128]{2,1...) custom-call(f32[32,128]{1,0:T(8,128)S(1)} %broadcast_in_dim.2.rate_r, ...), custom_call_target="tpu_custom_call" | custom-call | tf_op jit(solution)/shard_map/pallas_call | solution.py:336
  15.7 0.5 collective-permute-start
  16.2 1.7 %collective-permute-start.1 = (f32[2,32,128]{2,1,0:T(8,128)S(1)}, f32[2,32,128]{2,1,0:T(8,128)S(1)}, u32[]{:S(2)}, u32[]{:S(2)}) collective-permute-start(f32[2,32,128]{2,1,0:T(8,128)S(1)} %get-tuple-element.27), channel_id=1, source_target_pairs={{0,2},{1,3},{2,4},{3,5},{4,6},{5,7},{6,0},{7,1},{8,10},{9,11},{10,... | collective-permute-start | bytes 98312 | tf_op jit(solution)/shard_map/ppermute | solution.py:355
  17.9 2.2 %collective-permute-start.2 = (f32[2,32,128]{2,1,0:T(8,128)S(1)}, f32[2,32,128]{2,1,0:T(8,128)S(1)}, u32[]{:S(2)}, u32[]{:S(2)}) collective-permute-start(f32[2,32,128]{2,1,0:T(8,128)S(1)} %get-tuple-element.28), channel_id=1, source_target_pairs={{0,3},{1,4},{2,5},{3,6},{4,7},{5,0},{6,1},{7,2},{8,11},{9,12},{10,... | collective-permute-start | bytes 98312 | tf_op jit(solution)/shard_map/ppermute | solution.py:355
  20.1 1.5 %collective-permute-start.3 = (f32[2,32,128]{2,1,0:T(8,128)S(1)}, f32[2,32,128]{2,1,0:T(8,128)S(1)}, u32[]{:S(2)}, u32[]{:S(2)}) collective-permute-start(f32[2,32,128]{2,1,0:T(8,128)S(1)} %get-tuple-element.29), channel_id=1, source_target_pairs={{0,4},{1,5},{2,6},{3,7},{4,0},{5,1},{6,2},{7,3},{8,12},{9,13},{10,... | collective-permute-start | bytes 98312 | tf_op jit(solution)/shard_map/ppermute | solution.py:355
  21.6 1.1 %collective-permute-start.4 = (f32[2,32,128]{2,1,0:T(8,128)S(1)}, f32[2,32,128]{2,1,0:T(8,128)S(1)}, u32[]{:S(2)}, u32[]{:S(2)}) collective-permute-start(f32[2,32,128]{2,1,0:T(8,128)S(1)} %get-tuple-element.30), channel_id=1, source_target_pairs={{0,5},{1,6},{2,7},{3,0},{4,1},{5,2},{6,3},{7,4},{8,13},{9,14},{10,... | collective-permute-start | bytes 98312 | tf_op jit(solution)/shard_map/ppermute | solution.py:355
  22.6 3.0 %collective-permute-done.rest_0_ = f32[2,32,128]{2,1,0:T(8,128)S(1)} collective-permute-done((f32[2,32,128]{2,1,0:T(8,128)S(1)}, f32[2,32,128]{2,1,0:T(8,128)S(1)}, u32[]{:S(2)}, u32[]{:S(2)}) %collective-permute-start) | collective-permute-done | bytes 32800 | tf_op jit(solution)/shard_map/ppermute | solution.py:355
  25.6 0.0 collective-permute-start.5
  25.6 0.9 %collective-permute-done.1.rest_1_ = f32[2,32,128]{2,1,0:T(8,128)S(1)} collective-permute-done((f32[2,32,128]{2,1,0:T(8,128)S(1)}, f32[2,32,128]{2,1,0:T(8,128)S(1)}, u32[]{:S(2)}, u32[]{:S(2)}) %collective-permute-start.1) | collective-permute-done | bytes 32800 | tf_op jit(solution)/shard_map/ppermute | solution.py:355
  26.6 0.0 collective-permute-start.6
  26.6 0.6 shard_map.84.own_ref
  27.1 3.0 %collective-permute-done.2.rest_2_ = f32[2,32,128]{2,1,0:T(8,128)S(1)} collective-permute-done((f32[2,32,128]{2,1,0:T(8,128)S(1)}, f32[2,32,128]{2,1,0:T(8,128)S(1)}, u32[]{:S(2)}, u32[]{:S(2)}) %collective-permute-start.2) | collective-permute-done | bytes 32800 | tf_op jit(solution)/shard_map/ppermute | solution.py:355
  30.1 0.9 %collective-permute-done.3.rest_3_ = f32[2,32,128]{2,1,0:T(8,128)S(1)} collective-permute-done((f32[2,32,128]{2,1,0:T(8,128)S(1)}, f32[2,32,128]{2,1,0:T(8,128)S(1)}, u32[]{:S(2)}, u32[]{:S(2)}) %collective-permute-start.3) | collective-permute-done | bytes 32800 | tf_op jit(solution)/shard_map/ppermute | solution.py:355
  31.0 0.0 collective-permute-done.4.rest_4_
  31.0 0.9 %collective-permute-done.5.rest_5_ = f32[2,32,128]{2,1,0:T(8,128)S(1)} collective-permute-done((f32[2,32,128]{2,1,0:T(8,128)S(1)}, f32[2,32,128]{2,1,0:T(8,128)S(1)}, u32[]{:S(2)}, u32[]{:S(2)}) %collective-permute-start.5) | collective-permute-done | bytes 32800 | tf_op jit(solution)/shard_map/ppermute | solution.py:355
  31.9 0.0 collective-permute-done.6.rest_6_
  31.9 0.0 all-to-all-done.rest_7_.ray
  31.9 12.9 %shard_map.85.rest_0_ = f32[8,24,128]{2,1,0:T(8,128)S(1)} custom-call(f32[32,128]{1,0:T(8,128)S(1)} %broadcast_in_dim.2.rate_ref, f32[2,32,16,128]{3,2,1,0:T(8,128)S(1)} %shard_map.84.own_ref, bf16[2,2,32,16,128]{4,3,2,1,0:T(8,128)(2,1)S(1)} %copy-done.7, f32[2,32,128]{2,1,0:T(8,128)S(1)} %collective-permute-done.rest_0_, ...), custom_call_target="tpu_custom_call" | custom-call | flops 20000000000 | bytes 4000000 | tf_op jit(solution)/shard_map/pallas_call | solution.py:336
  44.8 1.6 %collective-permute-start.7 = (f32[8,24,128]{2,1,0:T(8,128)S(1)}, f32[8,24,128]{2,1,0:T(8,128)S(1)}, u32[]{:S(2)}, u32[]{:S(2)}) collective-permute-start(f32[8,24,128]{2,1,0:T(8,128)S(1)} %shard_map.85.rest_0_), channel_id=1, source_target_pairs={{0,8},{8,0},{16,24},{24,16},{1,9},{9,1},{17,25},{25,17},{2,10},{10... | collective-permute-start | bytes 294920 | tf_op jit(solution)/shard_map/ppermute | solution.py:361
  46.4 1.5 %collective-permute-start.8 = (f32[8,24,128]{2,1,0:T(8,128)S(1)}, f32[8,24,128]{2,1,0:T(8,128)S(1)}, u32[]{:S(2)}, u32[]{:S(2)}) collective-permute-start(f32[8,24,128]{2,1,0:T(8,128)S(1)} %shard_map.85.rest_0_), channel_id=1, source_target_pairs={{0,16},{8,24},{16,0},{24,8},{1,17},{9,25},{17,1},{25,9},{2,18},{10... | collective-permute-start | bytes 294920 | tf_op jit(solution)/shard_map/ppermute | solution.py:361
  47.9 0.5 collective-permute-start.9
  48.4 1.4 %collective-permute-done.7.rest_1_ = f32[8,24,128]{2,1,0:T(8,128)S(1)} collective-permute-done((f32[8,24,128]{2,1,0:T(8,128)S(1)}, f32[8,24,128]{2,1,0:T(8,128)S(1)}, u32[]{:S(2)}, u32[]{:S(2)}) %collective-permute-start.7) | collective-permute-done | bytes 98336 | tf_op jit(solution)/shard_map/ppermute | solution.py:361
  49.7 2.4 %collective-permute-done.8.rest_2_ = f32[8,24,128]{2,1,0:T(8,128)S(1)} collective-permute-done((f32[8,24,128]{2,1,0:T(8,128)S(1)}, f32[8,24,128]{2,1,0:T(8,128)S(1)}, u32[]{:S(2)}, u32[]{:S(2)}) %collective-permute-start.8) | collective-permute-done | bytes 98336 | tf_op jit(solution)/shard_map/ppermute | solution.py:361
  52.1 1.3 %collective-permute-done.9.rest_3_ = f32[8,24,128]{2,1,0:T(8,128)S(1)} collective-permute-done((f32[8,24,128]{2,1,0:T(8,128)S(1)}, f32[8,24,128]{2,1,0:T(8,128)S(1)}, u32[]{:S(2)}, u32[]{:S(2)}) %collective-permute-start.9) | collective-permute-done | bytes 98336 | tf_op jit(solution)/shard_map/ppermute | solution.py:361
  53.4 15.7 %shard_map.86 = (f32[2,32,16,128]{3,2,1,0:T(8,128)S(1)}, f32[2,32,128]{2,1,0:T(8,128)S(1)}, f32[2,32,128]{2,1,0:T(8,128)S(1)}, f32[2,32,128]{2,1,0:T(8,128)S(1)}...) custom-call(f32[32,128]{1,0:T(8,128)S(1)} %broadcast_in_dim.2.rate_r, ...), custom_call_target="tpu_custom_call" | custom-call | flops 20000000000 | bytes 4000000 | tf_op jit(solution)/shard_map/pallas_call | solution.py:336
  69.2 0.0 collective-permute-start.10
  69.2 1.0 %collective-permute-start.11 = (f32[2,32,128]{2,1,0:T(8,128)S(1)}, f32[2,32,128]{2,1,0:T(8,128)S(1)}, u32[]{:S(2)}, u32[]{:S(2)}) collective-permute-start(f32[2,32,128]{2,1,0:T(8,128)S(1)} %get-tuple-element.35), channel_id=1, source_target_pairs={{0,2},{1,3},{2,4},{3,5},{4,6},{5,7},{6,0},{7,1},{8,10},{9,11},{10,... | collective-permute-start | bytes 98312 | tf_op jit(solution)/shard_map/ppermute | solution.py:355
  70.2 1.7 %collective-permute-start.12 = (f32[2,32,128]{2,1,0:T(8,128)S(1)}, f32[2,32,128]{2,1,0:T(8,128)S(1)}, u32[]{:S(2)}, u32[]{:S(2)}) collective-permute-start(f32[2,32,128]{2,1,0:T(8,128)S(1)} %get-tuple-element.36), channel_id=1, source_target_pairs={{0,3},{1,4},{2,5},{3,6},{4,7},{5,0},{6,1},{7,2},{8,11},{9,12},{10,... | collective-permute-start | bytes 98312 | tf_op jit(solution)/shard_map/ppermute | solution.py:355
  71.8 2.1 %collective-permute-start.13 = (f32[2,32,128]{2,1,0:T(8,128)S(1)}, f32[2,32,128]{2,1,0:T(8,128)S(1)}, u32[]{:S(2)}, u32[]{:S(2)}) collective-permute-start(f32[2,32,128]{2,1,0:T(8,128)S(1)} %get-tuple-element.37), channel_id=1, source_target_pairs={{0,4},{1,5},{2,6},{3,7},{4,0},{5,1},{6,2},{7,3},{8,12},{9,13},{10,... | collective-permute-start | bytes 98312 | tf_op jit(solution)/shard_map/ppermute | solution.py:355
  73.9 0.3 collective-permute-start.14
  74.3 0.1 collective-permute-done.10.rest_0_
  74.3 2.5 %collective-permute-start.15 = (f32[2,32,128]{2,1,0:T(8,128)S(1)}, f32[2,32,128]{2,1,0:T(8,128)S(1)}, u32[]{:S(2)}, u32[]{:S(2)}) collective-permute-start(f32[2,32,128]{2,1,0:T(8,128)S(1)} %get-tuple-element.39), channel_id=1, source_target_pairs={{0,6},{1,7},{2,0},{3,1},{4,2},{5,3},{6,4},{7,5},{8,14},{9,15},{10,... | collective-permute-start | bytes 98312 | tf_op jit(solution)/shard_map/ppermute | solution.py:355
  76.8 0.0 collective-permute-done.11.rest_1_
  76.8 1.4 %collective-permute-start.16 = (f32[2,32,128]{2,1,0:T(8,128)S(1)}, f32[2,32,128]{2,1,0:T(8,128)S(1)}, u32[]{:S(2)}, u32[]{:S(2)}) collective-permute-start(f32[2,32,128]{2,1,0:T(8,128)S(1)} %get-tuple-element.40), channel_id=1, source_target_pairs={{0,7},{1,0},{2,1},{3,2},{4,3},{5,4},{6,5},{7,6},{8,15},{9,8},{10,9... | collective-permute-start | bytes 98312 | tf_op jit(solution)/shard_map/ppermute | solution.py:355
  78.2 0.6 shard_map.87.own_ref
  78.8 0.0 collective-permute-done.12.rest_2_
  78.8 0.0 collective-permute-done.14.rest_4_
  78.8 0.0 collective-permute-done.15.rest_5_
  78.9 1.0 %collective-permute-done.16.rest_6_ = f32[2,32,128]{2,1,0:T(8,128)S(1)} collective-permute-done((f32[2,32,128]{2,1,0:T(8,128)S(1)}, f32[2,32,128]{2,1,0:T(8,128)S(1)}, u32[]{:S(2)}, u32[]{:S(2)}) %collective-permute-start.16) | collective-permute-done | bytes 32800 | tf_op jit(solution)/shard_map/ppermute | solution.py:355
  79.8 1.1 %shard_map.88 = f32[2,32,16,128]{3,2,1,0:T(8,128)} custom-call(f32[32,128]{1,0:T(8,128)S(1)} %broadcast_in_dim.2.rate_ref, f32[2,32,16,128]{3,2,1,0:T(8,128)S(1)} %copy-done, f32[2,32,16,128]{3,2,1,0:T(8,128)S(1)} %shard_map.87.own_ref, f32[2,32,128]{2,1,0:T(8,128)S(1)} %collective-permute-done.10.rest_0_, ...), custom_call_target="tpu_custom_call" | custom-call | tf_op jit(solution)/shard_map/pallas_call | solution.py:336
  (16 shorter events, 0.0 us)
Async XLA Ops:
  0.7 0.8 %copy-start.1 = (f32[32,2,256]{2,1,0:T(2,128)S(1)}, f32[32,2,256]{2,1,0:T(2,128)}, u32[]{:S(2)}) copy-start(f32[32,2,256]{2,1,0:T(2,128)} %weights_ref.1) | copy-start | bytes 196612
  1.6 0.8 copy-start.2
  2.3 0.8 copy-start.3
  3.1 0.8 copy-start.4
  5.9 6.5 %copy-start.8 = (f32[32]{0:T(128)S(1)}, f32[32]{0:T(128)}, u32[]{:S(2)}) copy-start(f32[32]{0:T(128)} %param.10) | copy-start | bytes 388
  5.9 6.5 %copy-start = (f32[2,32,16,128]{3,2,1,0:T(8,128)S(1)}, f32[2,32,16,128]{3,2,1,0:T(8,128)}, u32[]{:S(2)}) copy-start(f32[2,32,16,128]{3,2,1,0:T(8,128)} %alpha_ref.3) | copy-start | bytes 1572868
  5.9 26.0 %all-to-all-start = ((f32[8,5,24,128]{3,2,1,0:T(8,128)}), f32[8,5,24,128]{3,2,1,0:T(8,128)S(1)}, u32[]{:S(2)}, u32[]{:S(2)}) async-start(f32[8,5,24,128]{3,2,1,0:T(8,128)} %shard_map.83), calls=%async_computation | async-start | bytes 983040 | tf_op jit(solution)/shard_map/all_to_all | solution.py:374
  15.7 16.2 %copy-start.5 = (bf16[32,128,128]{2,1,0:T(8,128)(2,1)}, bf16[32,128,128]{2,1,0:T(8,128)(2,1)S(1)}, u32[]{:S(2)}) copy-start(bf16[32,128,128]{2,1,0:T(8,128)(2,1)S(1)} %get-tuple-element.24.low_ref) | copy-start | bytes 3145732
  15.7 9.9 %collective-permute-start = (f32[2,32,128]{2,1,0:T(8,128)S(1)}, f32[2,32,128]{2,1,0:T(8,128)S(1)}, u32[]{:S(2)}, u32[]{:S(2)}) collective-permute-start(f32[2,32,128]{2,1,0:T(8,128)S(1)} %get-tuple-element.26), channel_id=1, source_target_pairs={{0,1},{1,2},{2,3},{3,4},{4,5},{5,6},{6,7},{7,0},{8,9},{9,10},{10,1... | collective-permute-start | bytes 98312 | tf_op jit(solution)/shard_map/ppermute | solution.py:355
  16.2 10.3 %collective-permute-start.1 = (f32[2,32,128]{2,1,0:T(8,128)S(1)}, f32[2,32,128]{2,1,0:T(8,128)S(1)}, u32[]{:S(2)}, u32[]{:S(2)}) collective-permute-start(f32[2,32,128]{2,1,0:T(8,128)S(1)} %get-tuple-element.27), channel_id=1, source_target_pairs={{0,2},{1,3},{2,4},{3,5},{4,6},{5,7},{6,0},{7,1},{8,10},{9,11},{10,... | collective-permute-start | bytes 98312 | tf_op jit(solution)/shard_map/ppermute | solution.py:355
  17.9 12.2 %collective-permute-start.2 = (f32[2,32,128]{2,1,0:T(8,128)S(1)}, f32[2,32,128]{2,1,0:T(8,128)S(1)}, u32[]{:S(2)}, u32[]{:S(2)}) collective-permute-start(f32[2,32,128]{2,1,0:T(8,128)S(1)} %get-tuple-element.28), channel_id=1, source_target_pairs={{0,3},{1,4},{2,5},{3,6},{4,7},{5,0},{6,1},{7,2},{8,11},{9,12},{10,... | collective-permute-start | bytes 98312 | tf_op jit(solution)/shard_map/ppermute | solution.py:355
  20.1 10.9 %collective-permute-start.3 = (f32[2,32,128]{2,1,0:T(8,128)S(1)}, f32[2,32,128]{2,1,0:T(8,128)S(1)}, u32[]{:S(2)}, u32[]{:S(2)}) collective-permute-start(f32[2,32,128]{2,1,0:T(8,128)S(1)} %get-tuple-element.29), channel_id=1, source_target_pairs={{0,4},{1,5},{2,6},{3,7},{4,0},{5,1},{6,2},{7,3},{8,12},{9,13},{10,... | collective-permute-start | bytes 98312 | tf_op jit(solution)/shard_map/ppermute | solution.py:355
  21.6 9.4 %collective-permute-start.4 = (f32[2,32,128]{2,1,0:T(8,128)S(1)}, f32[2,32,128]{2,1,0:T(8,128)S(1)}, u32[]{:S(2)}, u32[]{:S(2)}) collective-permute-start(f32[2,32,128]{2,1,0:T(8,128)S(1)} %get-tuple-element.30), channel_id=1, source_target_pairs={{0,5},{1,6},{2,7},{3,0},{4,1},{5,2},{6,3},{7,4},{8,13},{9,14},{10,... | collective-permute-start | bytes 98312 | tf_op jit(solution)/shard_map/ppermute | solution.py:355
  25.6 6.3 %collective-permute-start.5 = (f32[2,32,128]{2,1,0:T(8,128)S(1)}, f32[2,32,128]{2,1,0:T(8,128)S(1)}, u32[]{:S(2)}, u32[]{:S(2)}) collective-permute-start(f32[2,32,128]{2,1,0:T(8,128)S(1)} %get-tuple-element.31), channel_id=1, source_target_pairs={{0,6},{1,7},{2,0},{3,1},{4,2},{5,3},{6,4},{7,5},{8,14},{9,15},{10,... | collective-permute-start | bytes 98312 | tf_op jit(solution)/shard_map/ppermute | solution.py:355
  26.6 5.3 %collective-permute-start.6 = (f32[2,32,128]{2,1,0:T(8,128)S(1)}, f32[2,32,128]{2,1,0:T(8,128)S(1)}, u32[]{:S(2)}, u32[]{:S(2)}) collective-permute-start(f32[2,32,128]{2,1,0:T(8,128)S(1)} %get-tuple-element.32), channel_id=1, source_target_pairs={{0,7},{1,0},{2,1},{3,2},{4,3},{5,4},{6,5},{7,6},{8,15},{9,8},{10,9... | collective-permute-start | bytes 98312 | tf_op jit(solution)/shard_map/ppermute | solution.py:355
  26.6 5.3 %copy-start.7 = (bf16[2,2,32,16,128]{4,3,2,1,0:T(8,128)(2,1)S(1)}, bf16[2,2,32,16,128]{4,3,2,1,0:T(8,128)(2,1)}, u32[]{:S(2)}) copy-start(bf16[2,2,32,16,128]{4,3,2,1,0:T(8,128)(2,1)} %members_ref.3) | copy-start | bytes 1572868
  31.9 21.5 %copy-start.6 = (bf16[32,128,128]{2,1,0:T(8,128)(2,1)S(1)}, bf16[32,128,128]{2,1,0:T(8,128)(2,1)}, u32[]{:S(2)}) copy-start(bf16[32,128,128]{2,1,0:T(8,128)(2,1)} %copy-done.5) | copy-start | bytes 3145732
  44.8 4.9 %collective-permute-start.7 = (f32[8,24,128]{2,1,0:T(8,128)S(1)}, f32[8,24,128]{2,1,0:T(8,128)S(1)}, u32[]{:S(2)}, u32[]{:S(2)}) collective-permute-start(f32[8,24,128]{2,1,0:T(8,128)S(1)} %shard_map.85.rest_0_), channel_id=1, source_target_pairs={{0,8},{8,0},{16,24},{24,16},{1,9},{9,1},{17,25},{25,17},{2,10},{10... | collective-permute-start | bytes 294920 | tf_op jit(solution)/shard_map/ppermute | solution.py:361
  46.4 5.8 %collective-permute-start.8 = (f32[8,24,128]{2,1,0:T(8,128)S(1)}, f32[8,24,128]{2,1,0:T(8,128)S(1)}, u32[]{:S(2)}, u32[]{:S(2)}) collective-permute-start(f32[8,24,128]{2,1,0:T(8,128)S(1)} %shard_map.85.rest_0_), channel_id=1, source_target_pairs={{0,16},{8,24},{16,0},{24,8},{1,17},{9,25},{17,1},{25,9},{2,18},{10... | collective-permute-start | bytes 294920 | tf_op jit(solution)/shard_map/ppermute | solution.py:361
  47.9 5.5 %collective-permute-start.9 = (f32[8,24,128]{2,1,0:T(8,128)S(1)}, f32[8,24,128]{2,1,0:T(8,128)S(1)}, u32[]{:S(2)}, u32[]{:S(2)}) collective-permute-start(f32[8,24,128]{2,1,0:T(8,128)S(1)} %shard_map.85.rest_0_), channel_id=1, source_target_pairs={{0,24},{8,16},{16,8},{24,0},{1,25},{9,17},{17,9},{25,1},{2,26},{10... | collective-permute-start | bytes 294920 | tf_op jit(solution)/shard_map/ppermute | solution.py:361
  69.2 5.2 %collective-permute-start.10 = (f32[2,32,128]{2,1,0:T(8,128)S(1)}, f32[2,32,128]{2,1,0:T(8,128)S(1)}, u32[]{:S(2)}, u32[]{:S(2)}) collective-permute-start(f32[2,32,128]{2,1,0:T(8,128)S(1)} %get-tuple-element.34), channel_id=1, source_target_pairs={{0,1},{1,2},{2,3},{3,4},{4,5},{5,6},{6,7},{7,0},{8,9},{9,10},{10,1... | collective-permute-start | bytes 98312 | tf_op jit(solution)/shard_map/ppermute | solution.py:355
  69.2 7.6 %collective-permute-start.11 = (f32[2,32,128]{2,1,0:T(8,128)S(1)}, f32[2,32,128]{2,1,0:T(8,128)S(1)}, u32[]{:S(2)}, u32[]{:S(2)}) collective-permute-start(f32[2,32,128]{2,1,0:T(8,128)S(1)} %get-tuple-element.35), channel_id=1, source_target_pairs={{0,2},{1,3},{2,4},{3,5},{4,6},{5,7},{6,0},{7,1},{8,10},{9,11},{10,... | collective-permute-start | bytes 98312 | tf_op jit(solution)/shard_map/ppermute | solution.py:355
  70.2 8.6 %collective-permute-start.12 = (f32[2,32,128]{2,1,0:T(8,128)S(1)}, f32[2,32,128]{2,1,0:T(8,128)S(1)}, u32[]{:S(2)}, u32[]{:S(2)}) collective-permute-start(f32[2,32,128]{2,1,0:T(8,128)S(1)} %get-tuple-element.36), channel_id=1, source_target_pairs={{0,3},{1,4},{2,5},{3,6},{4,7},{5,0},{6,1},{7,2},{8,11},{9,12},{10,... | collective-permute-start | bytes 98312 | tf_op jit(solution)/shard_map/ppermute | solution.py:355
  71.8 7.0 %collective-permute-start.13 = (f32[2,32,128]{2,1,0:T(8,128)S(1)}, f32[2,32,128]{2,1,0:T(8,128)S(1)}, u32[]{:S(2)}, u32[]{:S(2)}) collective-permute-start(f32[2,32,128]{2,1,0:T(8,128)S(1)} %get-tuple-element.37), channel_id=1, source_target_pairs={{0,4},{1,5},{2,6},{3,7},{4,0},{5,1},{6,2},{7,3},{8,12},{9,13},{10,... | collective-permute-start | bytes 98312 | tf_op jit(solution)/shard_map/ppermute | solution.py:355
  73.9 4.9 %collective-permute-start.14 = (f32[2,32,128]{2,1,0:T(8,128)S(1)}, f32[2,32,128]{2,1,0:T(8,128)S(1)}, u32[]{:S(2)}, u32[]{:S(2)}) collective-permute-start(f32[2,32,128]{2,1,0:T(8,128)S(1)} %get-tuple-element.38), channel_id=1, source_target_pairs={{0,5},{1,6},{2,7},{3,0},{4,1},{5,2},{6,3},{7,4},{8,13},{9,14},{10,... | collective-permute-start | bytes 98312 | tf_op jit(solution)/shard_map/ppermute | solution.py:355
  74.3 4.5 %collective-permute-start.15 = (f32[2,32,128]{2,1,0:T(8,128)S(1)}, f32[2,32,128]{2,1,0:T(8,128)S(1)}, u32[]{:S(2)}, u32[]{:S(2)}) collective-permute-start(f32[2,32,128]{2,1,0:T(8,128)S(1)} %get-tuple-element.39), channel_id=1, source_target_pairs={{0,6},{1,7},{2,0},{3,1},{4,2},{5,3},{6,4},{7,5},{8,14},{9,15},{10,... | collective-permute-start | bytes 98312 | tf_op jit(solution)/shard_map/ppermute | solution.py:355
  76.8 3.0 %collective-permute-start.16 = (f32[2,32,128]{2,1,0:T(8,128)S(1)}, f32[2,32,128]{2,1,0:T(8,128)S(1)}, u32[]{:S(2)}, u32[]{:S(2)}) collective-permute-start(f32[2,32,128]{2,1,0:T(8,128)S(1)} %get-tuple-element.40), channel_id=1, source_target_pairs={{0,7},{1,0},{2,1},{3,2},{4,3},{5,4},{6,5},{7,6},{8,15},{9,8},{10,9... | collective-permute-start | bytes 98312 | tf_op jit(solution)/shard_map/ppermute | solution.py:355

commit v3 on v2

--- a/solution.py
+++ b/solution.py
@@ -18,6 +18,7 @@
 Z_GAIN = (1.0 - Z_DECAY) ** 2 * math.sqrt((1.0 + Z_DECAY) / (1.0 - Z_DECAY))
 VMEM = pl.BlockSpec(memory_space=pltpu.VMEM)
 COST = pl.CostEstimate(flops=2 * 10**10, bytes_accessed=4 * 10**6, transcendentals=0)
+WIDE = pltpu.CompilerParams(vmem_limit_bytes=65000 * 1024)
 PARAMS = pltpu.CompilerParams(vmem_limit_bytes=48 * 1024 * 1024)
 
 
@@ -47,19 +48,30 @@
     return jnp.sqrt(x * series / (1.0 + jnp.exp(rate)))
 
 
-def pack_rays_kernel(per, owner_ref, cell_ref, weights_ref, observed_ref, precision_ref, out_ref):
-    rays, gates = observed_ref.shape
-    halves = gates // LANES
-    wide = out_ref.shape[0] * per
-    owner = owner_ref[...]
-    named = (owner == iota((rays, LANES), 1)).astype(F32)
-    earlier = (iota((rays, rays), 0) > iota((rays, rays), 1)).astype(F32)
-    rank = jnp.sum(dot(earlier, named) * named, axis=1, keepdims=True).astype(I32)
-    column = iota((rays, -(-wide // LANES) * LANES), 1)
-    target, row = column // per, column % per
-    picks = [
-        ((owner == target) & (rank * halves + half == row)).astype(F32).T[:wide] for half in range(halves)
-    ]
+def pack_rays_kernel(per, *refs):
+    given, (out_ref, rate_ref), held, sems = refs[:6], refs[6:8], refs[8:14], refs[14]
+    copies = [pltpu.make_async_copy(given[k], held[k], sems.at[k]) for k in range(6)]
+    for copy in copies:
+        copy.start()
+    for copy in copies:
+        copy.wait()
+    owner_ref, scales_ref, held = held[0], held[1], held[2:]
+    levels = rate_ref.shape[0]
+    here = iota((levels, levels), 0) == iota((levels, levels), 1)
+    scale = jnp.sum(jnp.where(here, scales_ref[...], 0.0), axis=1, keepdims=True)
+    rate_ref[...] = -1.0 / jnp.broadcast_to(scale, rate_ref.shape)
+    rays, gates = held[0].shape
+    tiles, halves = out_ref.shape[0], gates // LANES
+    part = lax.axis_index("mem")
+    row = iota((tiles * per, rays), 0)
+    target, wanted = row // per, row % per + part * per
+    named = owner_ref[...] == target
+    earlier = (iota((rays, rays), 0) < iota((rays, rays), 1)).astype(F32)
+    rank = dot(named.astype(F32), earlier).astype(I32)
+    picks = jnp.concatenate(
+        [(named & (rank * halves + half == wanted)).astype(F32) for half in range(halves)], axis=1
+    )
+    cell_ref, weights_ref, observed_ref, precision_ref = held
     fields = (
         cell_ref[...].astype(F32),
         weights_ref[:, 0, :],
@@ -67,17 +79,17 @@
         observed_ref[...],
         precision_ref[...],
     )
-    for f, field in enumerate(fields):
-        got = sum(
-            jnp.dot(
-                picks[half],
-                field[:, half * LANES : (half + 1) * LANES],
-                precision=lax.Precision.HIGHEST,
-                preferred_element_type=F32,
-            )
-            for half in range(halves)
-        )
-        out_ref[:, f] = got.reshape(-1, per, LANES)
+    stacked = jnp.concatenate(
+        [
+            jnp.concatenate([field[:, h * LANES : (h + 1) * LANES] for h in range(halves)], axis=0)
+            for field in fields
+        ],
+        axis=1,
+    )
+    got = jnp.dot(picks, stacked, precision=lax.Precision.HIGHEST, preferred_element_type=F32)
+    for t in range(tiles):
+        for f in range(len(fields)):
+            out_ref[t, f * per : (f + 1) * per] = got[t * per : (t + 1) * per, f * LANES : (f + 1) * LANES]
 
 
 def filter_levels(field_ref, out_ref):
@@ -121,7 +133,7 @@
     lax.fori_loop(0, levels, level, 0, unroll=2)
 
 
-def states(tiles, rate_ref, field_ref, outs):
+def states(tiles, rate_ref, field_ref, out_ref):
     members, levels, rows, columns = field_ref.shape
     place = lax.axis_index("tile")
     per = LANES // rows
@@ -138,16 +150,29 @@
         for b in range(members):
             field = field_ref[b, g * per : (g + 1) * per].reshape(per * rows, columns)
             got = dot3(both, field)
-            for k in range(1, tiles):
-                outs[k - 1][b, g * per : (g + 1) * per] = jnp.where(place + k < tiles, got[:per], got[per:])
-
-
-def first_kernel(tiles, rate_ref, alpha_ref, high_ref, low_ref, out_ref, *rest):
-    outs, scratch = rest[:-1], rest[-1]
+            for way in range(2):
+                out_ref[way, b, g * per : (g + 1) * per] = got[way * per : (way + 1) * per]
+
+
+def chip_kernel(tiles, rows, rate_ref, own_ref, partner_ref, *outs):
+    place = lax.axis_index("tile")
+    chip, upper, chips = place // 2, place % 2 == 1, tiles // 2
+    members = own_ref.shape[1]
+    across = jnp.exp(rate_ref[...] * rows)
+    for b in range(members):
+        first = [jnp.where(upper, partner_ref[way, b], own_ref[way, b]) for way in range(2)]
+        second = [jnp.where(upper, own_ref[way, b], partner_ref[way, b]) for way in range(2)]
+        forward = across * first[0] + second[0]
+        backward = first[1] + across * second[1]
+        for k in range(1, chips):
+            outs[k - 1][b] = jnp.where(chip + k < chips, forward, backward)
+
+
+def first_kernel(tiles, rate_ref, alpha_ref, high_ref, low_ref, out_ref, state_ref, scratch):
     columns_matrix(rate_ref, high_ref, low_ref)
     filter_levels(alpha_ref, scratch)
     filter_columns(scratch, high_ref, low_ref, out_ref)
-    states(tiles, rate_ref, out_ref, outs)
+    states(tiles, rate_ref, out_ref, state_ref)
 
 
 def within_kernel(tiles, rate_ref, field_ref, out_ref):
@@ -172,13 +197,15 @@
 
 def add_others(tiles, rate_ref, own_ref, received, out_ref, extra_ref=None):
     members, levels, rows, columns = own_ref.shape
+    partner_ref, received = received[0], received[1:]
     place = lax.axis_index("tile")
+    chip, upper, chips = place // 2, place % 2, tiles // 2
     rate = rate_ref[...]
-    zero = jnp.zeros((levels, columns), F32)
-    below, above = [zero] * members, [zero] * members
-    for k in range(1, tiles):
-        up = jnp.where(place >= k, jnp.exp(rate * (rows * (k - 1.0))), 0.0)
-        down = jnp.where(place < k, jnp.exp(rate * (rows * (tiles - k - 1.0))), 0.0)
+    below = [jnp.where(upper == 1, partner_ref[0, b], 0.0) for b in range(members)]
+    above = [jnp.where(upper == 0, partner_ref[1, b], 0.0) for b in range(members)]
+    for k in range(1, chips):
+        up = jnp.where(chip >= k, jnp.exp(rate * (rows * (2 * (k - 1) + upper)).astype(F32)), 0.0)
+        down = jnp.where(chip < k, jnp.exp(rate * (rows * (2 * (chips - k) - 1 - upper)).astype(F32)), 0.0)
         for b in range(members):
             below[b] = below[b] + up * received[k - 1][b]
             above[b] = above[b] + down * received[k - 1][b]
@@ -199,15 +226,13 @@
     return whole >> 7, whole & (LANES - 1)
 
 
-def chunks_of(shape):
-    tiles, per = shape[0], shape[-2]
-
+def chunks_of(count):
     def run(body):
         def step(c, _):
-            body(c // (per // 8), pl.ds(pl.multiple_of(c % (per // 8) * 8, 8), 8))
+            body(pl.ds(pl.multiple_of(c * 8, 8), 8))
             return 0
 
-        lax.fori_loop(0, tiles * (per // 8), step, 0, unroll=8)
+        lax.fori_loop(0, count // 8, step, 0, unroll=8)
 
     return run
 
@@ -227,9 +252,14 @@
     return rows
 
 
-def gather_kernel(tiles, rate_ref, own_ref, members_ref, *rest):
-    received, ray = rest[: tiles - 1], rest[tiles - 1]
-    out_ref, smooth_ref, table_ref = rest[tiles:]
+def gather_kernel(tiles, blocks, per, rate_ref, own_ref, members_ref, *rest):
+    received, rays = rest[: tiles // 2], rest[tiles // 2 : tiles // 2 + blocks]
+    out_ref, ray_ref, smooth_ref, table_ref = rest[tiles // 2 + blocks :]
+    for p in range(blocks):
+        for s in range(tiles):
+            to = (p * tiles + s) * per
+            for f in range(5):
+                ray_ref[f, to : to + per] = rays[p][s, f * per : (f + 1) * per]
     add_others(tiles, rate_ref, own_ref, received, smooth_ref)
     members, levels, rows, columns = own_ref.shape
     high_rows = levels * rows
@@ -252,11 +282,11 @@
     row_of = iota((256, LANES), 0).astype(F32).astype(BF16)
     lane_of = iota((LANES, LANES), 0)
 
-    @chunks_of(out_ref.shape)
-    def _(s, at):
-        high, low = indices(ray[s, 0, at, :])
+    @chunks_of(out_ref.shape[0])
+    def _(at):
+        high, low = indices(ray_ref[0, at, :])
         hot_row = hot_rows(high, row_of, high_rows)
-        first, second = ray[s, 1, at, :] * back, ray[s, 2, at, :] * back
+        first, second = ray_ref[1, at, :] * back, ray_ref[2, at, :] * back
         lines = []
         for pair in range(4):
             hot = jnp.concatenate([hot_row(2 * pair), hot_row(2 * pair + 1)], axis=1).astype(F8)
@@ -271,14 +301,20 @@
                 u = jnp.sum(jnp.where(here, part[:LANES], 0.0), axis=0, keepdims=True)
                 v = jnp.sum(jnp.where(here, part[LANES:], 0.0), axis=0, keepdims=True)
                 lines.append(u * first[r : r + 1] + v * second[r : r + 1])
-        out_ref[s, at, :] = jnp.concatenate(lines, axis=0)
-
-
-def scatter_kernel(tiles, blocks, rate_ref, high_ref, low_ref, members_ref, ray, *rest):
-    partial = rest[:blocks]
-    out_ref = rest[blocks]
-    outs = rest[blocks + 1 : blocks + tiles]
-    total_ref, mixed_ref = rest[blocks + tiles :]
+        out_ref[at, :] = jnp.concatenate(lines, axis=0)
+
+
+def scatter_kernel(tiles, blocks, rate_ref, high_ref, low_ref, members_ref, ray_ref, *rest):
+    partial, (out_ref, state_ref, total_ref, mixed_ref, value_ref) = rest[:blocks], rest[blocks:]
+    size = ray_ref.shape[1] // blocks
+    for p in range(blocks):
+        mine = slice(p * size, (p + 1) * size)
+        modelled = partial[0][mine]
+        for k in range(1, blocks):
+            modelled = modelled + partial[k][(p ^ k) * size : ((p ^ k) + 1) * size]
+        departure = ray_ref[4, mine] * (modelled - ray_ref[3, mine])
+        for f in range(2):
+            value_ref[f, mine] = ray_ref[1 + f, mine] * departure
     members, levels, rows, columns = out_ref.shape
     high_rows = levels * rows
     row_of = iota((256, LANES), 0).astype(F32).astype(BF16)
@@ -286,18 +322,14 @@
     none = jnp.zeros((), BF16)
     total_ref[...] = jnp.zeros_like(total_ref)
 
-    @chunks_of(partial[0].shape)
-    def _(s, at):
-        high, low = indices(ray[s, 0, at, :])
+    @chunks_of(ray_ref.shape[1])
+    def _(at):
+        high, low = indices(ray_ref[0, at, :])
         hot_row = hot_rows(high, row_of, high_rows)
         low = low.astype(F32)
-        modelled = partial[0][s, at, :]
-        for other in partial[1:]:
-            modelled = modelled + other[s, at, :]
-        departure = ray[s, 4, at, :] * (modelled - ray[s, 3, at, :])
         values = []
         for f in range(2):
-            value = ray[s, 1 + f, at, :] * departure
+            value = value_ref[f, at, :]
             part = value.astype(BF16).astype(F32)
             values.append((part, value - part))
         sides = [[], []]
@@ -324,22 +356,22 @@
             mixed_ref[b, l] = members_ref[b, 0, l].astype(F32) * u + members_ref[b, 1, l].astype(F32) * v
     filter_levels(mixed_ref, mixed_ref)
     filter_columns(mixed_ref, high_ref, low_ref, out_ref)
-    states(tiles, rate_ref, out_ref, outs)
+    states(tiles, rate_ref, out_ref, state_ref)
 
 
 def last_kernel(tiles, rate_ref, alpha_ref, own_ref, *rest):
     add_others(tiles, rate_ref, own_ref, rest[:-1], rest[-1], alpha_ref)
 
 
-def call(body, outs, scratch=(), cost=None):
+def call(body, outs, scratch=(), cost=None, specs=None, params=PARAMS):
     def run(*args):
         return pl.pallas_call(
             body,
             out_shape=outs,
-            in_specs=[VMEM] * len(args),
+            in_specs=specs or [VMEM] * len(args),
             out_specs=jax.tree.map(lambda _: VMEM, outs),
             scratch_shapes=list(scratch),
-            compiler_params=PARAMS,
+            compiler_params=params,
             cost_estimate=cost,
         )(*args)
 
@@ -350,51 +382,79 @@
     return jax.ShapeDtypeStruct(shape, dtype)
 
 
-def over_tiles(parts, tiles):
-    return [
-        lax.ppermute(part, "tile", [(i, (i + k) % tiles) for i in range(tiles)])
-        for k, part in enumerate(parts, 1)
-    ]
-
-
 def over_members(part, blocks):
     return [lax.ppermute(part, "mem", [(i, i ^ k) for i in range(blocks)]) for k in range(1, blocks)]
+
+
+def exchange(rate, own, rows, tiles):
+    chips = tiles // 2
+    partner = lax.ppermute(own, "tile", [(i, i ^ 1) for i in range(tiles)])
+    given = call(functools.partial(chip_kernel, tiles, rows), [shaped(*own.shape[1:])] * (chips - 1))(
+        rate, own, partner
+    )
+    return [
+        partner,
+        *(
+            lax.ppermute(
+                part, "tile", [(2 * c + h, 2 * ((c + k) % chips) + h) for c in range(chips) for h in range(2)]
+            )
+            for k, part in enumerate(given, 1)
+        ),
+    ]
 
 
 def per_device(alpha, members, scales, observed, precision, ray_weights, cell_index, owner):
     tiles, blocks = lax.axis_size("tile"), lax.axis_size("mem")
     count_rays, gates = observed.shape
     capacity = 3 * count_rays // tiles
-    per = -(-capacity * (gates // LANES) // 8) * 8
+    per = -(-capacity * (gates // LANES) // blocks)
     shape = alpha.shape
     count, levels, rows, columns = shape
-    ray = call(functools.partial(pack_rays_kernel, per), shaped(tiles, 5, per, LANES))(
-        owner, cell_index, ray_weights, observed, precision
-    )
-    ray = lax.all_to_all(ray, "tile", split_axis=0, concat_axis=0, tiled=True)
-    rate = jnp.broadcast_to((-1.0 / scales)[:, None], (levels, LANES))
-
-    state = shaped(count, levels, columns)
-    high, low, field, *given = call(
+    anywhere = pl.BlockSpec(memory_space=pltpu.HBM)
+    given = (
+        owner.reshape(1, count_rays),
+        scales.reshape(1, levels),
+        cell_index,
+        ray_weights,
+        observed,
+        precision,
+    )
+    sent, rate = call(
+        functools.partial(pack_rays_kernel, per),
+        [shaped(tiles, 5 * per, LANES), shaped(levels, LANES)],
+        [*(pltpu.VMEM(x.shape, x.dtype) for x in given), pltpu.SemaphoreType.DMA((6,))],
+        specs=[anywhere] * 6,
+        params=WIDE,
+    )(*given)
+    here = lax.all_to_all(sent, "tile", split_axis=0, concat_axis=0, tiled=True)
+    rays = [here, *over_members(here, blocks)]
+
+    state = shaped(2, count, levels, columns)
+    high, low, field, own = call(
         functools.partial(first_kernel, tiles),
-        [shaped(levels, columns, columns, dtype=BF16)] * 2 + [shaped(*shape)] + [state] * (tiles - 1),
+        [shaped(levels, columns, columns, dtype=BF16)] * 2 + [shaped(*shape), state],
         [pltpu.VMEM(shape, F32)],
     )(rate, alpha)
-    received = over_tiles(given, tiles)
+    received = exchange(rate, own, rows, tiles)
     own = call(functools.partial(within_kernel, tiles), shaped(*shape))(rate, field)
-    modelled = call(
-        functools.partial(gather_kernel, tiles),
-        shaped(tiles, per, LANES),
+    total = blocks * tiles * per
+    modelled, ray = call(
+        functools.partial(gather_kernel, tiles, blocks, per),
+        [shaped(total, LANES), shaped(5, total, LANES)],
         [pltpu.VMEM(shape, F32), pltpu.VMEM((2 * PIECES * LANES, levels * rows), F8)],
         COST,
-    )(rate, own, members, *received, ray)
-    field, *given = call(
+    )(rate, own, members, *received, *rays)
+    field, own = call(
         functools.partial(scatter_kernel, tiles, blocks),
-        [shaped(*shape)] + [state] * (tiles - 1),
-        [pltpu.VMEM((levels * rows, 2 * LANES), F32), pltpu.VMEM(shape, F32)],
+        [shaped(*shape), state],
+        [
+            pltpu.VMEM((levels * rows, 2 * LANES), F32),
+            pltpu.VMEM(shape, F32),
+            pltpu.VMEM((2, total, LANES), F32),
+        ],
         COST,
     )(rate, high, low, members, ray, modelled, *over_members(modelled, blocks))
-    received = over_tiles(given, tiles)
+    received = exchange(rate, own, rows, tiles)
     own = call(functools.partial(within_kernel, tiles), shaped(*shape))(rate, field)
     return call(functools.partial(last_kernel, tiles), shaped(*shape))(rate, alpha, own, *received)
 

time: 81.3 us -> 74 us (0.910)
  starting transfers between devices: 25.9 us -> 19.9 us
  local copies, waits for them, and re-layouts: 3.94 us -> 1.05 us
  waiting for transfers between devices: 14.8 us -> 16.4 us
    ppermute x14 -> x8, starting transfers between devices: 15.9 us -> 6.55 us  [the longest x6 6.03 us: exchange(): lax.ppermute(part, 'tile', [(2 * c + h, 2 * ((c + k) % chips) + h) for c...]
    ppermute x3 -> x6, starting transfers between devices: 3.55 us -> 7.04 us  [over_members(): lax.ppermute(part, 'mem', [(i, i ^ k) for i in range(blocks)])]
    unnamed x19 -> x8, local copies, waits for them, and re-layouts: 3.87 us -> 1.05 us
    all_to_all x1, waiting for transfers between devices: 0.01 us -> 1.94 us  [per_device(): here = lax.all_to_all(sent, 'tile', split_axis=0, concat_axis=0, tiled=True)]
    ppermute x3 -> x6, waiting for transfers between devices: 5.04 us -> 4.09 us  [over_members(): lax.ppermute(part, 'mem', [(i, i ^ k) for i in range(blocks)])]
    ppermute x14 -> x8, waiting for transfers between devices: 9.73 us -> 10.4 us  [the longest x6 9.14 us: exchange(): lax.ppermute(part, 'tile', [(2 * c + h, 2 * ((c + k) % chips) + h) for c...]
    pallas_call x7 -> x9, Pallas kernels: 36.1 us -> 36.1 us  [run(): pl.pallas_call(body, out_shape=outs, in_specs=specs or [VMEM] * len(args)...]
  transfers between devices with their start and end apart: 18 -> 15, of which waited for: 10 -> 9; matrix products, arithmetic and copies ran while one was open for 0% -> 0% of each run, Pallas kernels for 5% -> 6%
where the time goes in v3:
time: 74 us; the launch traced here: 73.6 us
  Pallas kernels  36.1 us (49%)
  starting transfers between devices  19.9 us (27%)
  waiting for transfers between devices  16.4 us (22%)
  local copies, waits for them, and re-layouts  1.05 us (1%)
    pallas_call x9, Pallas kernels, run(): pl.pallas_call(body, out_shape=outs, in_specs=specs or [VMEM] * len(args)...  36.1 us
    ppermute x6, waiting for transfers between devices, exchange(): lax.ppermute(part, 'tile', [(2 * c + h, 2 * ((c + k) % chips) + h) for c...  9.14 us
    ppermute x6, starting transfers between devices, over_members(): lax.ppermute(part, 'mem', [(i, i ^ k) for i in range(blocks)])  7.04 us
    all_to_all x1, starting transfers between devices, per_device(): here = lax.all_to_all(sent, 'tile', split_axis=0, concat_axis=0, tiled=True)  6.34 us
    ppermute x6, starting transfers between devices, exchange(): lax.ppermute(part, 'tile', [(2 * c + h, 2 * ((c + k) % chips) + h) for c...  6.03 us
    ppermute x6, waiting for transfers between devices, over_members(): lax.ppermute(part, 'mem', [(i, i ^ k) for i in range(blocks)])  4.09 us
    all_to_all x1, waiting for transfers between devices, per_device(): here = lax.all_to_all(sent, 'tile', split_axis=0, concat_axis=0, tiled=True)  1.94 us
  transfers between devices with their start and end apart: 15, of which 9 were waited for; matrix products, arithmetic and copies ran while one was open for 0% of the time, Pallas kernels for 6%

profile of v3, /device:TPU:0, one launch (start us, length us, event | category | flops | bytes accessed | tf_op | source)
XLA Modules:
  0.0 73.6 jit_solution(4393919935349130747)
XLA Ops:
  0.0 2.0 %shard_map.82 = (f32[8,30,128]{2,1,0:T(8,128)}, f32[32,128]{1,0:T(8,128)}) custom-call(s32[1,32]{1,0:T(1,128)} %bitcast.2, f32[1,32]{1,0:T(1,128)} %bitcast.3, s32[32,256]{1,0:T(8,128)} %refs_2_.1, f32[32,2,256]{2,1,0:T(2,128)} %refs_3_.1, f32[32,256]{1,0:T(8,128)} %refs_4_.1, f32[32,256]{1,0:T(8,128)} %refs_5_.1), custom_call_target="tpu_custom_call" | custom-call | tf_op jit(solution)/shard_map/pallas_call | solution.py:368
  2.1 0.0 copy-start.2
  2.1 6.3 %all-to-all-start = ((f32[8,30,128]{2,1,0:T(8,128)}), f32[8,30,128]{2,1,0:T(8,128)S(1)}, u32[]{:S(2)}, u32[]{:S(2)}) async-start(f32[8,30,128]{2,1,0:T(8,128)} %get-tuple-element.29), calls=%async_computation | async-start | bytes 262144 | tf_op jit(solution)/shard_map/all_to_all | solution.py:429
  8.4 0.0 copy-done.2
  8.4 0.0 copy-start
  8.4 1.0 %copy-done = f32[2,32,16,128]{3,2,1,0:T(8,128)S(1)} copy-done((f32[2,32,16,128]{3,2,1,0:T(8,128)S(1)}, f32[2,32,16,128]{3,2,1,0:T(8,128)}, u32[]{:S(2)}) %copy-start) | copy-done | bytes 524312
  9.5 3.3 %shard_map.83 = (bf16[32,128,128]{2,1,0:T(8,128)(2,1)S(1)}, bf16[32,128,128]{2,1,0:T(8,128)(2,1)S(1)}, f32[2,32,16,128]{3,2,1,0:T(8,128)S(1)}, f32[2,2,32,128]{3,2,1,0:T(8,128)S(1)}) custom-call(f32[32,128]{1,0:T(8,128)S(1)} %copy-done.2, f32[2,32,16,128]{3,2,1,0:T(8,128)S(1)} %copy-done), custom_call_target="tpu_custom_call" | custom-call | tf_op jit(solution)/shard_map/pallas_call | solution.py:368
  12.7 0.5 collective-permute-start
  13.2 1.9 %all-to-all-done.rest_4_ = f32[8,30,128]{2,1,0:T(8,128)S(1)} async-done(((f32[8,30,128]{2,1,0:T(8,128)}), f32[8,30,128]{2,1,0:T(8,128)S(1)}, u32[]{:S(2)}, u32[]{:S(2)}) %all-to-all-start) | async-done | bytes 122912 | tf_op jit(solution)/shard_map/all_to_all | solution.py:429
  15.2 2.4 %collective-permute-start.6 = (f32[8,30,128]{2,1,0:T(8,128)S(1)}, f32[8,30,128]{2,1,0:T(8,128)S(1)}, u32[]{:S(2)}, u32[]{:S(2)}) collective-permute-start(f32[8,30,128]{2,1,0:T(8,128)S(1)} %all-to-all-done.rest_4_), channel_id=1, source_target_pairs={{0,24},{8,16},{16,8},{24,0},{1,25},{9,17},{17,9},{25,1},{2,26},{10... | collective-permute-start | bytes 368648 | tf_op jit(solution)/shard_map/ppermute | solution.py:386
  17.6 0.5 collective-permute-start.5
  18.1 0.5 collective-permute-start.4
  18.7 0.0 collective-permute-done.partner_ref.rest_0_
  18.7 1.0 %collective-permute-start.1 = (f32[2,32,128]{2,1,0:T(8,128)S(1)}, f32[2,32,128]{2,1,0:T(8,128)S(1)}, u32[]{:S(2)}, u32[]{:S(2)}) collective-permute-start(f32[2,32,128]{2,1,0:T(8,128)S(1)} %get-tuple-element.26), channel_id=1, source_target_pairs={{0,2},{1,3},{2,4},{3,5},{4,6},{5,7},{6,0},{7,1},{8,10},{9,11},{10,... | collective-permute-start | bytes 98312 | tf_op jit(solution)/shard_map/ppermute | solution.py:398
  19.7 1.2 %collective-permute-start.2 = (f32[2,32,128]{2,1,0:T(8,128)S(1)}, f32[2,32,128]{2,1,0:T(8,128)S(1)}, u32[]{:S(2)}, u32[]{:S(2)}) collective-permute-start(f32[2,32,128]{2,1,0:T(8,128)S(1)} %get-tuple-element.27), channel_id=1, source_target_pairs={{0,4},{1,5},{2,6},{3,7},{4,0},{5,1},{6,2},{7,3},{8,12},{9,13},{10,... | collective-permute-start | bytes 98312 | tf_op jit(solution)/shard_map/ppermute | solution.py:398
  20.9 3.9 %collective-permute-done.1.rest_1_ = f32[2,32,128]{2,1,0:T(8,128)S(1)} collective-permute-done((f32[2,32,128]{2,1,0:T(8,128)S(1)}, f32[2,32,128]{2,1,0:T(8,128)S(1)}, u32[]{:S(2)}, u32[]{:S(2)}) %collective-permute-start.1) | collective-permute-done | bytes 32800 | tf_op jit(solution)/shard_map/ppermute | solution.py:398
  24.8 0.0 collective-permute-start.3
  24.8 0.0 copy-start.3
  24.8 0.6 shard_map.84.own_ref
  25.4 0.0 collective-permute-done.2.rest_2_
  25.4 3.3 %collective-permute-done.3.rest_3_ = f32[2,32,128]{2,1,0:T(8,128)S(1)} collective-permute-done((f32[2,32,128]{2,1,0:T(8,128)S(1)}, f32[2,32,128]{2,1,0:T(8,128)S(1)}, u32[]{:S(2)}, u32[]{:S(2)}) %collective-permute-start.3) | collective-permute-done | bytes 32800 | tf_op jit(solution)/shard_map/ppermute | solution.py:398
  28.7 0.0 collective-permute-done.6.rest_7_
  28.7 0.0 collective-permute-done.5.rest_6_
  28.7 0.0 collective-permute-done.4.rest_5_
  28.7 0.0 copy-done.3
  28.7 12.8 %shard_map.86 = (f32[192,128]{1,0:T(8,128)S(1)}, f32[5,192,128]{2,1,0:T(8,128)S(1)}) custom-call(f32[32,128]{1,0:T(8,128)S(1)} %copy-done.2, f32[2,32,16,128]{3,2,1,0:T(8,128)S(1)} %shard_map.84.own_ref, bf16[2,2,32,16,128]{4,3,2,1,0:T(8,128)(2,1)S(1)} %copy-done.3, f32[2,2,32,128]{3,2,1,0:T(8,128)S(1)} %collective-permute-done.partner_ref.rest_0_, ...), custom_call_target="tpu_custom_call" | custom-call | flops 20000000000 | bytes 4000000 | tf_op jit(solution)/shard_map/pallas_call | solution.py:368
  41.6 2.5 %collective-permute-start.9 = (f32[192,128]{1,0:T(8,128)S(1)}, f32[192,128]{1,0:T(8,128)S(1)}, u32[]{:S(2)}, u32[]{:S(2)}) collective-permute-start(f32[192,128]{1,0:T(8,128)S(1)} %get-tuple-element.31.rest_0_), channel_id=1, source_target_pairs={{0,24},{8,16},{16,8},{24,0},{1,25},{9,17},{17,9},{25,1},{2,26},{10... | collective-permute-start | bytes 294920 | tf_op jit(solution)/shard_map/ppermute | solution.py:386
  44.1 0.5 collective-permute-start.8
  44.6 0.5 collective-permute-start.7
  45.1 2.0 %collective-permute-done.9.rest_3_ = f32[192,128]{1,0:T(8,128)S(1)} collective-permute-done((f32[192,128]{1,0:T(8,128)S(1)}, f32[192,128]{1,0:T(8,128)S(1)}, u32[]{:S(2)}, u32[]{:S(2)}) %collective-permute-start.9) | collective-permute-done | bytes 98336 | tf_op jit(solution)/shard_map/ppermute | solution.py:386
  47.2 1.5 %collective-permute-done.8.rest_2_ = f32[192,128]{1,0:T(8,128)S(1)} collective-permute-done((f32[192,128]{1,0:T(8,128)S(1)}, f32[192,128]{1,0:T(8,128)S(1)}, u32[]{:S(2)}, u32[]{:S(2)}) %collective-permute-start.8) | collective-permute-done | bytes 98336 | tf_op jit(solution)/shard_map/ppermute | solution.py:386
  48.7 0.5 collective-permute-done.7.rest_1_
  49.2 15.7 %shard_map.87 = (f32[2,32,16,128]{3,2,1,0:T(8,128)S(1)}, f32[2,2,32,128]{3,2,1,0:T(8,128)S(1)}) custom-call(f32[32,128]{1,0:T(8,128)S(1)} %copy-done.2, bf16[32,128,128]{2,1,0:T(8,128)(2,1)S(1)} %get-tuple-element.22.high_ref, bf16[32,128,128]{2,1,0:T(8,128)(2,1)S(1)} %get-tuple-element.23.low_ref, bf16[2,2,32,16,128]{4,3,2,1,0:T(8,128)(2,1)S(1)} %copy-done.3, ...), custom_call_target="tpu_custom_call" | custom-call | flops 20000000000 | bytes 4000000 | tf_op jit(solution)/shard_map/pallas_call | solution.py:368
  64.9 0.0 collective-permute-start.10
  64.9 1.3 %collective-permute-done.10.partner_ref.rest_0_ = f32[2,2,32,128]{3,2,1,0:T(8,128)S(1)} collective-permute-done((f32[2,2,32,128]{3,2,1,0:T(8,128)S(1)}, f32[2,2,32,128]{3,2,1,0:T(8,128)S(1)}, u32[]{:S(2)}, u32[]{:S(2)}) %collective-permute-start.10) | collective-permute-done | bytes 65568 | tf_op jit(solution)/shard_map/ppermute | solution.py:391
  66.2 0.1 collective-permute-start.11
  66.3 2.3 %collective-permute-start.12 = (f32[2,32,128]{2,1,0:T(8,128)S(1)}, f32[2,32,128]{2,1,0:T(8,128)S(1)}, u32[]{:S(2)}, u32[]{:S(2)}) collective-permute-start(f32[2,32,128]{2,1,0:T(8,128)S(1)} %get-tuple-element.35), channel_id=1, source_target_pairs={{0,4},{1,5},{2,6},{3,7},{4,0},{5,1},{6,2},{7,3},{8,12},{9,13},{10,... | collective-permute-start | bytes 98312 | tf_op jit(solution)/shard_map/ppermute | solution.py:398
  68.7 1.5 %collective-permute-start.13 = (f32[2,32,128]{2,1,0:T(8,128)S(1)}, f32[2,32,128]{2,1,0:T(8,128)S(1)}, u32[]{:S(2)}, u32[]{:S(2)}) collective-permute-start(f32[2,32,128]{2,1,0:T(8,128)S(1)} %get-tuple-element.36), channel_id=1, source_target_pairs={{0,6},{1,7},{2,0},{3,1},{4,2},{5,3},{6,4},{7,5},{8,14},{9,15},{10,... | collective-permute-start | bytes 98312 | tf_op jit(solution)/shard_map/ppermute | solution.py:398
  70.1 0.0 copy-start.1
  70.1 0.6 shard_map.88.own_ref
  70.7 1.5 %collective-permute-done.11.rest_1_ = f32[2,32,128]{2,1,0:T(8,128)S(1)} collective-permute-done((f32[2,32,128]{2,1,0:T(8,128)S(1)}, f32[2,32,128]{2,1,0:T(8,128)S(1)}, u32[]{:S(2)}, u32[]{:S(2)}) %collective-permute-start.11) | collective-permute-done | bytes 32800 | tf_op jit(solution)/shard_map/ppermute | solution.py:398
  72.2 0.0 collective-permute-done.12.rest_2_
  72.2 0.3 collective-permute-done.13.rest_3_
  72.6 0.0 copy-done.1
  72.6 1.0 %shard_map.90 = f32[2,32,16,128]{3,2,1,0:T(8,128)} custom-call(f32[32,128]{1,0:T(8,128)S(1)} %copy-done.2, f32[2,32,16,128]{3,2,1,0:T(8,128)S(1)} %copy-done.1, f32[2,32,16,128]{3,2,1,0:T(8,128)S(1)} %shard_map.88.own_ref, f32[2,2,32,128]{3,2,1,0:T(8,128)S(1)} %collective-permute-done.10.partner_ref.rest_0_, ...), custom_call_target="tpu_custom_call" | custom-call | tf_op jit(solution)/shard_map/pallas_call | solution.py:368
  (2 shorter events, 0.0 us)
Async XLA Ops:
  2.1 6.3 %copy-start.2 = (f32[32,128]{1,0:T(8,128)S(1)}, f32[32,128]{1,0:T(8,128)}, u32[]{:S(2)}) copy-start(f32[32,128]{1,0:T(8,128)} %get-tuple-element.21.rate_ref) | copy-start | bytes 49156
  2.1 13.1 %all-to-all-start = ((f32[8,30,128]{2,1,0:T(8,128)}), f32[8,30,128]{2,1,0:T(8,128)S(1)}, u32[]{:S(2)}, u32[]{:S(2)}) async-start(f32[8,30,128]{2,1,0:T(8,128)} %get-tuple-element.29), calls=%async_computation | async-start | bytes 262144 | tf_op jit(solution)/shard_map/all_to_all | solution.py:429
  8.4 1.0 %copy-start = (f32[2,32,16,128]{3,2,1,0:T(8,128)S(1)}, f32[2,32,16,128]{3,2,1,0:T(8,128)}, u32[]{:S(2)}) copy-start(f32[2,32,16,128]{3,2,1,0:T(8,128)} %alpha_ref.3) | copy-start | bytes 1572868
  12.7 6.0 %collective-permute-start = (f32[2,2,32,128]{3,2,1,0:T(8,128)S(1)}, f32[2,2,32,128]{3,2,1,0:T(8,128)S(1)}, u32[]{:S(2)}, u32[]{:S(2)}) collective-permute-start(f32[2,2,32,128]{3,2,1,0:T(8,128)S(1)} %get-tuple-element.25.own_ref), channel_id=1, source_target_pairs={{0,1},{1,0},{2,3},{3,2},{4,5},{5,4},{6,7},{7,6},{8,9},{9,8},{10,11... | collective-permute-start | bytes 196616 | tf_op jit(solution)/shard_map/ppermute | solution.py:391
  15.2 13.5 %collective-permute-start.6 = (f32[8,30,128]{2,1,0:T(8,128)S(1)}, f32[8,30,128]{2,1,0:T(8,128)S(1)}, u32[]{:S(2)}, u32[]{:S(2)}) collective-permute-start(f32[8,30,128]{2,1,0:T(8,128)S(1)} %all-to-all-done.rest_4_), channel_id=1, source_target_pairs={{0,24},{8,16},{16,8},{24,0},{1,25},{9,17},{17,9},{25,1},{2,26},{10... | collective-permute-start | bytes 368648 | tf_op jit(solution)/shard_map/ppermute | solution.py:386
  17.6 11.1 %collective-permute-start.5 = (f32[8,30,128]{2,1,0:T(8,128)S(1)}, f32[8,30,128]{2,1,0:T(8,128)S(1)}, u32[]{:S(2)}, u32[]{:S(2)}) collective-permute-start(f32[8,30,128]{2,1,0:T(8,128)S(1)} %all-to-all-done.rest_4_), channel_id=1, source_target_pairs={{0,16},{8,24},{16,0},{24,8},{1,17},{9,25},{17,1},{25,9},{2,18},{10... | collective-permute-start | bytes 368648 | tf_op jit(solution)/shard_map/ppermute | solution.py:386
  18.1 10.6 %collective-permute-start.4 = (f32[8,30,128]{2,1,0:T(8,128)S(1)}, f32[8,30,128]{2,1,0:T(8,128)S(1)}, u32[]{:S(2)}, u32[]{:S(2)}) collective-permute-start(f32[8,30,128]{2,1,0:T(8,128)S(1)} %all-to-all-done.rest_4_), channel_id=1, source_target_pairs={{0,8},{8,0},{16,24},{24,16},{1,9},{9,1},{17,25},{25,17},{2,10},{10... | collective-permute-start | bytes 368648 | tf_op jit(solution)/shard_map/ppermute | solution.py:386
  18.7 6.1 %collective-permute-start.1 = (f32[2,32,128]{2,1,0:T(8,128)S(1)}, f32[2,32,128]{2,1,0:T(8,128)S(1)}, u32[]{:S(2)}, u32[]{:S(2)}) collective-permute-start(f32[2,32,128]{2,1,0:T(8,128)S(1)} %get-tuple-element.26), channel_id=1, source_target_pairs={{0,2},{1,3},{2,4},{3,5},{4,6},{5,7},{6,0},{7,1},{8,10},{9,11},{10,... | collective-permute-start | bytes 98312 | tf_op jit(solution)/shard_map/ppermute | solution.py:398
  19.7 5.7 %collective-permute-start.2 = (f32[2,32,128]{2,1,0:T(8,128)S(1)}, f32[2,32,128]{2,1,0:T(8,128)S(1)}, u32[]{:S(2)}, u32[]{:S(2)}) collective-permute-start(f32[2,32,128]{2,1,0:T(8,128)S(1)} %get-tuple-element.27), channel_id=1, source_target_pairs={{0,4},{1,5},{2,6},{3,7},{4,0},{5,1},{6,2},{7,3},{8,12},{9,13},{10,... | collective-permute-start | bytes 98312 | tf_op jit(solution)/shard_map/ppermute | solution.py:398
  24.8 3.9 %collective-permute-start.3 = (f32[2,32,128]{2,1,0:T(8,128)S(1)}, f32[2,32,128]{2,1,0:T(8,128)S(1)}, u32[]{:S(2)}, u32[]{:S(2)}) collective-permute-start(f32[2,32,128]{2,1,0:T(8,128)S(1)} %get-tuple-element.28), channel_id=1, source_target_pairs={{0,6},{1,7},{2,0},{3,1},{4,2},{5,3},{6,4},{7,5},{8,14},{9,15},{10,... | collective-permute-start | bytes 98312 | tf_op jit(solution)/shard_map/ppermute | solution.py:398
  24.8 3.9 %copy-start.3 = (bf16[2,2,32,16,128]{4,3,2,1,0:T(8,128)(2,1)S(1)}, bf16[2,2,32,16,128]{4,3,2,1,0:T(8,128)(2,1)}, u32[]{:S(2)}) copy-start(bf16[2,2,32,16,128]{4,3,2,1,0:T(8,128)(2,1)} %members_ref.3) | copy-start | bytes 1572868
  41.6 5.6 %collective-permute-start.9 = (f32[192,128]{1,0:T(8,128)S(1)}, f32[192,128]{1,0:T(8,128)S(1)}, u32[]{:S(2)}, u32[]{:S(2)}) collective-permute-start(f32[192,128]{1,0:T(8,128)S(1)} %get-tuple-element.31.rest_0_), channel_id=1, source_target_pairs={{0,24},{8,16},{16,8},{24,0},{1,25},{9,17},{17,9},{25,1},{2,26},{10... | collective-permute-start | bytes 294920 | tf_op jit(solution)/shard_map/ppermute | solution.py:386
  44.1 4.6 %collective-permute-start.8 = (f32[192,128]{1,0:T(8,128)S(1)}, f32[192,128]{1,0:T(8,128)S(1)}, u32[]{:S(2)}, u32[]{:S(2)}) collective-permute-start(f32[192,128]{1,0:T(8,128)S(1)} %get-tuple-element.31.rest_0_), channel_id=1, source_target_pairs={{0,16},{8,24},{16,0},{24,8},{1,17},{9,25},{17,1},{25,9},{2,18},{10... | collective-permute-start | bytes 294920 | tf_op jit(solution)/shard_map/ppermute | solution.py:386
  44.6 4.6 %collective-permute-start.7 = (f32[192,128]{1,0:T(8,128)S(1)}, f32[192,128]{1,0:T(8,128)S(1)}, u32[]{:S(2)}, u32[]{:S(2)}) collective-permute-start(f32[192,128]{1,0:T(8,128)S(1)} %get-tuple-element.31.rest_0_), channel_id=1, source_target_pairs={{0,8},{8,0},{16,24},{24,16},{1,9},{9,1},{17,25},{25,17},{2,10},{10... | collective-permute-start | bytes 294920 | tf_op jit(solution)/shard_map/ppermute | solution.py:386
  64.9 1.3 %collective-permute-start.10 = (f32[2,2,32,128]{3,2,1,0:T(8,128)S(1)}, f32[2,2,32,128]{3,2,1,0:T(8,128)S(1)}, u32[]{:S(2)}, u32[]{:S(2)}) collective-permute-start(f32[2,2,32,128]{3,2,1,0:T(8,128)S(1)} %get-tuple-element.33.own_ref), channel_id=1, source_target_pairs={{0,1},{1,0},{2,3},{3,2},{4,5},{5,4},{6,7},{7,6},{8,9},{9,8},{10,11... | collective-permute-start | bytes 196616 | tf_op jit(solution)/shard_map/ppermute | solution.py:391
  66.2 6.0 %collective-permute-start.11 = (f32[2,32,128]{2,1,0:T(8,128)S(1)}, f32[2,32,128]{2,1,0:T(8,128)S(1)}, u32[]{:S(2)}, u32[]{:S(2)}) collective-permute-start(f32[2,32,128]{2,1,0:T(8,128)S(1)} %get-tuple-element.34), channel_id=1, source_target_pairs={{0,2},{1,3},{2,4},{3,5},{4,6},{5,7},{6,0},{7,1},{8,10},{9,11},{10,... | collective-permute-start | bytes 98312 | tf_op jit(solution)/shard_map/ppermute | solution.py:398
  66.3 5.9 %collective-permute-start.12 = (f32[2,32,128]{2,1,0:T(8,128)S(1)}, f32[2,32,128]{2,1,0:T(8,128)S(1)}, u32[]{:S(2)}, u32[]{:S(2)}) collective-permute-start(f32[2,32,128]{2,1,0:T(8,128)S(1)} %get-tuple-element.35), channel_id=1, source_target_pairs={{0,4},{1,5},{2,6},{3,7},{4,0},{5,1},{6,2},{7,3},{8,12},{9,13},{10,... | collective-permute-start | bytes 98312 | tf_op jit(solution)/shard_map/ppermute | solution.py:398
  68.7 3.9 %collective-permute-start.13 = (f32[2,32,128]{2,1,0:T(8,128)S(1)}, f32[2,32,128]{2,1,0:T(8,128)S(1)}, u32[]{:S(2)}, u32[]{:S(2)}) collective-permute-start(f32[2,32,128]{2,1,0:T(8,128)S(1)} %get-tuple-element.36), channel_id=1, source_target_pairs={{0,6},{1,7},{2,0},{3,1},{4,2},{5,3},{6,4},{7,5},{8,14},{9,15},{10,... | collective-permute-start | bytes 98312 | tf_op jit(solution)/shard_map/ppermute | solution.py:398
  70.1 2.5 %copy-start.1 = (f32[2,32,16,128]{3,2,1,0:T(8,128)S(1)}, f32[2,32,16,128]{3,2,1,0:T(8,128)}, u32[]{:S(2)}) copy-start(f32[2,32,16,128]{3,2,1,0:T(8,128)} %alpha_ref.3) | copy-start | bytes 1572868

commit v4 on v3

--- a/solution.py
+++ b/solution.py
@@ -62,9 +62,8 @@
     rate_ref[...] = -1.0 / jnp.broadcast_to(scale, rate_ref.shape)
     rays, gates = held[0].shape
     tiles, halves = out_ref.shape[0], gates // LANES
-    part = lax.axis_index("mem")
     row = iota((tiles * per, rays), 0)
-    target, wanted = row // per, row % per + part * per
+    target, wanted = row // per, row % per
     named = owner_ref[...] == target
     earlier = (iota((rays, rays), 0) < iota((rays, rays), 1)).astype(F32)
     rank = dot(named.astype(F32), earlier).astype(I32)
@@ -252,14 +251,12 @@
     return rows
 
 
-def gather_kernel(tiles, blocks, per, rate_ref, own_ref, members_ref, *rest):
-    received, rays = rest[: tiles // 2], rest[tiles // 2 : tiles // 2 + blocks]
-    out_ref, ray_ref, smooth_ref, table_ref = rest[tiles // 2 + blocks :]
-    for p in range(blocks):
-        for s in range(tiles):
-            to = (p * tiles + s) * per
-            for f in range(5):
-                ray_ref[f, to : to + per] = rays[p][s, f * per : (f + 1) * per]
+def gather_kernel(tiles, per, rate_ref, own_ref, members_ref, *rest):
+    received, rays = rest[: tiles // 2], rest[tiles // 2]
+    out_ref, ray_ref, smooth_ref, table_ref = rest[tiles // 2 + 1 :]
+    for s in range(tiles):
+        for f in range(5):
+            ray_ref[f, s * per : (s + 1) * per] = rays[s, f * per : (f + 1) * per]
     add_others(tiles, rate_ref, own_ref, received, smooth_ref)
     members, levels, rows, columns = own_ref.shape
     high_rows = levels * rows
@@ -306,15 +303,12 @@
 
 def scatter_kernel(tiles, blocks, rate_ref, high_ref, low_ref, members_ref, ray_ref, *rest):
     partial, (out_ref, state_ref, total_ref, mixed_ref, value_ref) = rest[:blocks], rest[blocks:]
-    size = ray_ref.shape[1] // blocks
-    for p in range(blocks):
-        mine = slice(p * size, (p + 1) * size)
-        modelled = partial[0][mine]
-        for k in range(1, blocks):
-            modelled = modelled + partial[k][(p ^ k) * size : ((p ^ k) + 1) * size]
-        departure = ray_ref[4, mine] * (modelled - ray_ref[3, mine])
-        for f in range(2):
-            value_ref[f, mine] = ray_ref[1 + f, mine] * departure
+    modelled = partial[0][...]
+    for other in partial[1:]:
+        modelled = modelled + other[...]
+    departure = ray_ref[4] * (modelled - ray_ref[3])
+    for f in range(2):
+        value_ref[f] = ray_ref[1 + f] * departure
     members, levels, rows, columns = out_ref.shape
     high_rows = levels * rows
     row_of = iota((256, LANES), 0).astype(F32).astype(BF16)
@@ -407,7 +401,7 @@
     tiles, blocks = lax.axis_size("tile"), lax.axis_size("mem")
     count_rays, gates = observed.shape
     capacity = 3 * count_rays // tiles
-    per = -(-capacity * (gates // LANES) // blocks)
+    per = capacity * (gates // LANES)
     shape = alpha.shape
     count, levels, rows, columns = shape
     anywhere = pl.BlockSpec(memory_space=pltpu.HBM)
@@ -427,7 +421,6 @@
         params=WIDE,
     )(*given)
     here = lax.all_to_all(sent, "tile", split_axis=0, concat_axis=0, tiled=True)
-    rays = [here, *over_members(here, blocks)]
 
     state = shaped(2, count, levels, columns)
     high, low, field, own = call(
@@ -437,13 +430,13 @@
     )(rate, alpha)
     received = exchange(rate, own, rows, tiles)
     own = call(functools.partial(within_kernel, tiles), shaped(*shape))(rate, field)
-    total = blocks * tiles * per
+    total = tiles * per
     modelled, ray = call(
-        functools.partial(gather_kernel, tiles, blocks, per),
+        functools.partial(gather_kernel, tiles, per),
         [shaped(total, LANES), shaped(5, total, LANES)],
         [pltpu.VMEM(shape, F32), pltpu.VMEM((2 * PIECES * LANES, levels * rows), F8)],
         COST,
-    )(rate, own, members, *received, *rays)
+    )(rate, own, members, *received, here)
     field, own = call(
         functools.partial(scatter_kernel, tiles, blocks),
         [shaped(*shape), state],

time: 74 us -> 71.4 us (0.965)
  waiting for transfers between devices: 16.4 us -> 13.4 us
    ppermute x6, starting transfers between devices: 6.03 us -> 9.63 us  [exchange(): lax.ppermute(part, 'tile', [(2 * c + h, 2 * ((c + k) % chips) + h) for c...]
    ppermute x6 -> x3, starting transfers between devices: 7.04 us -> 3.55 us  [over_members(): lax.ppermute(part, 'mem', [(i, i ^ k) for i in range(blocks)])]
    ppermute x6, waiting for transfers between devices: 9.14 us -> 7.13 us  [exchange(): lax.ppermute(part, 'tile', [(2 * c + h, 2 * ((c + k) % chips) + h) for c...]
    all_to_all x1, waiting for transfers between devices: 1.94 us -> 0.01 us  [per_device(): here = lax.all_to_all(sent, 'tile', split_axis=0, concat_axis=0, tiled=True)]
    ppermute x2, waiting for transfers between devices: 1.27 us -> 2.17 us  [exchange(): partner = lax.ppermute(own, 'tile', [(i, i ^ 1) for i in range(tiles)])]
    ppermute x6 -> x3, waiting for transfers between devices: 4.09 us -> 4.08 us  [over_members(): lax.ppermute(part, 'mem', [(i, i ^ k) for i in range(blocks)])]
  transfers between devices with their start and end apart: 15 -> 12, of which waited for: 9 -> 9; matrix products, arithmetic and copies ran while one was open for 0% -> 0% of each run, Pallas kernels for 6% -> 6%
where the time goes in v4:
time: 71.4 us; the launch traced here: 71.1 us
  Pallas kernels  36.5 us (51%)
  starting transfers between devices  20.2 us (28%)
  waiting for transfers between devices  13.4 us (19%)
  local copies, waits for them, and re-layouts  1.03 us (1%)
    pallas_call x9, Pallas kernels, run(): pl.pallas_call(body, out_shape=outs, in_specs=specs or [VMEM] * len(args)...  36.5 us
    ppermute x6, starting transfers between devices, exchange(): lax.ppermute(part, 'tile', [(2 * c + h, 2 * ((c + k) % chips) + h) for c...  9.63 us
    ppermute x6, waiting for transfers between devices, exchange(): lax.ppermute(part, 'tile', [(2 * c + h, 2 * ((c + k) % chips) + h) for c...  7.13 us
    all_to_all x1, starting transfers between devices, per_device(): here = lax.all_to_all(sent, 'tile', split_axis=0, concat_axis=0, tiled=True)  6.47 us
    ppermute x3, waiting for transfers between devices, over_members(): lax.ppermute(part, 'mem', [(i, i ^ k) for i in range(blocks)])  4.08 us
    ppermute x3, starting transfers between devices, over_members(): lax.ppermute(part, 'mem', [(i, i ^ k) for i in range(blocks)])  3.55 us
    ppermute x2, waiting for transfers between devices, exchange(): partner = lax.ppermute(own, 'tile', [(i, i ^ 1) for i in range(tiles)])  2.17 us
  transfers between devices with their start and end apart: 12, of which 9 were waited for; matrix products, arithmetic and copies ran while one was open for 0% of the time, Pallas kernels for 6%

profile of v4, /device:TPU:0, one launch (start us, length us, event | category | flops | bytes accessed | tf_op | source)
XLA Modules:
  0.0 71.1 jit_solution(4339589433923843342)
XLA Ops:
  0.0 2.4 %shard_map.82 = (f32[8,120,128]{2,1,0:T(8,128)}, f32[32,128]{1,0:T(8,128)}) custom-call(s32[1,32]{1,0:T(1,128)} %bitcast.2, f32[1,32]{1,0:T(1,128)} %bitcast.3, s32[32,256]{1,0:T(8,128)} %refs_2_.1, f32[32,2,256]{2,1,0:T(2,128)} %refs_3_.1, f32[32,256]{1,0:T(8,128)} %refs_4_.1, f32[32,256]{1,0:T(8,128)} %refs_5_.1), custom_call_target="tpu_custom_call" | custom-call | tf_op jit(solution)/shard_map/pallas_call | solution.py:362
  2.5 0.0 copy-start
  2.5 0.0 copy-start.1
  2.5 6.5 %all-to-all-start = ((f32[8,120,128]{2,1,0:T(8,128)}), f32[8,120,128]{2,1,0:T(8,128)S(1)}, u32[]{:S(2)}, u32[]{:S(2)}) async-start(f32[8,120,128]{2,1,0:T(8,128)} %get-tuple-element.29), calls=%async_computation | async-start | bytes 983040 | tf_op jit(solution)/shard_map/all_to_all | solution.py:423
  8.9 0.0 copy-done
  8.9 0.0 copy-done.1
  9.0 3.3 %shard_map.83 = (bf16[32,128,128]{2,1,0:T(8,128)(2,1)S(1)}, bf16[32,128,128]{2,1,0:T(8,128)(2,1)S(1)}, f32[2,32,16,128]{3,2,1,0:T(8,128)S(1)}, f32[2,2,32,128]{3,2,1,0:T(8,128)S(1)}) custom-call(f32[32,128]{1,0:T(8,128)S(1)} %copy-done.1, f32[2,32,16,128]{3,2,1,0:T(8,128)S(1)} %copy-done), custom_call_target="tpu_custom_call" | custom-call | tf_op jit(solution)/shard_map/pallas_call | solution.py:362
  12.2 0.0 copy-start.2
  12.2 1.0 %copy-done.2 = bf16[32,128,128]{2,1,0:T(8,128)(2,1)} copy-done((bf16[32,128,128]{2,1,0:T(8,128)(2,1)}, bf16[32,128,128]{2,1,0:T(8,128)(2,1)S(1)}, u32[]{:S(2)}) %copy-start.2) | copy-done | bytes 1048600
  13.2 0.5 collective-permute-start
  13.7 0.9 %collective-permute-done.partner_ref.rest_0_ = f32[2,2,32,128]{3,2,1,0:T(8,128)S(1)} collective-permute-done((f32[2,2,32,128]{3,2,1,0:T(8,128)S(1)}, f32[2,2,32,128]{3,2,1,0:T(8,128)S(1)}, u32[]{:S(2)}, u32[]{:S(2)}) %collective-permute-start) | collective-permute-done | bytes 65568 | tf_op jit(solution)/shard_map/ppermute | solution.py:385
  14.7 1.9 %collective-permute-start.1 = (f32[2,32,128]{2,1,0:T(8,128)S(1)}, f32[2,32,128]{2,1,0:T(8,128)S(1)}, u32[]{:S(2)}, u32[]{:S(2)}) collective-permute-start(f32[2,32,128]{2,1,0:T(8,128)S(1)} %get-tuple-element.26), channel_id=1, source_target_pairs={{0,2},{1,3},{2,4},{3,5},{4,6},{5,7},{6,0},{7,1},{8,10},{9,11},{10,... | collective-permute-start | bytes 98312 | tf_op jit(solution)/shard_map/ppermute | solution.py:392
  16.6 2.4 %collective-permute-start.2 = (f32[2,32,128]{2,1,0:T(8,128)S(1)}, f32[2,32,128]{2,1,0:T(8,128)S(1)}, u32[]{:S(2)}, u32[]{:S(2)}) collective-permute-start(f32[2,32,128]{2,1,0:T(8,128)S(1)} %get-tuple-element.27), channel_id=1, source_target_pairs={{0,4},{1,5},{2,6},{3,7},{4,0},{5,1},{6,2},{7,3},{8,12},{9,13},{10,... | collective-permute-start | bytes 98312 | tf_op jit(solution)/shard_map/ppermute | solution.py:392
  19.0 1.5 %collective-permute-start.3 = (f32[2,32,128]{2,1,0:T(8,128)S(1)}, f32[2,32,128]{2,1,0:T(8,128)S(1)}, u32[]{:S(2)}, u32[]{:S(2)}) collective-permute-start(f32[2,32,128]{2,1,0:T(8,128)S(1)} %get-tuple-element.28), channel_id=1, source_target_pairs={{0,6},{1,7},{2,0},{3,1},{4,2},{5,3},{6,4},{7,5},{8,14},{9,15},{10,... | collective-permute-start | bytes 98312 | tf_op jit(solution)/shard_map/ppermute | solution.py:392
  20.4 0.0 copy-start.4
  20.4 0.6 shard_map.84.own_ref
  21.0 2.2 %collective-permute-done.1.rest_1_ = f32[2,32,128]{2,1,0:T(8,128)S(1)} collective-permute-done((f32[2,32,128]{2,1,0:T(8,128)S(1)}, f32[2,32,128]{2,1,0:T(8,128)S(1)}, u32[]{:S(2)}, u32[]{:S(2)}) %collective-permute-start.1) | collective-permute-done | bytes 32800 | tf_op jit(solution)/shard_map/ppermute | solution.py:392
  23.2 2.8 %collective-permute-done.2.rest_2_ = f32[2,32,128]{2,1,0:T(8,128)S(1)} collective-permute-done((f32[2,32,128]{2,1,0:T(8,128)S(1)}, f32[2,32,128]{2,1,0:T(8,128)S(1)}, u32[]{:S(2)}, u32[]{:S(2)}) %collective-permute-start.2) | collective-permute-done | bytes 32800 | tf_op jit(solution)/shard_map/ppermute | solution.py:392
  26.1 0.0 collective-permute-done.3.rest_3_
  26.1 0.0 all-to-all-done.rest_4_
  26.1 0.0 copy-done.4
  26.1 0.0 copy-start.3
  26.1 12.8 %shard_map.86 = (f32[192,128]{1,0:T(8,128)S(1)}, f32[5,192,128]{2,1,0:T(8,128)S(1)}) custom-call(f32[32,128]{1,0:T(8,128)S(1)} %copy-done.1, f32[2,32,16,128]{3,2,1,0:T(8,128)S(1)} %shard_map.84.own_ref, bf16[2,2,32,16,128]{4,3,2,1,0:T(8,128)(2,1)S(1)} %copy-done.4, f32[2,2,32,128]{3,2,1,0:T(8,128)S(1)} %collective-permute-done.partner_ref.rest_0_, ...), custom_call_target="tpu_custom_call" | custom-call | flops 20000000000 | bytes 4000000 | tf_op jit(solution)/shard_map/pallas_call | solution.py:362
  38.9 2.5 %collective-permute-start.6 = (f32[192,128]{1,0:T(8,128)S(1)}, f32[192,128]{1,0:T(8,128)S(1)}, u32[]{:S(2)}, u32[]{:S(2)}) collective-permute-start(f32[192,128]{1,0:T(8,128)S(1)} %get-tuple-element.31.rest_0_), channel_id=1, source_target_pairs={{0,24},{8,16},{16,8},{24,0},{1,25},{9,17},{17,9},{25,1},{2,26},{10... | collective-permute-start | bytes 294920 | tf_op jit(solution)/shard_map/ppermute | solution.py:380
  41.4 0.5 collective-permute-start.5
  41.9 0.5 collective-permute-start.4
  42.5 2.3 %collective-permute-done.6.rest_3_ = f32[192,128]{1,0:T(8,128)S(1)} collective-permute-done((f32[192,128]{1,0:T(8,128)S(1)}, f32[192,128]{1,0:T(8,128)S(1)}, u32[]{:S(2)}, u32[]{:S(2)}) %collective-permute-start.6) | collective-permute-done | bytes 98336 | tf_op jit(solution)/shard_map/ppermute | solution.py:380
  44.8 1.4 %collective-permute-done.5.rest_2_ = f32[192,128]{1,0:T(8,128)S(1)} collective-permute-done((f32[192,128]{1,0:T(8,128)S(1)}, f32[192,128]{1,0:T(8,128)S(1)}, u32[]{:S(2)}, u32[]{:S(2)}) %collective-permute-start.5) | collective-permute-done | bytes 98336 | tf_op jit(solution)/shard_map/ppermute | solution.py:380
  46.2 0.4 collective-permute-done.4.rest_1_
  46.5 0.0 copy-done.3
  46.5 15.7 %shard_map.87 = (f32[2,32,16,128]{3,2,1,0:T(8,128)S(1)}, f32[2,2,32,128]{3,2,1,0:T(8,128)S(1)}) custom-call(f32[32,128]{1,0:T(8,128)S(1)} %copy-done.1, bf16[32,128,128]{2,1,0:T(8,128)(2,1)S(1)} %get-tuple-element.22.high_ref, bf16[32,128,128]{2,1,0:T(8,128)(2,1)S(1)} %copy-done.3, bf16[2,2,32,16,128]{4,3,2,1,0:T(8,128)(2,1)S(1)} %copy-done.4, ...), custom_call_target="tpu_custom_call" | custom-call | flops 20000000000 | bytes 4000000 | tf_op jit(solution)/shard_map/pallas_call | solution.py:362
  62.3 0.0 collective-permute-start.7
  62.3 1.3 %collective-permute-done.7.partner_ref.rest_0_ = f32[2,2,32,128]{3,2,1,0:T(8,128)S(1)} collective-permute-done((f32[2,2,32,128]{3,2,1,0:T(8,128)S(1)}, f32[2,2,32,128]{3,2,1,0:T(8,128)S(1)}, u32[]{:S(2)}, u32[]{:S(2)}) %collective-permute-start.7) | collective-permute-done | bytes 65568 | tf_op jit(solution)/shard_map/ppermute | solution.py:385
  63.6 1.0 %collective-permute-start.8 = (f32[2,32,128]{2,1,0:T(8,128)S(1)}, f32[2,32,128]{2,1,0:T(8,128)S(1)}, u32[]{:S(2)}, u32[]{:S(2)}) collective-permute-start(f32[2,32,128]{2,1,0:T(8,128)S(1)} %get-tuple-element.34), channel_id=1, source_target_pairs={{0,2},{1,3},{2,4},{3,5},{4,6},{5,7},{6,0},{7,1},{8,10},{9,11},{10,... | collective-permute-start | bytes 98312 | tf_op jit(solution)/shard_map/ppermute | solution.py:392
  64.5 1.5 %collective-permute-start.9 = (f32[2,32,128]{2,1,0:T(8,128)S(1)}, f32[2,32,128]{2,1,0:T(8,128)S(1)}, u32[]{:S(2)}, u32[]{:S(2)}) collective-permute-start(f32[2,32,128]{2,1,0:T(8,128)S(1)} %get-tuple-element.35), channel_id=1, source_target_pairs={{0,4},{1,5},{2,6},{3,7},{4,0},{5,1},{6,2},{7,3},{8,12},{9,13},{10,... | collective-permute-start | bytes 98312 | tf_op jit(solution)/shard_map/ppermute | solution.py:392
  66.0 1.4 %collective-permute-start.10 = (f32[2,32,128]{2,1,0:T(8,128)S(1)}, f32[2,32,128]{2,1,0:T(8,128)S(1)}, u32[]{:S(2)}, u32[]{:S(2)}) collective-permute-start(f32[2,32,128]{2,1,0:T(8,128)S(1)} %get-tuple-element.36), channel_id=1, source_target_pairs={{0,6},{1,7},{2,0},{3,1},{4,2},{5,3},{6,4},{7,5},{8,14},{9,15},{10,... | collective-permute-start | bytes 98312 | tf_op jit(solution)/shard_map/ppermute | solution.py:392
  67.4 0.6 shard_map.88.own_ref
  68.0 1.6 %collective-permute-done.8.rest_1_ = f32[2,32,128]{2,1,0:T(8,128)S(1)} collective-permute-done((f32[2,32,128]{2,1,0:T(8,128)S(1)}, f32[2,32,128]{2,1,0:T(8,128)S(1)}, u32[]{:S(2)}, u32[]{:S(2)}) %collective-permute-start.8) | collective-permute-done | bytes 32800 | tf_op jit(solution)/shard_map/ppermute | solution.py:392
  69.6 0.5 collective-permute-done.9.rest_2_
  70.1 0.0 collective-permute-done.10.rest_3_
  70.1 1.0 %shard_map.90 = f32[2,32,16,128]{3,2,1,0:T(8,128)} custom-call(f32[32,128]{1,0:T(8,128)S(1)} %copy-done.1, f32[2,32,16,128]{3,2,1,0:T(8,128)S(1)} %copy-done, f32[2,32,16,128]{3,2,1,0:T(8,128)S(1)} %shard_map.88.own_ref, f32[2,2,32,128]{3,2,1,0:T(8,128)S(1)} %collective-permute-done.7.partner_ref.rest_0_, f32[2,32,128]{2,1,0:T(8,128)S(1)} %collective-permute-done.8.rest_1_, ...), custom_call_target="tpu_custom_call" | custom-call | tf_op jit(solution)/shard_map/pallas_call | solution.py:362
  (2 shorter events, 0.0 us)
Async XLA Ops:
  2.5 6.5 %copy-start = (f32[2,32,16,128]{3,2,1,0:T(8,128)S(1)}, f32[2,32,16,128]{3,2,1,0:T(8,128)}, u32[]{:S(2)}) copy-start(f32[2,32,16,128]{3,2,1,0:T(8,128)} %alpha_ref.3) | copy-start | bytes 1572868
  2.5 6.5 %copy-start.1 = (f32[32,128]{1,0:T(8,128)S(1)}, f32[32,128]{1,0:T(8,128)}, u32[]{:S(2)}) copy-start(f32[32,128]{1,0:T(8,128)} %get-tuple-element.21.rate_ref) | copy-start | bytes 49156
  2.5 23.6 %all-to-all-start = ((f32[8,120,128]{2,1,0:T(8,128)}), f32[8,120,128]{2,1,0:T(8,128)S(1)}, u32[]{:S(2)}, u32[]{:S(2)}) async-start(f32[8,120,128]{2,1,0:T(8,128)} %get-tuple-element.29), calls=%async_computation | async-start | bytes 983040 | tf_op jit(solution)/shard_map/all_to_all | solution.py:423
  12.2 1.0 %copy-start.2 = (bf16[32,128,128]{2,1,0:T(8,128)(2,1)}, bf16[32,128,128]{2,1,0:T(8,128)(2,1)S(1)}, u32[]{:S(2)}) copy-start(bf16[32,128,128]{2,1,0:T(8,128)(2,1)S(1)} %get-tuple-element.23.low_ref) | copy-start | bytes 3145732
  13.2 1.4 %collective-permute-start = (f32[2,2,32,128]{3,2,1,0:T(8,128)S(1)}, f32[2,2,32,128]{3,2,1,0:T(8,128)S(1)}, u32[]{:S(2)}, u32[]{:S(2)}) collective-permute-start(f32[2,2,32,128]{3,2,1,0:T(8,128)S(1)} %get-tuple-element.25.own_ref), channel_id=1, source_target_pairs={{0,1},{1,0},{2,3},{3,2},{4,5},{5,4},{6,7},{7,6},{8,9},{9,8},{10,11... | collective-permute-start | bytes 196616 | tf_op jit(solution)/shard_map/ppermute | solution.py:385
  14.7 8.5 %collective-permute-start.1 = (f32[2,32,128]{2,1,0:T(8,128)S(1)}, f32[2,32,128]{2,1,0:T(8,128)S(1)}, u32[]{:S(2)}, u32[]{:S(2)}) collective-permute-start(f32[2,32,128]{2,1,0:T(8,128)S(1)} %get-tuple-element.26), channel_id=1, source_target_pairs={{0,2},{1,3},{2,4},{3,5},{4,6},{5,7},{6,0},{7,1},{8,10},{9,11},{10,... | collective-permute-start | bytes 98312 | tf_op jit(solution)/shard_map/ppermute | solution.py:392
  16.6 9.5 %collective-permute-start.2 = (f32[2,32,128]{2,1,0:T(8,128)S(1)}, f32[2,32,128]{2,1,0:T(8,128)S(1)}, u32[]{:S(2)}, u32[]{:S(2)}) collective-permute-start(f32[2,32,128]{2,1,0:T(8,128)S(1)} %get-tuple-element.27), channel_id=1, source_target_pairs={{0,4},{1,5},{2,6},{3,7},{4,0},{5,1},{6,2},{7,3},{8,12},{9,13},{10,... | collective-permute-start | bytes 98312 | tf_op jit(solution)/shard_map/ppermute | solution.py:392
  19.0 7.1 %collective-permute-start.3 = (f32[2,32,128]{2,1,0:T(8,128)S(1)}, f32[2,32,128]{2,1,0:T(8,128)S(1)}, u32[]{:S(2)}, u32[]{:S(2)}) collective-permute-start(f32[2,32,128]{2,1,0:T(8,128)S(1)} %get-tuple-element.28), channel_id=1, source_target_pairs={{0,6},{1,7},{2,0},{3,1},{4,2},{5,3},{6,4},{7,5},{8,14},{9,15},{10,... | collective-permute-start | bytes 98312 | tf_op jit(solution)/shard_map/ppermute | solution.py:392
  20.4 5.6 %copy-start.4 = (bf16[2,2,32,16,128]{4,3,2,1,0:T(8,128)(2,1)S(1)}, bf16[2,2,32,16,128]{4,3,2,1,0:T(8,128)(2,1)}, u32[]{:S(2)}) copy-start(bf16[2,2,32,16,128]{4,3,2,1,0:T(8,128)(2,1)} %members_ref.3) | copy-start | bytes 1572868
  26.1 20.5 %copy-start.3 = (bf16[32,128,128]{2,1,0:T(8,128)(2,1)S(1)}, bf16[32,128,128]{2,1,0:T(8,128)(2,1)}, u32[]{:S(2)}) copy-start(bf16[32,128,128]{2,1,0:T(8,128)(2,1)} %copy-done.2) | copy-start | bytes 3145732
  38.9 5.9 %collective-permute-start.6 = (f32[192,128]{1,0:T(8,128)S(1)}, f32[192,128]{1,0:T(8,128)S(1)}, u32[]{:S(2)}, u32[]{:S(2)}) collective-permute-start(f32[192,128]{1,0:T(8,128)S(1)} %get-tuple-element.31.rest_0_), channel_id=1, source_target_pairs={{0,24},{8,16},{16,8},{24,0},{1,25},{9,17},{17,9},{25,1},{2,26},{10... | collective-permute-start | bytes 294920 | tf_op jit(solution)/shard_map/ppermute | solution.py:380
  41.4 4.8 %collective-permute-start.5 = (f32[192,128]{1,0:T(8,128)S(1)}, f32[192,128]{1,0:T(8,128)S(1)}, u32[]{:S(2)}, u32[]{:S(2)}) collective-permute-start(f32[192,128]{1,0:T(8,128)S(1)} %get-tuple-element.31.rest_0_), channel_id=1, source_target_pairs={{0,16},{8,24},{16,0},{24,8},{1,17},{9,25},{17,1},{25,9},{2,18},{10... | collective-permute-start | bytes 294920 | tf_op jit(solution)/shard_map/ppermute | solution.py:380
  41.9 4.6 %collective-permute-start.4 = (f32[192,128]{1,0:T(8,128)S(1)}, f32[192,128]{1,0:T(8,128)S(1)}, u32[]{:S(2)}, u32[]{:S(2)}) collective-permute-start(f32[192,128]{1,0:T(8,128)S(1)} %get-tuple-element.31.rest_0_), channel_id=1, source_target_pairs={{0,8},{8,0},{16,24},{24,16},{1,9},{9,1},{17,25},{25,17},{2,10},{10... | collective-permute-start | bytes 294920 | tf_op jit(solution)/shard_map/ppermute | solution.py:380
  62.3 1.3 %collective-permute-start.7 = (f32[2,2,32,128]{3,2,1,0:T(8,128)S(1)}, f32[2,2,32,128]{3,2,1,0:T(8,128)S(1)}, u32[]{:S(2)}, u32[]{:S(2)}) collective-permute-start(f32[2,2,32,128]{3,2,1,0:T(8,128)S(1)} %get-tuple-element.33.own_ref), channel_id=1, source_target_pairs={{0,1},{1,0},{2,3},{3,2},{4,5},{5,4},{6,7},{7,6},{8,9},{9,8},{10,11... | collective-permute-start | bytes 196616 | tf_op jit(solution)/shard_map/ppermute | solution.py:385
  63.6 6.0 %collective-permute-start.8 = (f32[2,32,128]{2,1,0:T(8,128)S(1)}, f32[2,32,128]{2,1,0:T(8,128)S(1)}, u32[]{:S(2)}, u32[]{:S(2)}) collective-permute-start(f32[2,32,128]{2,1,0:T(8,128)S(1)} %get-tuple-element.34), channel_id=1, source_target_pairs={{0,2},{1,3},{2,4},{3,5},{4,6},{5,7},{6,0},{7,1},{8,10},{9,11},{10,... | collective-permute-start | bytes 98312 | tf_op jit(solution)/shard_map/ppermute | solution.py:392
  64.5 5.6 %collective-permute-start.9 = (f32[2,32,128]{2,1,0:T(8,128)S(1)}, f32[2,32,128]{2,1,0:T(8,128)S(1)}, u32[]{:S(2)}, u32[]{:S(2)}) collective-permute-start(f32[2,32,128]{2,1,0:T(8,128)S(1)} %get-tuple-element.35), channel_id=1, source_target_pairs={{0,4},{1,5},{2,6},{3,7},{4,0},{5,1},{6,2},{7,3},{8,12},{9,13},{10,... | collective-permute-start | bytes 98312 | tf_op jit(solution)/shard_map/ppermute | solution.py:392
  66.0 4.1 %collective-permute-start.10 = (f32[2,32,128]{2,1,0:T(8,128)S(1)}, f32[2,32,128]{2,1,0:T(8,128)S(1)}, u32[]{:S(2)}, u32[]{:S(2)}) collective-permute-start(f32[2,32,128]{2,1,0:T(8,128)S(1)} %get-tuple-element.36), channel_id=1, source_target_pairs={{0,6},{1,7},{2,0},{3,1},{4,2},{5,3},{6,4},{7,5},{8,14},{9,15},{10,... | collective-permute-start | bytes 98312 | tf_op jit(solution)/shard_map/ppermute | solution.py:392

commit v5 on v4

--- a/solution.py
+++ b/solution.py
@@ -231,7 +231,7 @@
             body(pl.ds(pl.multiple_of(c * 8, 8), 8))
             return 0
 
-        lax.fori_loop(0, count // 8, step, 0, unroll=8)
+        lax.fori_loop(0, count // 8, step, 0, unroll=math.gcd(count // 8, 24))
 
     return run
 
@@ -307,8 +307,11 @@
     for other in partial[1:]:
         modelled = modelled + other[...]
     departure = ray_ref[4] * (modelled - ray_ref[3])
+    given = [ray_ref[1 + f] * departure for f in range(2)]
+    largest = jnp.maximum(jnp.max(jnp.maximum(jnp.abs(given[0]), jnp.abs(given[1]))), 1e-30)
+    scale, back = 256.0 / largest, largest * (1.0 / 256.0)
     for f in range(2):
-        value_ref[f] = ray_ref[1 + f] * departure
+        value_ref[f] = given[f] * scale
     members, levels, rows, columns = out_ref.shape
     high_rows = levels * rows
     row_of = iota((256, LANES), 0).astype(F32).astype(BF16)
@@ -321,31 +324,34 @@
         high, low = indices(ray_ref[0, at, :])
         hot_row = hot_rows(high, row_of, high_rows)
         low = low.astype(F32)
-        values = []
-        for f in range(2):
-            value = value_ref[f, at, :]
-            part = value.astype(BF16).astype(F32)
-            values.append((part, value - part))
-        sides = [[], []]
+        pieces = []
+        rest_of = [value_ref[f, at, :] for f in range(2)]
+        for _ in range(PIECES):
+            for f in range(2):
+                piece = rest_of[f].astype(F8).astype(F32)
+                rest_of[f] = (rest_of[f] - piece) * 16.0
+                pieces.append(piece)
+        sides = []
         for r in range(8):
             here = lane_of == low[r : r + 1].astype(BF16)
-            for piece in range(2):
-                sides[piece].append(
-                    jnp.concatenate(
-                        [jnp.where(here, values[f][piece][r : r + 1].astype(BF16), none) for f in range(2)], axis=0
-                    )
-                )
-        left = [hot_row(r) for r in range(8)]
+            sides.append(
+                jnp.concatenate(
+                    [jnp.where(here, piece[r : r + 1].astype(BF16), none) for piece in pieces], axis=0
+                ).astype(F8)
+            )
         total_ref[...] += lax.dot_general(
-            jnp.concatenate(left + left, axis=1),
-            jnp.concatenate(sides[0] + sides[1], axis=1),
+            jnp.concatenate([hot_row(r).astype(F8) for r in range(8)], axis=1),
+            jnp.concatenate(sides, axis=1),
             (((1,), (1,)), ((), ())),
             preferred_element_type=F32,
         )
 
     for l in range(levels):
-        u = total_ref[l * rows : (l + 1) * rows, :LANES]
-        v = total_ref[l * rows : (l + 1) * rows, LANES:]
+        total = total_ref[l * rows : (l + 1) * rows]
+        both = total[:, : 2 * LANES]
+        for k in range(1, PIECES):
+            both = both + total[:, 2 * k * LANES : 2 * (k + 1) * LANES] * 16.0**-k
+        u, v = both[:, :LANES] * back, both[:, LANES:] * back
         for b in range(members):
             mixed_ref[b, l] = members_ref[b, 0, l].astype(F32) * u + members_ref[b, 1, l].astype(F32) * v
     filter_levels(mixed_ref, mixed_ref)
@@ -441,7 +447,7 @@
         functools.partial(scatter_kernel, tiles, blocks),
         [shaped(*shape), state],
         [
-            pltpu.VMEM((levels * rows, 2 * LANES), F32),
+            pltpu.VMEM((levels * rows, 2 * PIECES * LANES), F32),
             pltpu.VMEM(shape, F32),
             pltpu.VMEM((2, total, LANES), F32),
         ],

time: 71.4 us -> 67.6 us (0.947)
  Pallas kernels: 36.5 us -> 32.7 us
    pallas_call x9, Pallas kernels: 36.5 us -> 32.7 us  [run(): pl.pallas_call(body, out_shape=outs, in_specs=specs or [VMEM] * len(args)...]
  transfers between devices with their start and end apart: 12 -> 12, of which waited for: 9 -> 9; matrix products, arithmetic and copies ran while one was open for 0% -> 0% of each run, Pallas kernels for 6% -> 7%
where the time goes in v5:
time: 67.6 us; the launch traced here: 67.3 us
  Pallas kernels  32.7 us (48%)
  starting transfers between devices  20.1 us (30%)
  waiting for transfers between devices  13.4 us (20%)
  local copies, waits for them, and re-layouts  1.03 us (2%)
    pallas_call x9, Pallas kernels, run(): pl.pallas_call(body, out_shape=outs, in_specs=specs or [VMEM] * len(args)...  32.7 us
    ppermute x6, starting transfers between devices, exchange(): lax.ppermute(part, 'tile', [(2 * c + h, 2 * ((c + k) % chips) + h) for c...  9.63 us
    ppermute x6, waiting for transfers between devices, exchange(): lax.ppermute(part, 'tile', [(2 * c + h, 2 * ((c + k) % chips) + h) for c...  7.13 us
    all_to_all x1, starting transfers between devices, per_device(): here = lax.all_to_all(sent, 'tile', split_axis=0, concat_axis=0, tiled=True)  6.47 us
    ppermute x3, waiting for transfers between devices, over_members(): lax.ppermute(part, 'mem', [(i, i ^ k) for i in range(blocks)])  4.08 us
    ppermute x3, starting transfers between devices, over_members(): lax.ppermute(part, 'mem', [(i, i ^ k) for i in range(blocks)])  3.55 us
    ppermute x2, waiting for transfers between devices, exchange(): partner = lax.ppermute(own, 'tile', [(i, i ^ 1) for i in range(tiles)])  2.17 us
  transfers between devices with their start and end apart: 12, of which 9 were waited for; matrix products, arithmetic and copies ran while one was open for 0% of the time, Pallas kernels for 7%

profile of v5, /device:TPU:0, one launch (start us, length us, event | category | flops | bytes accessed | tf_op | source)
XLA Modules:
  0.0 67.3 jit_solution(1655595499108753520)
XLA Ops:
  0.0 2.4 %shard_map.82 = (f32[8,120,128]{2,1,0:T(8,128)}, f32[32,128]{1,0:T(8,128)}) custom-call(s32[1,32]{1,0:T(1,128)} %bitcast.2, f32[1,32]{1,0:T(1,128)} %bitcast.3, s32[32,256]{1,0:T(8,128)} %refs_2_.1, f32[32,2,256]{2,1,0:T(2,128)} %refs_3_.1, f32[32,256]{1,0:T(8,128)} %refs_4_.1, f32[32,256]{1,0:T(8,128)} %refs_5_.1), custom_call_target="tpu_custom_call" | custom-call | tf_op jit(solution)/shard_map/pallas_call | solution.py:368
  2.5 0.0 copy-start
  2.5 0.0 copy-start.1
  2.5 6.5 %all-to-all-start = ((f32[8,120,128]{2,1,0:T(8,128)}), f32[8,120,128]{2,1,0:T(8,128)S(1)}, u32[]{:S(2)}, u32[]{:S(2)}) async-start(f32[8,120,128]{2,1,0:T(8,128)} %get-tuple-element.29), calls=%async_computation | async-start | bytes 983040 | tf_op jit(solution)/shard_map/all_to_all | solution.py:429
  8.9 0.0 copy-done
  8.9 0.0 copy-done.1
  9.0 3.3 %shard_map.83 = (bf16[32,128,128]{2,1,0:T(8,128)(2,1)S(1)}, bf16[32,128,128]{2,1,0:T(8,128)(2,1)S(1)}, f32[2,32,16,128]{3,2,1,0:T(8,128)S(1)}, f32[2,2,32,128]{3,2,1,0:T(8,128)S(1)}) custom-call(f32[32,128]{1,0:T(8,128)S(1)} %copy-done.1, f32[2,32,16,128]{3,2,1,0:T(8,128)S(1)} %copy-done), custom_call_target="tpu_custom_call" | custom-call | tf_op jit(solution)/shard_map/pallas_call | solution.py:368
  12.2 0.0 copy-start.2
  12.2 1.0 %copy-done.2 = bf16[32,128,128]{2,1,0:T(8,128)(2,1)} copy-done((bf16[32,128,128]{2,1,0:T(8,128)(2,1)}, bf16[32,128,128]{2,1,0:T(8,128)(2,1)S(1)}, u32[]{:S(2)}) %copy-start.2) | copy-done | bytes 1048600
  13.2 0.5 collective-permute-start
  13.7 0.9 %collective-permute-done.partner_ref.rest_0_ = f32[2,2,32,128]{3,2,1,0:T(8,128)S(1)} collective-permute-done((f32[2,2,32,128]{3,2,1,0:T(8,128)S(1)}, f32[2,2,32,128]{3,2,1,0:T(8,128)S(1)}, u32[]{:S(2)}, u32[]{:S(2)}) %collective-permute-start) | collective-permute-done | bytes 65568 | tf_op jit(solution)/shard_map/ppermute | solution.py:391
  14.7 1.9 %collective-permute-start.1 = (f32[2,32,128]{2,1,0:T(8,128)S(1)}, f32[2,32,128]{2,1,0:T(8,128)S(1)}, u32[]{:S(2)}, u32[]{:S(2)}) collective-permute-start(f32[2,32,128]{2,1,0:T(8,128)S(1)} %get-tuple-element.26), channel_id=1, source_target_pairs={{0,2},{1,3},{2,4},{3,5},{4,6},{5,7},{6,0},{7,1},{8,10},{9,11},{10,... | collective-permute-start | bytes 98312 | tf_op jit(solution)/shard_map/ppermute | solution.py:398
  16.6 2.4 %collective-permute-start.2 = (f32[2,32,128]{2,1,0:T(8,128)S(1)}, f32[2,32,128]{2,1,0:T(8,128)S(1)}, u32[]{:S(2)}, u32[]{:S(2)}) collective-permute-start(f32[2,32,128]{2,1,0:T(8,128)S(1)} %get-tuple-element.27), channel_id=1, source_target_pairs={{0,4},{1,5},{2,6},{3,7},{4,0},{5,1},{6,2},{7,3},{8,12},{9,13},{10,... | collective-permute-start | bytes 98312 | tf_op jit(solution)/shard_map/ppermute | solution.py:398
  19.0 1.5 %collective-permute-start.3 = (f32[2,32,128]{2,1,0:T(8,128)S(1)}, f32[2,32,128]{2,1,0:T(8,128)S(1)}, u32[]{:S(2)}, u32[]{:S(2)}) collective-permute-start(f32[2,32,128]{2,1,0:T(8,128)S(1)} %get-tuple-element.28), channel_id=1, source_target_pairs={{0,6},{1,7},{2,0},{3,1},{4,2},{5,3},{6,4},{7,5},{8,14},{9,15},{10,... | collective-permute-start | bytes 98312 | tf_op jit(solution)/shard_map/ppermute | solution.py:398
  20.4 0.0 copy-start.4
  20.4 0.6 shard_map.84.own_ref
  21.0 2.2 %collective-permute-done.1.rest_1_ = f32[2,32,128]{2,1,0:T(8,128)S(1)} collective-permute-done((f32[2,32,128]{2,1,0:T(8,128)S(1)}, f32[2,32,128]{2,1,0:T(8,128)S(1)}, u32[]{:S(2)}, u32[]{:S(2)}) %collective-permute-start.1) | collective-permute-done | bytes 32800 | tf_op jit(solution)/shard_map/ppermute | solution.py:398
  23.2 2.8 %collective-permute-done.2.rest_2_ = f32[2,32,128]{2,1,0:T(8,128)S(1)} collective-permute-done((f32[2,32,128]{2,1,0:T(8,128)S(1)}, f32[2,32,128]{2,1,0:T(8,128)S(1)}, u32[]{:S(2)}, u32[]{:S(2)}) %collective-permute-start.2) | collective-permute-done | bytes 32800 | tf_op jit(solution)/shard_map/ppermute | solution.py:398
  26.1 0.0 collective-permute-done.3.rest_3_
  26.1 0.0 all-to-all-done.rest_4_
  26.1 0.0 copy-done.4
  26.1 0.0 copy-start.3
  26.1 12.4 %shard_map.86 = (f32[192,128]{1,0:T(8,128)S(1)}, f32[5,192,128]{2,1,0:T(8,128)S(1)}) custom-call(f32[32,128]{1,0:T(8,128)S(1)} %copy-done.1, f32[2,32,16,128]{3,2,1,0:T(8,128)S(1)} %shard_map.84.own_ref, bf16[2,2,32,16,128]{4,3,2,1,0:T(8,128)(2,1)S(1)} %copy-done.4, f32[2,2,32,128]{3,2,1,0:T(8,128)S(1)} %collective-permute-done.partner_ref.rest_0_, ...), custom_call_target="tpu_custom_call" | custom-call | flops 20000000000 | bytes 4000000 | tf_op jit(solution)/shard_map/pallas_call | solution.py:368
  38.5 2.5 %collective-permute-start.6 = (f32[192,128]{1,0:T(8,128)S(1)}, f32[192,128]{1,0:T(8,128)S(1)}, u32[]{:S(2)}, u32[]{:S(2)}) collective-permute-start(f32[192,128]{1,0:T(8,128)S(1)} %get-tuple-element.31.rest_0_), channel_id=1, source_target_pairs={{0,24},{8,16},{16,8},{24,0},{1,25},{9,17},{17,9},{25,1},{2,26},{10... | collective-permute-start | bytes 294920 | tf_op jit(solution)/shard_map/ppermute | solution.py:386
  41.0 0.5 collective-permute-start.5
  41.5 0.5 collective-permute-start.4
  42.1 2.3 %collective-permute-done.6.rest_3_ = f32[192,128]{1,0:T(8,128)S(1)} collective-permute-done((f32[192,128]{1,0:T(8,128)S(1)}, f32[192,128]{1,0:T(8,128)S(1)}, u32[]{:S(2)}, u32[]{:S(2)}) %collective-permute-start.6) | collective-permute-done | bytes 98336 | tf_op jit(solution)/shard_map/ppermute | solution.py:386
  44.4 1.4 %collective-permute-done.5.rest_2_ = f32[192,128]{1,0:T(8,128)S(1)} collective-permute-done((f32[192,128]{1,0:T(8,128)S(1)}, f32[192,128]{1,0:T(8,128)S(1)}, u32[]{:S(2)}, u32[]{:S(2)}) %collective-permute-start.5) | collective-permute-done | bytes 98336 | tf_op jit(solution)/shard_map/ppermute | solution.py:386
  45.8 0.4 collective-permute-done.4.rest_1_
  46.2 0.0 copy-done.3
  46.2 12.3 %shard_map.87 = (f32[2,32,16,128]{3,2,1,0:T(8,128)S(1)}, f32[2,2,32,128]{3,2,1,0:T(8,128)S(1)}) custom-call(f32[32,128]{1,0:T(8,128)S(1)} %copy-done.1, bf16[32,128,128]{2,1,0:T(8,128)(2,1)S(1)} %get-tuple-element.22.high_ref, bf16[32,128,128]{2,1,0:T(8,128)(2,1)S(1)} %copy-done.3, bf16[2,2,32,16,128]{4,3,2,1,0:T(8,128)(2,1)S(1)} %copy-done.4, ...), custom_call_target="tpu_custom_call" | custom-call | flops 20000000000 | bytes 4000000 | tf_op jit(solution)/shard_map/pallas_call | solution.py:368
  58.5 0.0 collective-permute-start.7
  58.5 1.3 %collective-permute-done.7.partner_ref.rest_0_ = f32[2,2,32,128]{3,2,1,0:T(8,128)S(1)} collective-permute-done((f32[2,2,32,128]{3,2,1,0:T(8,128)S(1)}, f32[2,2,32,128]{3,2,1,0:T(8,128)S(1)}, u32[]{:S(2)}, u32[]{:S(2)}) %collective-permute-start.7) | collective-permute-done | bytes 65568 | tf_op jit(solution)/shard_map/ppermute | solution.py:391
  59.8 1.0 %collective-permute-start.8 = (f32[2,32,128]{2,1,0:T(8,128)S(1)}, f32[2,32,128]{2,1,0:T(8,128)S(1)}, u32[]{:S(2)}, u32[]{:S(2)}) collective-permute-start(f32[2,32,128]{2,1,0:T(8,128)S(1)} %get-tuple-element.34), channel_id=1, source_target_pairs={{0,2},{1,3},{2,4},{3,5},{4,6},{5,7},{6,0},{7,1},{8,10},{9,11},{10,... | collective-permute-start | bytes 98312 | tf_op jit(solution)/shard_map/ppermute | solution.py:398
  60.7 1.5 %collective-permute-start.9 = (f32[2,32,128]{2,1,0:T(8,128)S(1)}, f32[2,32,128]{2,1,0:T(8,128)S(1)}, u32[]{:S(2)}, u32[]{:S(2)}) collective-permute-start(f32[2,32,128]{2,1,0:T(8,128)S(1)} %get-tuple-element.35), channel_id=1, source_target_pairs={{0,4},{1,5},{2,6},{3,7},{4,0},{5,1},{6,2},{7,3},{8,12},{9,13},{10,... | collective-permute-start | bytes 98312 | tf_op jit(solution)/shard_map/ppermute | solution.py:398
  62.2 1.4 %collective-permute-start.10 = (f32[2,32,128]{2,1,0:T(8,128)S(1)}, f32[2,32,128]{2,1,0:T(8,128)S(1)}, u32[]{:S(2)}, u32[]{:S(2)}) collective-permute-start(f32[2,32,128]{2,1,0:T(8,128)S(1)} %get-tuple-element.36), channel_id=1, source_target_pairs={{0,6},{1,7},{2,0},{3,1},{4,2},{5,3},{6,4},{7,5},{8,14},{9,15},{10,... | collective-permute-start | bytes 98312 | tf_op jit(solution)/shard_map/ppermute | solution.py:398
  63.6 0.6 shard_map.88.own_ref
  64.2 1.6 %collective-permute-done.8.rest_1_ = f32[2,32,128]{2,1,0:T(8,128)S(1)} collective-permute-done((f32[2,32,128]{2,1,0:T(8,128)S(1)}, f32[2,32,128]{2,1,0:T(8,128)S(1)}, u32[]{:S(2)}, u32[]{:S(2)}) %collective-permute-start.8) | collective-permute-done | bytes 32800 | tf_op jit(solution)/shard_map/ppermute | solution.py:398
  65.8 0.5 collective-permute-done.9.rest_2_
  66.3 0.0 collective-permute-done.10.rest_3_
  66.3 1.0 %shard_map.90 = f32[2,32,16,128]{3,2,1,0:T(8,128)} custom-call(f32[32,128]{1,0:T(8,128)S(1)} %copy-done.1, f32[2,32,16,128]{3,2,1,0:T(8,128)S(1)} %copy-done, f32[2,32,16,128]{3,2,1,0:T(8,128)S(1)} %shard_map.88.own_ref, f32[2,2,32,128]{3,2,1,0:T(8,128)S(1)} %collective-permute-done.7.partner_ref.rest_0_, f32[2,32,128]{2,1,0:T(8,128)S(1)} %collective-permute-done.8.rest_1_, ...), custom_call_target="tpu_custom_call" | custom-call | tf_op jit(solution)/shard_map/pallas_call | solution.py:368
  (2 shorter events, 0.0 us)
Async XLA Ops:
  2.5 6.5 %copy-start = (f32[2,32,16,128]{3,2,1,0:T(8,128)S(1)}, f32[2,32,16,128]{3,2,1,0:T(8,128)}, u32[]{:S(2)}) copy-start(f32[2,32,16,128]{3,2,1,0:T(8,128)} %alpha_ref.3) | copy-start | bytes 1572868
  2.5 6.5 %copy-start.1 = (f32[32,128]{1,0:T(8,128)S(1)}, f32[32,128]{1,0:T(8,128)}, u32[]{:S(2)}) copy-start(f32[32,128]{1,0:T(8,128)} %get-tuple-element.21.rate_ref) | copy-start | bytes 49156
  2.5 23.6 %all-to-all-start = ((f32[8,120,128]{2,1,0:T(8,128)}), f32[8,120,128]{2,1,0:T(8,128)S(1)}, u32[]{:S(2)}, u32[]{:S(2)}) async-start(f32[8,120,128]{2,1,0:T(8,128)} %get-tuple-element.29), calls=%async_computation | async-start | bytes 983040 | tf_op jit(solution)/shard_map/all_to_all | solution.py:429
  12.2 1.0 %copy-start.2 = (bf16[32,128,128]{2,1,0:T(8,128)(2,1)}, bf16[32,128,128]{2,1,0:T(8,128)(2,1)S(1)}, u32[]{:S(2)}) copy-start(bf16[32,128,128]{2,1,0:T(8,128)(2,1)S(1)} %get-tuple-element.23.low_ref) | copy-start | bytes 3145732
  13.2 1.4 %collective-permute-start = (f32[2,2,32,128]{3,2,1,0:T(8,128)S(1)}, f32[2,2,32,128]{3,2,1,0:T(8,128)S(1)}, u32[]{:S(2)}, u32[]{:S(2)}) collective-permute-start(f32[2,2,32,128]{3,2,1,0:T(8,128)S(1)} %get-tuple-element.25.own_ref), channel_id=1, source_target_pairs={{0,1},{1,0},{2,3},{3,2},{4,5},{5,4},{6,7},{7,6},{8,9},{9,8},{10,11... | collective-permute-start | bytes 196616 | tf_op jit(solution)/shard_map/ppermute | solution.py:391
  14.7 8.5 %collective-permute-start.1 = (f32[2,32,128]{2,1,0:T(8,128)S(1)}, f32[2,32,128]{2,1,0:T(8,128)S(1)}, u32[]{:S(2)}, u32[]{:S(2)}) collective-permute-start(f32[2,32,128]{2,1,0:T(8,128)S(1)} %get-tuple-element.26), channel_id=1, source_target_pairs={{0,2},{1,3},{2,4},{3,5},{4,6},{5,7},{6,0},{7,1},{8,10},{9,11},{10,... | collective-permute-start | bytes 98312 | tf_op jit(solution)/shard_map/ppermute | solution.py:398
  16.6 9.5 %collective-permute-start.2 = (f32[2,32,128]{2,1,0:T(8,128)S(1)}, f32[2,32,128]{2,1,0:T(8,128)S(1)}, u32[]{:S(2)}, u32[]{:S(2)}) collective-permute-start(f32[2,32,128]{2,1,0:T(8,128)S(1)} %get-tuple-element.27), channel_id=1, source_target_pairs={{0,4},{1,5},{2,6},{3,7},{4,0},{5,1},{6,2},{7,3},{8,12},{9,13},{10,... | collective-permute-start | bytes 98312 | tf_op jit(solution)/shard_map/ppermute | solution.py:398
  19.0 7.1 %collective-permute-start.3 = (f32[2,32,128]{2,1,0:T(8,128)S(1)}, f32[2,32,128]{2,1,0:T(8,128)S(1)}, u32[]{:S(2)}, u32[]{:S(2)}) collective-permute-start(f32[2,32,128]{2,1,0:T(8,128)S(1)} %get-tuple-element.28), channel_id=1, source_target_pairs={{0,6},{1,7},{2,0},{3,1},{4,2},{5,3},{6,4},{7,5},{8,14},{9,15},{10,... | collective-permute-start | bytes 98312 | tf_op jit(solution)/shard_map/ppermute | solution.py:398
  20.4 5.6 %copy-start.4 = (bf16[2,2,32,16,128]{4,3,2,1,0:T(8,128)(2,1)S(1)}, bf16[2,2,32,16,128]{4,3,2,1,0:T(8,128)(2,1)}, u32[]{:S(2)}) copy-start(bf16[2,2,32,16,128]{4,3,2,1,0:T(8,128)(2,1)} %members_ref.3) | copy-start | bytes 1572868
  26.1 20.1 %copy-start.3 = (bf16[32,128,128]{2,1,0:T(8,128)(2,1)S(1)}, bf16[32,128,128]{2,1,0:T(8,128)(2,1)}, u32[]{:S(2)}) copy-start(bf16[32,128,128]{2,1,0:T(8,128)(2,1)} %copy-done.2) | copy-start | bytes 3145732
  38.5 5.9 %collective-permute-start.6 = (f32[192,128]{1,0:T(8,128)S(1)}, f32[192,128]{1,0:T(8,128)S(1)}, u32[]{:S(2)}, u32[]{:S(2)}) collective-permute-start(f32[192,128]{1,0:T(8,128)S(1)} %get-tuple-element.31.rest_0_), channel_id=1, source_target_pairs={{0,24},{8,16},{16,8},{24,0},{1,25},{9,17},{17,9},{25,1},{2,26},{10... | collective-permute-start | bytes 294920 | tf_op jit(solution)/shard_map/ppermute | solution.py:386
  41.0 4.8 %collective-permute-start.5 = (f32[192,128]{1,0:T(8,128)S(1)}, f32[192,128]{1,0:T(8,128)S(1)}, u32[]{:S(2)}, u32[]{:S(2)}) collective-permute-start(f32[192,128]{1,0:T(8,128)S(1)} %get-tuple-element.31.rest_0_), channel_id=1, source_target_pairs={{0,16},{8,24},{16,0},{24,8},{1,17},{9,25},{17,1},{25,9},{2,18},{10... | collective-permute-start | bytes 294920 | tf_op jit(solution)/shard_map/ppermute | solution.py:386
  41.5 4.6 %collective-permute-start.4 = (f32[192,128]{1,0:T(8,128)S(1)}, f32[192,128]{1,0:T(8,128)S(1)}, u32[]{:S(2)}, u32[]{:S(2)}) collective-permute-start(f32[192,128]{1,0:T(8,128)S(1)} %get-tuple-element.31.rest_0_), channel_id=1, source_target_pairs={{0,8},{8,0},{16,24},{24,16},{1,9},{9,1},{17,25},{25,17},{2,10},{10... | collective-permute-start | bytes 294920 | tf_op jit(solution)/shard_map/ppermute | solution.py:386
  58.5 1.3 %collective-permute-start.7 = (f32[2,2,32,128]{3,2,1,0:T(8,128)S(1)}, f32[2,2,32,128]{3,2,1,0:T(8,128)S(1)}, u32[]{:S(2)}, u32[]{:S(2)}) collective-permute-start(f32[2,2,32,128]{3,2,1,0:T(8,128)S(1)} %get-tuple-element.33.own_ref), channel_id=1, source_target_pairs={{0,1},{1,0},{2,3},{3,2},{4,5},{5,4},{6,7},{7,6},{8,9},{9,8},{10,11... | collective-permute-start | bytes 196616 | tf_op jit(solution)/shard_map/ppermute | solution.py:391
  59.8 6.0 %collective-permute-start.8 = (f32[2,32,128]{2,1,0:T(8,128)S(1)}, f32[2,32,128]{2,1,0:T(8,128)S(1)}, u32[]{:S(2)}, u32[]{:S(2)}) collective-permute-start(f32[2,32,128]{2,1,0:T(8,128)S(1)} %get-tuple-element.34), channel_id=1, source_target_pairs={{0,2},{1,3},{2,4},{3,5},{4,6},{5,7},{6,0},{7,1},{8,10},{9,11},{10,... | collective-permute-start | bytes 98312 | tf_op jit(solution)/shard_map/ppermute | solution.py:398
  60.7 5.6 %collective-permute-start.9 = (f32[2,32,128]{2,1,0:T(8,128)S(1)}, f32[2,32,128]{2,1,0:T(8,128)S(1)}, u32[]{:S(2)}, u32[]{:S(2)}) collective-permute-start(f32[2,32,128]{2,1,0:T(8,128)S(1)} %get-tuple-element.35), channel_id=1, source_target_pairs={{0,4},{1,5},{2,6},{3,7},{4,0},{5,1},{6,2},{7,3},{8,12},{9,13},{10,... | collective-permute-start | bytes 98312 | tf_op jit(solution)/shard_map/ppermute | solution.py:398
  62.2 4.1 %collective-permute-start.10 = (f32[2,32,128]{2,1,0:T(8,128)S(1)}, f32[2,32,128]{2,1,0:T(8,128)S(1)}, u32[]{:S(2)}, u32[]{:S(2)}) collective-permute-start(f32[2,32,128]{2,1,0:T(8,128)S(1)} %get-tuple-element.36), channel_id=1, source_target_pairs={{0,6},{1,7},{2,0},{3,1},{4,2},{5,3},{6,4},{7,5},{8,14},{9,15},{10,... | collective-permute-start | bytes 98312 | tf_op jit(solution)/shard_map/ppermute | solution.py:398

commit v6 on v5

--- a/solution.py
+++ b/solution.py
@@ -53,7 +53,7 @@
     copies = [pltpu.make_async_copy(given[k], held[k], sems.at[k]) for k in range(6)]
     for copy in copies:
         copy.start()
-    for copy in copies:
+    for copy in copies[:2]:
         copy.wait()
     owner_ref, scales_ref, held = held[0], held[1], held[2:]
     levels = rate_ref.shape[0]
@@ -68,8 +68,10 @@
     earlier = (iota((rays, rays), 0) < iota((rays, rays), 1)).astype(F32)
     rank = dot(named.astype(F32), earlier).astype(I32)
     picks = jnp.concatenate(
-        [(named & (rank * halves + half == wanted)).astype(F32) for half in range(halves)], axis=1
-    )
+        [(named & (rank * halves + half == wanted)).astype(F32).astype(BF16) for half in range(halves)], axis=1
+    )
+    for copy in copies[2:]:
+        copy.wait()
     cell_ref, weights_ref, observed_ref, precision_ref = held
     fields = (
         cell_ref[...].astype(F32),
@@ -85,7 +87,9 @@
         ],
         axis=1,
     )
-    got = jnp.dot(picks, stacked, precision=lax.Precision.HIGHEST, preferred_element_type=F32)
+    high = stacked.astype(BF16)
+    middle, low = split(stacked - high.astype(F32))
+    got = dot(picks, high) + (dot(picks, middle) + dot(picks, low))
     for t in range(tiles):
         for f in range(len(fields)):
             out_ref[t, f * per : (f + 1) * per] = got[t * per : (t + 1) * per, f * LANES : (f + 1) * LANES]
@@ -114,7 +118,7 @@
         out_ref[:, l] = total.reshape(members, rows, columns)
         return 0
 
-    lax.fori_loop(0, levels, level, 0, unroll=4)
+    lax.fori_loop(0, levels, level, 0, unroll=8)
 
 
 def columns_matrix(rate_ref, high_ref, low_ref):
@@ -129,7 +133,7 @@
         high_ref[l], low_ref[l] = split(matrix)
         return 0
 
-    lax.fori_loop(0, levels, level, 0, unroll=2)
+    lax.fori_loop(0, levels, level, 0, unroll=8)
 
 
 def states(tiles, rate_ref, field_ref, out_ref):

time: 67.6 us -> 66.7 us (0.987)
  Pallas kernels: 32.7 us -> 31.2 us
    pallas_call x9, Pallas kernels: 32.7 us -> 31.2 us  [run(): pl.pallas_call(body, out_shape=outs, in_specs=specs or [VMEM] * len(args)...]
  transfers between devices with their start and end apart: 12 -> 12, of which waited for: 9 -> 9; matrix products, arithmetic and copies ran while one was open for 0% -> 0% of each run, Pallas kernels for 7% -> 6%
where the time goes in v6:
time: 66.7 us; the launch traced here: 66.5 us
  Pallas kernels  31.2 us (47%)
  starting transfers between devices  20.2 us (30%)
  waiting for transfers between devices  14 us (21%)
  local copies, waits for them, and re-layouts  1.03 us (2%)
    pallas_call x9, Pallas kernels, run(): pl.pallas_call(body, out_shape=outs, in_specs=specs or [VMEM] * len(args)...  31.2 us
    ppermute x6, starting transfers between devices, exchange(): lax.ppermute(part, 'tile', [(2 * c + h, 2 * ((c + k) % chips) + h) for c...  9.63 us
    ppermute x6, waiting for transfers between devices, exchange(): lax.ppermute(part, 'tile', [(2 * c + h, 2 * ((c + k) % chips) + h) for c...  7.77 us
    all_to_all x1, starting transfers between devices, per_device(): here = lax.all_to_all(sent, 'tile', split_axis=0, concat_axis=0, tiled=True)  6.47 us
    ppermute x3, waiting for transfers between devices, over_members(): lax.ppermute(part, 'mem', [(i, i ^ k) for i in range(blocks)])  4.08 us
    ppermute x3, starting transfers between devices, over_members(): lax.ppermute(part, 'mem', [(i, i ^ k) for i in range(blocks)])  3.55 us
    ppermute x2, waiting for transfers between devices, exchange(): partner = lax.ppermute(own, 'tile', [(i, i ^ 1) for i in range(tiles)])  2.17 us
  transfers between devices with their start and end apart: 12, of which 9 were waited for; matrix products, arithmetic and copies ran while one was open for 0% of the time, Pallas kernels for 6%

profile of v6, /device:TPU:0, one launch (start us, length us, event | category | flops | bytes accessed | tf_op | source)
XLA Modules:
  0.0 66.5 jit_solution(3741111943815773233)
XLA Ops:
  0.0 2.1 %shard_map.82 = (f32[8,120,128]{2,1,0:T(8,128)}, f32[32,128]{1,0:T(8,128)}) custom-call(s32[1,32]{1,0:T(1,128)} %bitcast.2, f32[1,32]{1,0:T(1,128)} %bitcast.3, s32[32,256]{1,0:T(8,128)} %refs_2_.1, f32[32,2,256]{2,1,0:T(2,128)} %refs_3_.1, f32[32,256]{1,0:T(8,128)} %refs_4_.1, f32[32,256]{1,0:T(8,128)} %refs_5_.1), custom_call_target="tpu_custom_call" | custom-call | tf_op jit(solution)/shard_map/pallas_call | solution.py:372
  2.1 0.0 copy-start
  2.1 0.0 copy-start.1
  2.1 6.5 %all-to-all-start = ((f32[8,120,128]{2,1,0:T(8,128)}), f32[8,120,128]{2,1,0:T(8,128)S(1)}, u32[]{:S(2)}, u32[]{:S(2)}) async-start(f32[8,120,128]{2,1,0:T(8,128)} %get-tuple-element.29), calls=%async_computation | async-start | bytes 983040 | tf_op jit(solution)/shard_map/all_to_all | solution.py:433
  8.6 0.0 copy-done
  8.6 0.0 copy-done.1
  8.6 2.6 %shard_map.83 = (bf16[32,128,128]{2,1,0:T(8,128)(2,1)S(1)}, bf16[32,128,128]{2,1,0:T(8,128)(2,1)S(1)}, f32[2,32,16,128]{3,2,1,0:T(8,128)S(1)}, f32[2,2,32,128]{3,2,1,0:T(8,128)S(1)}) custom-call(f32[32,128]{1,0:T(8,128)S(1)} %copy-done.1, f32[2,32,16,128]{3,2,1,0:T(8,128)S(1)} %copy-done), custom_call_target="tpu_custom_call" | custom-call | tf_op jit(solution)/shard_map/pallas_call | solution.py:372
  11.3 0.0 copy-start.2
  11.3 1.0 %copy-done.2 = bf16[32,128,128]{2,1,0:T(8,128)(2,1)} copy-done((bf16[32,128,128]{2,1,0:T(8,128)(2,1)}, bf16[32,128,128]{2,1,0:T(8,128)(2,1)S(1)}, u32[]{:S(2)}) %copy-start.2) | copy-done | bytes 1048600
  12.3 0.5 collective-permute-start
  12.8 0.9 %collective-permute-done.partner_ref.rest_0_ = f32[2,2,32,128]{3,2,1,0:T(8,128)S(1)} collective-permute-done((f32[2,2,32,128]{3,2,1,0:T(8,128)S(1)}, f32[2,2,32,128]{3,2,1,0:T(8,128)S(1)}, u32[]{:S(2)}, u32[]{:S(2)}) %collective-permute-start) | collective-permute-done | bytes 65568 | tf_op jit(solution)/shard_map/ppermute | solution.py:395
  13.7 1.9 %collective-permute-start.1 = (f32[2,32,128]{2,1,0:T(8,128)S(1)}, f32[2,32,128]{2,1,0:T(8,128)S(1)}, u32[]{:S(2)}, u32[]{:S(2)}) collective-permute-start(f32[2,32,128]{2,1,0:T(8,128)S(1)} %get-tuple-element.26), channel_id=1, source_target_pairs={{0,2},{1,3},{2,4},{3,5},{4,6},{5,7},{6,0},{7,1},{8,10},{9,11},{10,... | collective-permute-start | bytes 98312 | tf_op jit(solution)/shard_map/ppermute | solution.py:402
  15.6 2.4 %collective-permute-start.2 = (f32[2,32,128]{2,1,0:T(8,128)S(1)}, f32[2,32,128]{2,1,0:T(8,128)S(1)}, u32[]{:S(2)}, u32[]{:S(2)}) collective-permute-start(f32[2,32,128]{2,1,0:T(8,128)S(1)} %get-tuple-element.27), channel_id=1, source_target_pairs={{0,4},{1,5},{2,6},{3,7},{4,0},{5,1},{6,2},{7,3},{8,12},{9,13},{10,... | collective-permute-start | bytes 98312 | tf_op jit(solution)/shard_map/ppermute | solution.py:402
  18.0 1.5 %collective-permute-start.3 = (f32[2,32,128]{2,1,0:T(8,128)S(1)}, f32[2,32,128]{2,1,0:T(8,128)S(1)}, u32[]{:S(2)}, u32[]{:S(2)}) collective-permute-start(f32[2,32,128]{2,1,0:T(8,128)S(1)} %get-tuple-element.28), channel_id=1, source_target_pairs={{0,6},{1,7},{2,0},{3,1},{4,2},{5,3},{6,4},{7,5},{8,14},{9,15},{10,... | collective-permute-start | bytes 98312 | tf_op jit(solution)/shard_map/ppermute | solution.py:402
  19.4 0.0 copy-start.4
  19.4 0.6 shard_map.84.own_ref
  20.0 2.8 %collective-permute-done.1.rest_1_ = f32[2,32,128]{2,1,0:T(8,128)S(1)} collective-permute-done((f32[2,32,128]{2,1,0:T(8,128)S(1)}, f32[2,32,128]{2,1,0:T(8,128)S(1)}, u32[]{:S(2)}, u32[]{:S(2)}) %collective-permute-start.1) | collective-permute-done | bytes 32800 | tf_op jit(solution)/shard_map/ppermute | solution.py:402
  22.8 2.9 %collective-permute-done.2.rest_2_ = f32[2,32,128]{2,1,0:T(8,128)S(1)} collective-permute-done((f32[2,32,128]{2,1,0:T(8,128)S(1)}, f32[2,32,128]{2,1,0:T(8,128)S(1)}, u32[]{:S(2)}, u32[]{:S(2)}) %collective-permute-start.2) | collective-permute-done | bytes 32800 | tf_op jit(solution)/shard_map/ppermute | solution.py:402
  25.7 0.0 collective-permute-done.3.rest_3_
  25.7 0.0 all-to-all-done.rest_4_
  25.7 0.0 copy-done.4
  25.7 0.0 copy-start.3
  25.7 12.4 %shard_map.86 = (f32[192,128]{1,0:T(8,128)S(1)}, f32[5,192,128]{2,1,0:T(8,128)S(1)}) custom-call(f32[32,128]{1,0:T(8,128)S(1)} %copy-done.1, f32[2,32,16,128]{3,2,1,0:T(8,128)S(1)} %shard_map.84.own_ref, bf16[2,2,32,16,128]{4,3,2,1,0:T(8,128)(2,1)S(1)} %copy-done.4, f32[2,2,32,128]{3,2,1,0:T(8,128)S(1)} %collective-permute-done.partner_ref.rest_0_, ...), custom_call_target="tpu_custom_call" | custom-call | flops 20000000000 | bytes 4000000 | tf_op jit(solution)/shard_map/pallas_call | solution.py:372
  38.2 2.5 %collective-permute-start.6 = (f32[192,128]{1,0:T(8,128)S(1)}, f32[192,128]{1,0:T(8,128)S(1)}, u32[]{:S(2)}, u32[]{:S(2)}) collective-permute-start(f32[192,128]{1,0:T(8,128)S(1)} %get-tuple-element.31.rest_0_), channel_id=1, source_target_pairs={{0,24},{8,16},{16,8},{24,0},{1,25},{9,17},{17,9},{25,1},{2,26},{10... | collective-permute-start | bytes 294920 | tf_op jit(solution)/shard_map/ppermute | solution.py:390
  40.7 0.5 collective-permute-start.5
  41.2 0.5 collective-permute-start.4
  41.7 2.3 %collective-permute-done.6.rest_3_ = f32[192,128]{1,0:T(8,128)S(1)} collective-permute-done((f32[192,128]{1,0:T(8,128)S(1)}, f32[192,128]{1,0:T(8,128)S(1)}, u32[]{:S(2)}, u32[]{:S(2)}) %collective-permute-start.6) | collective-permute-done | bytes 98336 | tf_op jit(solution)/shard_map/ppermute | solution.py:390
  44.1 1.4 %collective-permute-done.5.rest_2_ = f32[192,128]{1,0:T(8,128)S(1)} collective-permute-done((f32[192,128]{1,0:T(8,128)S(1)}, f32[192,128]{1,0:T(8,128)S(1)}, u32[]{:S(2)}, u32[]{:S(2)}) %collective-permute-start.5) | collective-permute-done | bytes 98336 | tf_op jit(solution)/shard_map/ppermute | solution.py:390
  45.5 0.4 collective-permute-done.4.rest_1_
  45.8 0.0 copy-done.3
  45.8 11.8 %shard_map.87 = (f32[2,32,16,128]{3,2,1,0:T(8,128)S(1)}, f32[2,2,32,128]{3,2,1,0:T(8,128)S(1)}) custom-call(f32[32,128]{1,0:T(8,128)S(1)} %copy-done.1, bf16[32,128,128]{2,1,0:T(8,128)(2,1)S(1)} %get-tuple-element.22.high_ref, bf16[32,128,128]{2,1,0:T(8,128)(2,1)S(1)} %copy-done.3, bf16[2,2,32,16,128]{4,3,2,1,0:T(8,128)(2,1)S(1)} %copy-done.4, ...), custom_call_target="tpu_custom_call" | custom-call | flops 20000000000 | bytes 4000000 | tf_op jit(solution)/shard_map/pallas_call | solution.py:372
  57.6 0.0 collective-permute-start.7
  57.6 1.3 %collective-permute-done.7.partner_ref.rest_0_ = f32[2,2,32,128]{3,2,1,0:T(8,128)S(1)} collective-permute-done((f32[2,2,32,128]{3,2,1,0:T(8,128)S(1)}, f32[2,2,32,128]{3,2,1,0:T(8,128)S(1)}, u32[]{:S(2)}, u32[]{:S(2)}) %collective-permute-start.7) | collective-permute-done | bytes 65568 | tf_op jit(solution)/shard_map/ppermute | solution.py:395
  58.9 1.0 %collective-permute-start.8 = (f32[2,32,128]{2,1,0:T(8,128)S(1)}, f32[2,32,128]{2,1,0:T(8,128)S(1)}, u32[]{:S(2)}, u32[]{:S(2)}) collective-permute-start(f32[2,32,128]{2,1,0:T(8,128)S(1)} %get-tuple-element.34), channel_id=1, source_target_pairs={{0,2},{1,3},{2,4},{3,5},{4,6},{5,7},{6,0},{7,1},{8,10},{9,11},{10,... | collective-permute-start | bytes 98312 | tf_op jit(solution)/shard_map/ppermute | solution.py:402
  59.9 1.5 %collective-permute-start.9 = (f32[2,32,128]{2,1,0:T(8,128)S(1)}, f32[2,32,128]{2,1,0:T(8,128)S(1)}, u32[]{:S(2)}, u32[]{:S(2)}) collective-permute-start(f32[2,32,128]{2,1,0:T(8,128)S(1)} %get-tuple-element.35), channel_id=1, source_target_pairs={{0,4},{1,5},{2,6},{3,7},{4,0},{5,1},{6,2},{7,3},{8,12},{9,13},{10,... | collective-permute-start | bytes 98312 | tf_op jit(solution)/shard_map/ppermute | solution.py:402
  61.4 1.4 %collective-permute-start.10 = (f32[2,32,128]{2,1,0:T(8,128)S(1)}, f32[2,32,128]{2,1,0:T(8,128)S(1)}, u32[]{:S(2)}, u32[]{:S(2)}) collective-permute-start(f32[2,32,128]{2,1,0:T(8,128)S(1)} %get-tuple-element.36), channel_id=1, source_target_pairs={{0,6},{1,7},{2,0},{3,1},{4,2},{5,3},{6,4},{7,5},{8,14},{9,15},{10,... | collective-permute-start | bytes 98312 | tf_op jit(solution)/shard_map/ppermute | solution.py:402
  62.8 0.6 shard_map.88.own_ref
  63.4 1.6 %collective-permute-done.8.rest_1_ = f32[2,32,128]{2,1,0:T(8,128)S(1)} collective-permute-done((f32[2,32,128]{2,1,0:T(8,128)S(1)}, f32[2,32,128]{2,1,0:T(8,128)S(1)}, u32[]{:S(2)}, u32[]{:S(2)}) %collective-permute-start.8) | collective-permute-done | bytes 32800 | tf_op jit(solution)/shard_map/ppermute | solution.py:402
  64.9 0.5 collective-permute-done.9.rest_2_
  65.5 0.0 collective-permute-done.10.rest_3_
  65.5 1.0 %shard_map.90 = f32[2,32,16,128]{3,2,1,0:T(8,128)} custom-call(f32[32,128]{1,0:T(8,128)S(1)} %copy-done.1, f32[2,32,16,128]{3,2,1,0:T(8,128)S(1)} %copy-done, f32[2,32,16,128]{3,2,1,0:T(8,128)S(1)} %shard_map.88.own_ref, f32[2,2,32,128]{3,2,1,0:T(8,128)S(1)} %collective-permute-done.7.partner_ref.rest_0_, f32[2,32,128]{2,1,0:T(8,128)S(1)} %collective-permute-done.8.rest_1_, ...), custom_call_target="tpu_custom_call" | custom-call | tf_op jit(solution)/shard_map/pallas_call | solution.py:372
  (2 shorter events, 0.0 us)
Async XLA Ops:
  2.1 6.5 %copy-start = (f32[2,32,16,128]{3,2,1,0:T(8,128)S(1)}, f32[2,32,16,128]{3,2,1,0:T(8,128)}, u32[]{:S(2)}) copy-start(f32[2,32,16,128]{3,2,1,0:T(8,128)} %alpha_ref.3) | copy-start | bytes 1572868
  2.1 6.5 %copy-start.1 = (f32[32,128]{1,0:T(8,128)S(1)}, f32[32,128]{1,0:T(8,128)}, u32[]{:S(2)}) copy-start(f32[32,128]{1,0:T(8,128)} %get-tuple-element.21.rate_ref) | copy-start | bytes 49156
  2.1 23.6 %all-to-all-start = ((f32[8,120,128]{2,1,0:T(8,128)}), f32[8,120,128]{2,1,0:T(8,128)S(1)}, u32[]{:S(2)}, u32[]{:S(2)}) async-start(f32[8,120,128]{2,1,0:T(8,128)} %get-tuple-element.29), calls=%async_computation | async-start | bytes 983040 | tf_op jit(solution)/shard_map/all_to_all | solution.py:433
  11.3 1.0 %copy-start.2 = (bf16[32,128,128]{2,1,0:T(8,128)(2,1)}, bf16[32,128,128]{2,1,0:T(8,128)(2,1)S(1)}, u32[]{:S(2)}) copy-start(bf16[32,128,128]{2,1,0:T(8,128)(2,1)S(1)} %get-tuple-element.23.low_ref) | copy-start | bytes 3145732
  12.3 1.4 %collective-permute-start = (f32[2,2,32,128]{3,2,1,0:T(8,128)S(1)}, f32[2,2,32,128]{3,2,1,0:T(8,128)S(1)}, u32[]{:S(2)}, u32[]{:S(2)}) collective-permute-start(f32[2,2,32,128]{3,2,1,0:T(8,128)S(1)} %get-tuple-element.25.own_ref), channel_id=1, source_target_pairs={{0,1},{1,0},{2,3},{3,2},{4,5},{5,4},{6,7},{7,6},{8,9},{9,8},{10,11... | collective-permute-start | bytes 196616 | tf_op jit(solution)/shard_map/ppermute | solution.py:395
  13.7 9.1 %collective-permute-start.1 = (f32[2,32,128]{2,1,0:T(8,128)S(1)}, f32[2,32,128]{2,1,0:T(8,128)S(1)}, u32[]{:S(2)}, u32[]{:S(2)}) collective-permute-start(f32[2,32,128]{2,1,0:T(8,128)S(1)} %get-tuple-element.26), channel_id=1, source_target_pairs={{0,2},{1,3},{2,4},{3,5},{4,6},{5,7},{6,0},{7,1},{8,10},{9,11},{10,... | collective-permute-start | bytes 98312 | tf_op jit(solution)/shard_map/ppermute | solution.py:402
  15.6 10.1 %collective-permute-start.2 = (f32[2,32,128]{2,1,0:T(8,128)S(1)}, f32[2,32,128]{2,1,0:T(8,128)S(1)}, u32[]{:S(2)}, u32[]{:S(2)}) collective-permute-start(f32[2,32,128]{2,1,0:T(8,128)S(1)} %get-tuple-element.27), channel_id=1, source_target_pairs={{0,4},{1,5},{2,6},{3,7},{4,0},{5,1},{6,2},{7,3},{8,12},{9,13},{10,... | collective-permute-start | bytes 98312 | tf_op jit(solution)/shard_map/ppermute | solution.py:402
  18.0 7.7 %collective-permute-start.3 = (f32[2,32,128]{2,1,0:T(8,128)S(1)}, f32[2,32,128]{2,1,0:T(8,128)S(1)}, u32[]{:S(2)}, u32[]{:S(2)}) collective-permute-start(f32[2,32,128]{2,1,0:T(8,128)S(1)} %get-tuple-element.28), channel_id=1, source_target_pairs={{0,6},{1,7},{2,0},{3,1},{4,2},{5,3},{6,4},{7,5},{8,14},{9,15},{10,... | collective-permute-start | bytes 98312 | tf_op jit(solution)/shard_map/ppermute | solution.py:402
  19.4 6.3 %copy-start.4 = (bf16[2,2,32,16,128]{4,3,2,1,0:T(8,128)(2,1)S(1)}, bf16[2,2,32,16,128]{4,3,2,1,0:T(8,128)(2,1)}, u32[]{:S(2)}) copy-start(bf16[2,2,32,16,128]{4,3,2,1,0:T(8,128)(2,1)} %members_ref.3) | copy-start | bytes 1572868
  25.7 20.1 %copy-start.3 = (bf16[32,128,128]{2,1,0:T(8,128)(2,1)S(1)}, bf16[32,128,128]{2,1,0:T(8,128)(2,1)}, u32[]{:S(2)}) copy-start(bf16[32,128,128]{2,1,0:T(8,128)(2,1)} %copy-done.2) | copy-start | bytes 3145732
  38.2 5.9 %collective-permute-start.6 = (f32[192,128]{1,0:T(8,128)S(1)}, f32[192,128]{1,0:T(8,128)S(1)}, u32[]{:S(2)}, u32[]{:S(2)}) collective-permute-start(f32[192,128]{1,0:T(8,128)S(1)} %get-tuple-element.31.rest_0_), channel_id=1, source_target_pairs={{0,24},{8,16},{16,8},{24,0},{1,25},{9,17},{17,9},{25,1},{2,26},{10... | collective-permute-start | bytes 294920 | tf_op jit(solution)/shard_map/ppermute | solution.py:390
  40.7 4.8 %collective-permute-start.5 = (f32[192,128]{1,0:T(8,128)S(1)}, f32[192,128]{1,0:T(8,128)S(1)}, u32[]{:S(2)}, u32[]{:S(2)}) collective-permute-start(f32[192,128]{1,0:T(8,128)S(1)} %get-tuple-element.31.rest_0_), channel_id=1, source_target_pairs={{0,16},{8,24},{16,0},{24,8},{1,17},{9,25},{17,1},{25,9},{2,18},{10... | collective-permute-start | bytes 294920 | tf_op jit(solution)/shard_map/ppermute | solution.py:390
  41.2 4.6 %collective-permute-start.4 = (f32[192,128]{1,0:T(8,128)S(1)}, f32[192,128]{1,0:T(8,128)S(1)}, u32[]{:S(2)}, u32[]{:S(2)}) collective-permute-start(f32[192,128]{1,0:T(8,128)S(1)} %get-tuple-element.31.rest_0_), channel_id=1, source_target_pairs={{0,8},{8,0},{16,24},{24,16},{1,9},{9,1},{17,25},{25,17},{2,10},{10... | collective-permute-start | bytes 294920 | tf_op jit(solution)/shard_map/ppermute | solution.py:390
  57.6 1.3 %collective-permute-start.7 = (f32[2,2,32,128]{3,2,1,0:T(8,128)S(1)}, f32[2,2,32,128]{3,2,1,0:T(8,128)S(1)}, u32[]{:S(2)}, u32[]{:S(2)}) collective-permute-start(f32[2,2,32,128]{3,2,1,0:T(8,128)S(1)} %get-tuple-element.33.own_ref), channel_id=1, source_target_pairs={{0,1},{1,0},{2,3},{3,2},{4,5},{5,4},{6,7},{7,6},{8,9},{9,8},{10,11... | collective-permute-start | bytes 196616 | tf_op jit(solution)/shard_map/ppermute | solution.py:395
  58.9 6.0 %collective-permute-start.8 = (f32[2,32,128]{2,1,0:T(8,128)S(1)}, f32[2,32,128]{2,1,0:T(8,128)S(1)}, u32[]{:S(2)}, u32[]{:S(2)}) collective-permute-start(f32[2,32,128]{2,1,0:T(8,128)S(1)} %get-tuple-element.34), channel_id=1, source_target_pairs={{0,2},{1,3},{2,4},{3,5},{4,6},{5,7},{6,0},{7,1},{8,10},{9,11},{10,... | collective-permute-start | bytes 98312 | tf_op jit(solution)/shard_map/ppermute | solution.py:402
  59.9 5.6 %collective-permute-start.9 = (f32[2,32,128]{2,1,0:T(8,128)S(1)}, f32[2,32,128]{2,1,0:T(8,128)S(1)}, u32[]{:S(2)}, u32[]{:S(2)}) collective-permute-start(f32[2,32,128]{2,1,0:T(8,128)S(1)} %get-tuple-element.35), channel_id=1, source_target_pairs={{0,4},{1,5},{2,6},{3,7},{4,0},{5,1},{6,2},{7,3},{8,12},{9,13},{10,... | collective-permute-start | bytes 98312 | tf_op jit(solution)/shard_map/ppermute | solution.py:402
  61.4 4.1 %collective-permute-start.10 = (f32[2,32,128]{2,1,0:T(8,128)S(1)}, f32[2,32,128]{2,1,0:T(8,128)S(1)}, u32[]{:S(2)}, u32[]{:S(2)}) collective-permute-start(f32[2,32,128]{2,1,0:T(8,128)S(1)} %get-tuple-element.36), channel_id=1, source_target_pairs={{0,6},{1,7},{2,0},{3,1},{4,2},{5,3},{6,4},{7,5},{8,14},{9,15},{10,... | collective-permute-start | bytes 98312 | tf_op jit(solution)/shard_map/ppermute | solution.py:402

commit v7 on v6

--- a/solution.py
+++ b/solution.py
@@ -118,7 +118,7 @@
         out_ref[:, l] = total.reshape(members, rows, columns)
         return 0
 
-    lax.fori_loop(0, levels, level, 0, unroll=8)
+    lax.fori_loop(0, levels, level, 0, unroll=16)
 
 
 def columns_matrix(rate_ref, high_ref, low_ref):
@@ -133,7 +133,7 @@
         high_ref[l], low_ref[l] = split(matrix)
         return 0
 
-    lax.fori_loop(0, levels, level, 0, unroll=8)
+    lax.fori_loop(0, levels, level, 0, unroll=16)
 
 
 def states(tiles, rate_ref, field_ref, out_ref):

time: 66.7 us -> 66.5 us (level)
  transfers between devices with their start and end apart: 12 -> 12, of which waited for: 9 -> 9; matrix products, arithmetic and copies ran while one was open for 0% -> 0% of each run, Pallas kernels for 6% -> 5%
where the time goes in v7:
time: 66.5 us; the launch traced here: 66.3 us
  Pallas kernels  30.7 us (46%)
  starting transfers between devices  20.2 us (30%)
  waiting for transfers between devices  14.3 us (22%)
  local copies, waits for them, and re-layouts  1.03 us (2%)
    pallas_call x9, Pallas kernels, run(): pl.pallas_call(body, out_shape=outs, in_specs=specs or [VMEM] * len(args)...  30.7 us
    ppermute x6, starting transfers between devices, exchange(): lax.ppermute(part, 'tile', [(2 * c + h, 2 * ((c + k) % chips) + h) for c...  9.63 us
    ppermute x6, waiting for transfers between devices, exchange(): lax.ppermute(part, 'tile', [(2 * c + h, 2 * ((c + k) % chips) + h) for c...  8.04 us
    all_to_all x1, starting transfers between devices, per_device(): here = lax.all_to_all(sent, 'tile', split_axis=0, concat_axis=0, tiled=True)  6.47 us
    ppermute x3, waiting for transfers between devices, over_members(): lax.ppermute(part, 'mem', [(i, i ^ k) for i in range(blocks)])  4.08 us
    ppermute x3, starting transfers between devices, over_members(): lax.ppermute(part, 'mem', [(i, i ^ k) for i in range(blocks)])  3.55 us
    ppermute x2, waiting for transfers between devices, exchange(): partner = lax.ppermute(own, 'tile', [(i, i ^ 1) for i in range(tiles)])  2.17 us
  transfers between devices with their start and end apart: 12, of which 9 were waited for; matrix products, arithmetic and copies ran while one was open for 0% of the time, Pallas kernels for 5%

profile of v7, /device:TPU:0, one launch (start us, length us, event | category | flops | bytes accessed | tf_op | source)
XLA Modules:
  0.0 66.3 jit_solution(3494654967949543686)
XLA Ops:
  0.0 2.1 %shard_map.82 = (f32[8,120,128]{2,1,0:T(8,128)}, f32[32,128]{1,0:T(8,128)}) custom-call(s32[1,32]{1,0:T(1,128)} %bitcast.2, f32[1,32]{1,0:T(1,128)} %bitcast.3, s32[32,256]{1,0:T(8,128)} %refs_2_.1, f32[32,2,256]{2,1,0:T(2,128)} %refs_3_.1, f32[32,256]{1,0:T(8,128)} %refs_4_.1, f32[32,256]{1,0:T(8,128)} %refs_5_.1), custom_call_target="tpu_custom_call" | custom-call | tf_op jit(solution)/shard_map/pallas_call | solution.py:372
  2.1 0.0 copy-start
  2.1 0.0 copy-start.1
  2.1 6.5 %all-to-all-start = ((f32[8,120,128]{2,1,0:T(8,128)}), f32[8,120,128]{2,1,0:T(8,128)S(1)}, u32[]{:S(2)}, u32[]{:S(2)}) async-start(f32[8,120,128]{2,1,0:T(8,128)} %get-tuple-element.29), calls=%async_computation | async-start | bytes 983040 | tf_op jit(solution)/shard_map/all_to_all | solution.py:433
  8.6 0.0 copy-done
  8.6 0.0 copy-done.1
  8.6 2.4 %shard_map.83 = (bf16[32,128,128]{2,1,0:T(8,128)(2,1)S(1)}, bf16[32,128,128]{2,1,0:T(8,128)(2,1)S(1)}, f32[2,32,16,128]{3,2,1,0:T(8,128)S(1)}, f32[2,2,32,128]{3,2,1,0:T(8,128)S(1)}) custom-call(f32[32,128]{1,0:T(8,128)S(1)} %copy-done.1, f32[2,32,16,128]{3,2,1,0:T(8,128)S(1)} %copy-done), custom_call_target="tpu_custom_call" | custom-call | tf_op jit(solution)/shard_map/pallas_call | solution.py:372
  11.0 0.0 copy-start.2
  11.0 1.0 %copy-done.2 = bf16[32,128,128]{2,1,0:T(8,128)(2,1)} copy-done((bf16[32,128,128]{2,1,0:T(8,128)(2,1)}, bf16[32,128,128]{2,1,0:T(8,128)(2,1)S(1)}, u32[]{:S(2)}) %copy-start.2) | copy-done | bytes 1048600
  12.0 0.5 collective-permute-start
  12.5 0.9 %collective-permute-done.partner_ref.rest_0_ = f32[2,2,32,128]{3,2,1,0:T(8,128)S(1)} collective-permute-done((f32[2,2,32,128]{3,2,1,0:T(8,128)S(1)}, f32[2,2,32,128]{3,2,1,0:T(8,128)S(1)}, u32[]{:S(2)}, u32[]{:S(2)}) %collective-permute-start) | collective-permute-done | bytes 65568 | tf_op jit(solution)/shard_map/ppermute | solution.py:395
  13.4 1.9 %collective-permute-start.1 = (f32[2,32,128]{2,1,0:T(8,128)S(1)}, f32[2,32,128]{2,1,0:T(8,128)S(1)}, u32[]{:S(2)}, u32[]{:S(2)}) collective-permute-start(f32[2,32,128]{2,1,0:T(8,128)S(1)} %get-tuple-element.26), channel_id=1, source_target_pairs={{0,2},{1,3},{2,4},{3,5},{4,6},{5,7},{6,0},{7,1},{8,10},{9,11},{10,... | collective-permute-start | bytes 98312 | tf_op jit(solution)/shard_map/ppermute | solution.py:402
  15.3 2.4 %collective-permute-start.2 = (f32[2,32,128]{2,1,0:T(8,128)S(1)}, f32[2,32,128]{2,1,0:T(8,128)S(1)}, u32[]{:S(2)}, u32[]{:S(2)}) collective-permute-start(f32[2,32,128]{2,1,0:T(8,128)S(1)} %get-tuple-element.27), channel_id=1, source_target_pairs={{0,4},{1,5},{2,6},{3,7},{4,0},{5,1},{6,2},{7,3},{8,12},{9,13},{10,... | collective-permute-start | bytes 98312 | tf_op jit(solution)/shard_map/ppermute | solution.py:402
  17.7 1.5 %collective-permute-start.3 = (f32[2,32,128]{2,1,0:T(8,128)S(1)}, f32[2,32,128]{2,1,0:T(8,128)S(1)}, u32[]{:S(2)}, u32[]{:S(2)}) collective-permute-start(f32[2,32,128]{2,1,0:T(8,128)S(1)} %get-tuple-element.28), channel_id=1, source_target_pairs={{0,6},{1,7},{2,0},{3,1},{4,2},{5,3},{6,4},{7,5},{8,14},{9,15},{10,... | collective-permute-start | bytes 98312 | tf_op jit(solution)/shard_map/ppermute | solution.py:402
  19.2 0.0 copy-start.4
  19.2 0.6 shard_map.84.own_ref
  19.8 3.0 %collective-permute-done.1.rest_1_ = f32[2,32,128]{2,1,0:T(8,128)S(1)} collective-permute-done((f32[2,32,128]{2,1,0:T(8,128)S(1)}, f32[2,32,128]{2,1,0:T(8,128)S(1)}, u32[]{:S(2)}, u32[]{:S(2)}) %collective-permute-start.1) | collective-permute-done | bytes 32800 | tf_op jit(solution)/shard_map/ppermute | solution.py:402
  22.8 2.9 %collective-permute-done.2.rest_2_ = f32[2,32,128]{2,1,0:T(8,128)S(1)} collective-permute-done((f32[2,32,128]{2,1,0:T(8,128)S(1)}, f32[2,32,128]{2,1,0:T(8,128)S(1)}, u32[]{:S(2)}, u32[]{:S(2)}) %collective-permute-start.2) | collective-permute-done | bytes 32800 | tf_op jit(solution)/shard_map/ppermute | solution.py:402
  25.7 0.0 collective-permute-done.3.rest_3_
  25.7 0.0 all-to-all-done.rest_4_
  25.7 0.0 copy-done.4
  25.7 0.0 copy-start.3
  25.7 12.4 %shard_map.86 = (f32[192,128]{1,0:T(8,128)S(1)}, f32[5,192,128]{2,1,0:T(8,128)S(1)}) custom-call(f32[32,128]{1,0:T(8,128)S(1)} %copy-done.1, f32[2,32,16,128]{3,2,1,0:T(8,128)S(1)} %shard_map.84.own_ref, bf16[2,2,32,16,128]{4,3,2,1,0:T(8,128)(2,1)S(1)} %copy-done.4, f32[2,2,32,128]{3,2,1,0:T(8,128)S(1)} %collective-permute-done.partner_ref.rest_0_, ...), custom_call_target="tpu_custom_call" | custom-call | flops 20000000000 | bytes 4000000 | tf_op jit(solution)/shard_map/pallas_call | solution.py:372
  38.2 2.5 %collective-permute-start.6 = (f32[192,128]{1,0:T(8,128)S(1)}, f32[192,128]{1,0:T(8,128)S(1)}, u32[]{:S(2)}, u32[]{:S(2)}) collective-permute-start(f32[192,128]{1,0:T(8,128)S(1)} %get-tuple-element.31.rest_0_), channel_id=1, source_target_pairs={{0,24},{8,16},{16,8},{24,0},{1,25},{9,17},{17,9},{25,1},{2,26},{10... | collective-permute-start | bytes 294920 | tf_op jit(solution)/shard_map/ppermute | solution.py:390
  40.7 0.5 collective-permute-start.5
  41.2 0.5 collective-permute-start.4
  41.7 2.3 %collective-permute-done.6.rest_3_ = f32[192,128]{1,0:T(8,128)S(1)} collective-permute-done((f32[192,128]{1,0:T(8,128)S(1)}, f32[192,128]{1,0:T(8,128)S(1)}, u32[]{:S(2)}, u32[]{:S(2)}) %collective-permute-start.6) | collective-permute-done | bytes 98336 | tf_op jit(solution)/shard_map/ppermute | solution.py:390
  44.1 1.4 %collective-permute-done.5.rest_2_ = f32[192,128]{1,0:T(8,128)S(1)} collective-permute-done((f32[192,128]{1,0:T(8,128)S(1)}, f32[192,128]{1,0:T(8,128)S(1)}, u32[]{:S(2)}, u32[]{:S(2)}) %collective-permute-start.5) | collective-permute-done | bytes 98336 | tf_op jit(solution)/shard_map/ppermute | solution.py:390
  45.5 0.4 collective-permute-done.4.rest_1_
  45.8 0.0 copy-done.3
  45.8 11.6 %shard_map.87 = (f32[2,32,16,128]{3,2,1,0:T(8,128)S(1)}, f32[2,2,32,128]{3,2,1,0:T(8,128)S(1)}) custom-call(f32[32,128]{1,0:T(8,128)S(1)} %copy-done.1, bf16[32,128,128]{2,1,0:T(8,128)(2,1)S(1)} %get-tuple-element.22.high_ref, bf16[32,128,128]{2,1,0:T(8,128)(2,1)S(1)} %copy-done.3, bf16[2,2,32,16,128]{4,3,2,1,0:T(8,128)(2,1)S(1)} %copy-done.4, ...), custom_call_target="tpu_custom_call" | custom-call | flops 20000000000 | bytes 4000000 | tf_op jit(solution)/shard_map/pallas_call | solution.py:372
  57.4 0.0 collective-permute-start.7
  57.4 1.3 %collective-permute-done.7.partner_ref.rest_0_ = f32[2,2,32,128]{3,2,1,0:T(8,128)S(1)} collective-permute-done((f32[2,2,32,128]{3,2,1,0:T(8,128)S(1)}, f32[2,2,32,128]{3,2,1,0:T(8,128)S(1)}, u32[]{:S(2)}, u32[]{:S(2)}) %collective-permute-start.7) | collective-permute-done | bytes 65568 | tf_op jit(solution)/shard_map/ppermute | solution.py:395
  58.7 1.0 %collective-permute-start.8 = (f32[2,32,128]{2,1,0:T(8,128)S(1)}, f32[2,32,128]{2,1,0:T(8,128)S(1)}, u32[]{:S(2)}, u32[]{:S(2)}) collective-permute-start(f32[2,32,128]{2,1,0:T(8,128)S(1)} %get-tuple-element.34), channel_id=1, source_target_pairs={{0,2},{1,3},{2,4},{3,5},{4,6},{5,7},{6,0},{7,1},{8,10},{9,11},{10,... | collective-permute-start | bytes 98312 | tf_op jit(solution)/shard_map/ppermute | solution.py:402
  59.6 1.5 %collective-permute-start.9 = (f32[2,32,128]{2,1,0:T(8,128)S(1)}, f32[2,32,128]{2,1,0:T(8,128)S(1)}, u32[]{:S(2)}, u32[]{:S(2)}) collective-permute-start(f32[2,32,128]{2,1,0:T(8,128)S(1)} %get-tuple-element.35), channel_id=1, source_target_pairs={{0,4},{1,5},{2,6},{3,7},{4,0},{5,1},{6,2},{7,3},{8,12},{9,13},{10,... | collective-permute-start | bytes 98312 | tf_op jit(solution)/shard_map/ppermute | solution.py:402
  61.2 1.4 %collective-permute-start.10 = (f32[2,32,128]{2,1,0:T(8,128)S(1)}, f32[2,32,128]{2,1,0:T(8,128)S(1)}, u32[]{:S(2)}, u32[]{:S(2)}) collective-permute-start(f32[2,32,128]{2,1,0:T(8,128)S(1)} %get-tuple-element.36), channel_id=1, source_target_pairs={{0,6},{1,7},{2,0},{3,1},{4,2},{5,3},{6,4},{7,5},{8,14},{9,15},{10,... | collective-permute-start | bytes 98312 | tf_op jit(solution)/shard_map/ppermute | solution.py:402
  62.6 0.6 shard_map.88.own_ref
  63.1 1.6 %collective-permute-done.8.rest_1_ = f32[2,32,128]{2,1,0:T(8,128)S(1)} collective-permute-done((f32[2,32,128]{2,1,0:T(8,128)S(1)}, f32[2,32,128]{2,1,0:T(8,128)S(1)}, u32[]{:S(2)}, u32[]{:S(2)}) %collective-permute-start.8) | collective-permute-done | bytes 32800 | tf_op jit(solution)/shard_map/ppermute | solution.py:402
  64.7 0.5 collective-permute-done.9.rest_2_
  65.2 0.0 collective-permute-done.10.rest_3_
  65.2 1.0 %shard_map.90 = f32[2,32,16,128]{3,2,1,0:T(8,128)} custom-call(f32[32,128]{1,0:T(8,128)S(1)} %copy-done.1, f32[2,32,16,128]{3,2,1,0:T(8,128)S(1)} %copy-done, f32[2,32,16,128]{3,2,1,0:T(8,128)S(1)} %shard_map.88.own_ref, f32[2,2,32,128]{3,2,1,0:T(8,128)S(1)} %collective-permute-done.7.partner_ref.rest_0_, f32[2,32,128]{2,1,0:T(8,128)S(1)} %collective-permute-done.8.rest_1_, ...), custom_call_target="tpu_custom_call" | custom-call | tf_op jit(solution)/shard_map/pallas_call | solution.py:372
  (2 shorter events, 0.0 us)
Async XLA Ops:
  2.1 6.5 %copy-start = (f32[2,32,16,128]{3,2,1,0:T(8,128)S(1)}, f32[2,32,16,128]{3,2,1,0:T(8,128)}, u32[]{:S(2)}) copy-start(f32[2,32,16,128]{3,2,1,0:T(8,128)} %alpha_ref.3) | copy-start | bytes 1572868
  2.1 6.5 %copy-start.1 = (f32[32,128]{1,0:T(8,128)S(1)}, f32[32,128]{1,0:T(8,128)}, u32[]{:S(2)}) copy-start(f32[32,128]{1,0:T(8,128)} %get-tuple-element.21.rate_ref) | copy-start | bytes 49156
  2.1 23.6 %all-to-all-start = ((f32[8,120,128]{2,1,0:T(8,128)}), f32[8,120,128]{2,1,0:T(8,128)S(1)}, u32[]{:S(2)}, u32[]{:S(2)}) async-start(f32[8,120,128]{2,1,0:T(8,128)} %get-tuple-element.29), calls=%async_computation | async-start | bytes 983040 | tf_op jit(solution)/shard_map/all_to_all | solution.py:433
  11.0 1.0 %copy-start.2 = (bf16[32,128,128]{2,1,0:T(8,128)(2,1)}, bf16[32,128,128]{2,1,0:T(8,128)(2,1)S(1)}, u32[]{:S(2)}) copy-start(bf16[32,128,128]{2,1,0:T(8,128)(2,1)S(1)} %get-tuple-element.23.low_ref) | copy-start | bytes 3145732
  12.0 1.4 %collective-permute-start = (f32[2,2,32,128]{3,2,1,0:T(8,128)S(1)}, f32[2,2,32,128]{3,2,1,0:T(8,128)S(1)}, u32[]{:S(2)}, u32[]{:S(2)}) collective-permute-start(f32[2,2,32,128]{3,2,1,0:T(8,128)S(1)} %get-tuple-element.25.own_ref), channel_id=1, source_target_pairs={{0,1},{1,0},{2,3},{3,2},{4,5},{5,4},{6,7},{7,6},{8,9},{9,8},{10,11... | collective-permute-start | bytes 196616 | tf_op jit(solution)/shard_map/ppermute | solution.py:395
  13.4 9.4 %collective-permute-start.1 = (f32[2,32,128]{2,1,0:T(8,128)S(1)}, f32[2,32,128]{2,1,0:T(8,128)S(1)}, u32[]{:S(2)}, u32[]{:S(2)}) collective-permute-start(f32[2,32,128]{2,1,0:T(8,128)S(1)} %get-tuple-element.26), channel_id=1, source_target_pairs={{0,2},{1,3},{2,4},{3,5},{4,6},{5,7},{6,0},{7,1},{8,10},{9,11},{10,... | collective-permute-start | bytes 98312 | tf_op jit(solution)/shard_map/ppermute | solution.py:402
  15.3 10.4 %collective-permute-start.2 = (f32[2,32,128]{2,1,0:T(8,128)S(1)}, f32[2,32,128]{2,1,0:T(8,128)S(1)}, u32[]{:S(2)}, u32[]{:S(2)}) collective-permute-start(f32[2,32,128]{2,1,0:T(8,128)S(1)} %get-tuple-element.27), channel_id=1, source_target_pairs={{0,4},{1,5},{2,6},{3,7},{4,0},{5,1},{6,2},{7,3},{8,12},{9,13},{10,... | collective-permute-start | bytes 98312 | tf_op jit(solution)/shard_map/ppermute | solution.py:402
  17.7 8.0 %collective-permute-start.3 = (f32[2,32,128]{2,1,0:T(8,128)S(1)}, f32[2,32,128]{2,1,0:T(8,128)S(1)}, u32[]{:S(2)}, u32[]{:S(2)}) collective-permute-start(f32[2,32,128]{2,1,0:T(8,128)S(1)} %get-tuple-element.28), channel_id=1, source_target_pairs={{0,6},{1,7},{2,0},{3,1},{4,2},{5,3},{6,4},{7,5},{8,14},{9,15},{10,... | collective-permute-start | bytes 98312 | tf_op jit(solution)/shard_map/ppermute | solution.py:402
  19.2 6.6 %copy-start.4 = (bf16[2,2,32,16,128]{4,3,2,1,0:T(8,128)(2,1)S(1)}, bf16[2,2,32,16,128]{4,3,2,1,0:T(8,128)(2,1)}, u32[]{:S(2)}) copy-start(bf16[2,2,32,16,128]{4,3,2,1,0:T(8,128)(2,1)} %members_ref.3) | copy-start | bytes 1572868
  25.7 20.1 %copy-start.3 = (bf16[32,128,128]{2,1,0:T(8,128)(2,1)S(1)}, bf16[32,128,128]{2,1,0:T(8,128)(2,1)}, u32[]{:S(2)}) copy-start(bf16[32,128,128]{2,1,0:T(8,128)(2,1)} %copy-done.2) | copy-start | bytes 3145732
  38.2 5.9 %collective-permute-start.6 = (f32[192,128]{1,0:T(8,128)S(1)}, f32[192,128]{1,0:T(8,128)S(1)}, u32[]{:S(2)}, u32[]{:S(2)}) collective-permute-start(f32[192,128]{1,0:T(8,128)S(1)} %get-tuple-element.31.rest_0_), channel_id=1, source_target_pairs={{0,24},{8,16},{16,8},{24,0},{1,25},{9,17},{17,9},{25,1},{2,26},{10... | collective-permute-start | bytes 294920 | tf_op jit(solution)/shard_map/ppermute | solution.py:390
  40.7 4.8 %collective-permute-start.5 = (f32[192,128]{1,0:T(8,128)S(1)}, f32[192,128]{1,0:T(8,128)S(1)}, u32[]{:S(2)}, u32[]{:S(2)}) collective-permute-start(f32[192,128]{1,0:T(8,128)S(1)} %get-tuple-element.31.rest_0_), channel_id=1, source_target_pairs={{0,16},{8,24},{16,0},{24,8},{1,17},{9,25},{17,1},{25,9},{2,18},{10... | collective-permute-start | bytes 294920 | tf_op jit(solution)/shard_map/ppermute | solution.py:390
  41.2 4.6 %collective-permute-start.4 = (f32[192,128]{1,0:T(8,128)S(1)}, f32[192,128]{1,0:T(8,128)S(1)}, u32[]{:S(2)}, u32[]{:S(2)}) collective-permute-start(f32[192,128]{1,0:T(8,128)S(1)} %get-tuple-element.31.rest_0_), channel_id=1, source_target_pairs={{0,8},{8,0},{16,24},{24,16},{1,9},{9,1},{17,25},{25,17},{2,10},{10... | collective-permute-start | bytes 294920 | tf_op jit(solution)/shard_map/ppermute | solution.py:390
  57.4 1.3 %collective-permute-start.7 = (f32[2,2,32,128]{3,2,1,0:T(8,128)S(1)}, f32[2,2,32,128]{3,2,1,0:T(8,128)S(1)}, u32[]{:S(2)}, u32[]{:S(2)}) collective-permute-start(f32[2,2,32,128]{3,2,1,0:T(8,128)S(1)} %get-tuple-element.33.own_ref), channel_id=1, source_target_pairs={{0,1},{1,0},{2,3},{3,2},{4,5},{5,4},{6,7},{7,6},{8,9},{9,8},{10,11... | collective-permute-start | bytes 196616 | tf_op jit(solution)/shard_map/ppermute | solution.py:395
  58.7 6.0 %collective-permute-start.8 = (f32[2,32,128]{2,1,0:T(8,128)S(1)}, f32[2,32,128]{2,1,0:T(8,128)S(1)}, u32[]{:S(2)}, u32[]{:S(2)}) collective-permute-start(f32[2,32,128]{2,1,0:T(8,128)S(1)} %get-tuple-element.34), channel_id=1, source_target_pairs={{0,2},{1,3},{2,4},{3,5},{4,6},{5,7},{6,0},{7,1},{8,10},{9,11},{10,... | collective-permute-start | bytes 98312 | tf_op jit(solution)/shard_map/ppermute | solution.py:402
  59.6 5.6 %collective-permute-start.9 = (f32[2,32,128]{2,1,0:T(8,128)S(1)}, f32[2,32,128]{2,1,0:T(8,128)S(1)}, u32[]{:S(2)}, u32[]{:S(2)}) collective-permute-start(f32[2,32,128]{2,1,0:T(8,128)S(1)} %get-tuple-element.35), channel_id=1, source_target_pairs={{0,4},{1,5},{2,6},{3,7},{4,0},{5,1},{6,2},{7,3},{8,12},{9,13},{10,... | collective-permute-start | bytes 98312 | tf_op jit(solution)/shard_map/ppermute | solution.py:402
  61.2 4.1 %collective-permute-start.10 = (f32[2,32,128]{2,1,0:T(8,128)S(1)}, f32[2,32,128]{2,1,0:T(8,128)S(1)}, u32[]{:S(2)}, u32[]{:S(2)}) collective-permute-start(f32[2,32,128]{2,1,0:T(8,128)S(1)} %get-tuple-element.36), channel_id=1, source_target_pairs={{0,6},{1,7},{2,0},{3,1},{4,2},{5,3},{6,4},{7,5},{8,14},{9,15},{10,... | collective-permute-start | bytes 98312 | tf_op jit(solution)/shard_map/ppermute | solution.py:402
